TPU v7x, 32 devices: a whole 2x2x4 slice. The times are simulated.
32 devices in a mesh: dp: 4 (over y, core), expert: 8 (over z, x).
Axes of the slice: x: 2, y: 2, z: 4, core: 2. Of those that a mesh axis runs over, the one named last changes fastest.
Arguments:
- queries: bfloat16 [4, 1024, 2048], P('dp', 'expert'), may hold values from -5.5 to 5.5
- keys: bfloat16 [4, 1024, 2048], P('dp', 'expert'), may hold values from -5.5 to 5.5
- values: bfloat16 [4, 1024, 2048], P('dp', 'expert'), may hold values from -6 to 6
- doc_ids: int32 [4, 1024], P('dp', 'expert'), may hold values from 0 to 3, never falling along the last dimension, each value on 1 to 512 neighbouring positions
- expert_index: int32 [4, 1024, 2], P('dp', 'expert'), may hold values from 0 to 7, all different within a row; in each aligned block of 128 rows (0 to 127, 128 to 255, ..., all dimensions but the last counted through in order) at most 48 rows name the same one
- gates: float32 [4, 1024, 2], P('dp', 'expert'), may hold values from 0.1 to 1
- capacity: int32 [8], replicated, may hold values from 24 to 48, as said below
- norm_gain: float32 [2048], replicated, may hold values from 0.1 to 1.9
- gate_weight: bfloat16 [8, 2048, 1024], P('expert', 'dp'), may hold values from -0.125 to 0.125
- up_weight: bfloat16 [8, 2048, 1024], P('expert', 'dp'), may hold values from -0.125 to 0.125
- down_weight: bfloat16 [8, 1024, 2048], P('expert', 'dp'), may hold values from -0.1875 to 0.1875
Outputs:
- mixed: bfloat16 [4, 1024, 2048], P('dp', 'expert')
Inputs may be any that keep to these rules, and one draw needn't show every extreme that they name: `doc_ids`: never falls along a window; each protein has 1 to 512 residues, one exactly 512; every number of proteins below 4 appears. `expert_index`: the two experts of a residue differ; within the 128 residues of one device (aligned blocks of a window) no expert is named by more than 48 residues, a bound that some block reaches. Some expert has capacity exactly 48.
All inputs are finite; a program needn't handle non-finite values.
Results may differ from a plain program's by a relative error of at most 0.017.
Values may be sent and summed in bfloat16 or wider, within the bound.
No kernel may reach another device: no remote copies, remote signals or barrier semaphores. Data moves between devices by JAX's collectives and lax.ppermute only.
A program may use at most 64 MiB of HBM per device.

v0:
```python
import math

import jax
import jax.numpy as jnp
from jax import lax
from jax.sharding import PartitionSpec as P

HEAD_DIM = 128
TOP = 2
WINDOW = 512


def shifted_2(block, axis, distance):
    devices = range(lax.axis_size(axis))
    route = [(i - distance, i) for i in devices if i - distance in devices]
    return lax.ppermute(block, axis, route)


def attend_local(queries, key_rows, value_rows, query_docs, key_docs, query_start, key_start):
    rows_dev, width = queries.shape
    heads = width // HEAD_DIM
    q_block = min(512, rows_dev)
    before = key_rows.shape[0] - rows_dev

    def one_block(number):
        begin = number * q_block
        query_part = queries.reshape(q_block, heads, HEAD_DIM)
        key_part = key_rows.reshape(before + q_block, heads, HEAD_DIM)
        value_part = value_rows.reshape(before + q_block, heads, HEAD_DIM)
        query_pos = query_start + begin + jnp.arange(q_block, dtype=jnp.int32)
        key_pos = key_start + begin + jnp.arange(before + q_block, dtype=jnp.int32)
        allowed = (key_pos[None, :] <= query_pos[:, None]) & (
            key_pos[None, :] > query_pos[:, None] - WINDOW
        )
        allowed = allowed & (key_pos[None, :] >= 0) & (key_docs[None, :] == query_docs[:, None])
        scores = jnp.einsum(
            "qhd,khd->hqk", query_part, key_part, preferred_element_type=jnp.float32
        ) * (1.0 / math.sqrt(HEAD_DIM))
        scores = jnp.where(allowed[None], scores, -1e30)
        highest = jnp.max(scores, axis=-1, keepdims=True)
        expo = jnp.exp(scores - highest)
        probs = (expo / jnp.sum(expo, axis=-1, keepdims=True)).astype(jnp.bfloat16)
        result = jnp.einsum("hqk,khd->qhd", probs, value_part, preferred_element_type=jnp.float32)
        return result.reshape(q_block, width).astype(jnp.bfloat16)

    blocks = lax.map(one_block, jnp.arange(rows_dev // q_block, dtype=jnp.int32))
    return blocks.reshape(rows_dev, width)


def per_device(
    queries,
    keys,
    values,
    doc_ids,
    expert_index,
    gates,
    capacity,
    norm_gain,
    gate_weight,
    up_weight,
    down_weight,
):
    rows_dev = queries.shape[1]
    width = queries.shape[2]
    reach_back = (WINDOW - 1) // rows_dev + 1
    own_pair = jnp.stack([keys[0], values[0]], axis=0)
    own_docs = doc_ids[0].astype(jnp.bfloat16)
    earlier = []
    current = (own_pair, own_docs)
    for number in range(reach_back):
        current = shifted_2((current[0], current[1]), "expert", 1)
        earlier.insert(0, current)
    pair_all = jnp.concatenate([shifted[0] for shifted in earlier] + [own_pair], axis=1)
    docs_all = jnp.concatenate([shifted[1] for shifted in earlier] + [own_docs], axis=0)
    position = lax.axis_index("expert")
    attended = attend_local(
        queries[0],
        pair_all[0],
        pair_all[1],
        own_docs,
        docs_all,
        position * rows_dev,
        (position - reach_back) * rows_dev,
    )
    flat_att = attended.astype(jnp.float32)
    normed = (
        flat_att
        * lax.rsqrt(jnp.mean(flat_att * flat_att, axis=-1, keepdims=True) + 1e-05)
        * norm_gain
    ).astype(jnp.bfloat16)
    experts = lax.axis_size("expert")
    most = max(2, 3 * rows_dev * TOP // (2 * experts))
    chosen_flat = expert_index[0].reshape(-1)
    onehot = (chosen_flat[:, None] == jnp.arange(experts, dtype=jnp.int32)[None, :]).astype(
        jnp.int32
    )
    ranks = jnp.sum(onehot * (jnp.cumsum(onehot, axis=0) - 1), axis=1)
    limits = jnp.sum(onehot * capacity[None, :], axis=1)
    kept = ranks < limits
    slot = jnp.where(kept, chosen_flat * most + ranks, experts * most)
    token_of = jnp.arange(rows_dev * TOP, dtype=jnp.int32) // TOP
    slot_token = jnp.full((experts * most,), -1, jnp.int32).at[slot].set(token_of, mode="drop")
    filled = slot_token >= 0
    outgoing = jnp.where(
        filled[:, None], normed[jnp.maximum(slot_token, 0)], jnp.zeros((), jnp.bfloat16)
    )
    outgoing = outgoing.reshape(experts, most, width)
    received = lax.all_to_all(outgoing, "expert", split_axis=0, concat_axis=0, tiled=True)
    sources = received.shape[0]
    flat_rows = received.reshape(sources * most, width)
    columns = flat_rows
    gate_sum = jnp.dot(
        columns,
        lax.all_gather(gate_weight, "dp", axis=1, tiled=True)[0],
        preferred_element_type=jnp.float32,
    )
    up_sum = jnp.dot(
        columns,
        lax.all_gather(up_weight, "dp", axis=1, tiled=True)[0],
        preferred_element_type=jnp.float32,
    )
    hidden = (jax.nn.silu(gate_sum) * up_sum).astype(jnp.bfloat16)
    columns = hidden
    result = jnp.dot(
        columns,
        lax.all_gather(down_weight, "dp", axis=1, tiled=True)[0],
        preferred_element_type=jnp.float32,
    )
    answered = result.astype(jnp.bfloat16).reshape(sources, most, width)
    returned = lax.all_to_all(answered, "expert", split_axis=0, concat_axis=0, tiled=True)
    back_flat = returned.reshape(experts * most, width)
    picked = back_flat[jnp.minimum(slot, experts * most - 1)].reshape(rows_dev, TOP, width)
    weight = jnp.where(kept, gates[0].reshape(-1), 0.0).reshape(rows_dev, TOP)
    combined = flat_att
    for which in range(TOP):
        combined = combined + picked[:, which].astype(jnp.float32) * weight[:, which : which + 1]
    return combined.astype(jnp.bfloat16)[None]


def solution(mesh):
    placed = (
        P("dp", "expert", None),
        P("dp", "expert", None),
        P("dp", "expert", None),
        P("dp", "expert"),
        P("dp", "expert", None),
        P("dp", "expert", None),
        P(),
        P(),
        P("expert", "dp", None),
        P("expert", "dp", None),
        P("expert", "dp", None),
    )
    return jax.shard_map(
        per_device, mesh=mesh, in_specs=placed, out_specs=P("dp", "expert", None), check_vma=False
    )
```

profile of v0, /device:TPU:0, one launch (start us, length us, event | category | flops | bytes accessed | tf_op | source)
XLA Modules:
  0.0 246.8 jit_solution(877625172009056272)
XLA Ops:
  8.1 1.3 copy.33
  9.4 1.3 copy.32
  10.8 4.9 %collective-permute-start = (bf16[2,128,2048]{1,2,0:T(8,128)(2,1)S(1)}, bf16[2,128,2048]{1,2,0:T(8,128)(2,1)S(1)}, u32[]{:S(2)}, u32[]{:S(2)}) collective-permute-start(bf16[2,128,2048]{1,2,0:T(8,128)(2,1)S(1)} %pad_maximum_fusion), channel_id=1, source_target_pairs={{0,1},{1,2},{2,3},{3,4},{4,5},{5,6},{6,7},{8,9},{9,10},{10,11},{11... | collective-permute-start | bytes 3145736 | tf_op jit(solution)/shard_map/ppermute | solution.py:16
  15.7 22.3 %collective-permute-done = bf16[2,128,2048]{1,2,0:T(8,128)(2,1)S(1)} collective-permute-done((bf16[2,128,2048]{1,2,0:T(8,128)(2,1)S(1)}, bf16[2,128,2048]{1,2,0:T(8,128)(2,1)S(1)}, u32[]{:S(2)}, u32[]{:S(2)}) %collective-permute-start) | collective-permute-done | bytes 1048608 | tf_op jit(solution)/shard_map/ppermute | solution.py:16
  38.1 5.4 %collective-permute-start.1 = (bf16[2,128,2048]{1,2,0:T(8,128)(2,1)S(1)}, bf16[2,128,2048]{1,2,0:T(8,128)(2,1)}, u32[]{:S(2)}, u32[]{:S(2)}) collective-permute-start(bf16[2,128,2048]{1,2,0:T(8,128)(2,1)S(1)} %collective-permute-done), channel_id=1, source_target_pairs={{0,1},{1,2},{2,3},{3,4},{4,5},{5,6},{6,7},{8,9},{9,10},{10,11},{11... | collective-permute-start | bytes 3145736 | tf_op jit(solution)/shard_map/ppermute | solution.py:16
  43.5 3.3 %collective-permute-start.4 = (bf16[128]{0:T(256)(128)(2,1)S(1)}, bf16[128]{0:T(256)(128)(2,1)S(1)}, u32[]{:S(2)}, u32[]{:S(2)}) collective-permute-start(bf16[128]{0:T(256)(128)(2,1)S(1)} %convert_bitcast_fusion), channel_id=1, source_target_pairs={{0,1},{1,2},{2,3},{3,4},{4,5},{5,6},{6,7},{8,9},{9,10},{10,11},{11... | collective-permute-start | bytes 776 | tf_op jit(solution)/shard_map/ppermute | solution.py:16
  46.9 17.2 %collective-permute-done.1 = bf16[2,128,2048]{1,2,0:T(8,128)(2,1)} collective-permute-done((bf16[2,128,2048]{1,2,0:T(8,128)(2,1)S(1)}, bf16[2,128,2048]{1,2,0:T(8,128)(2,1)}, u32[]{:S(2)}, u32[]{:S(2)}) %collective-permute-start.1) | collective-permute-done | bytes 1048608 | tf_op jit(solution)/shard_map/ppermute | solution.py:16
  64.1 5.5 %collective-permute-start.2 = (bf16[2,128,2048]{1,2,0:T(8,128)(2,1)}, bf16[2,128,2048]{1,2,0:T(8,128)(2,1)}, u32[]{:S(2)}, u32[]{:S(2)}) collective-permute-start(bf16[2,128,2048]{1,2,0:T(8,128)(2,1)} %collective-permute-done.1), channel_id=1, source_target_pairs={{0,1},{1,2},{2,3},{3,4},{4,5},{5,6},{6,7},{8,9},{9,10},{10,11},{11... | collective-permute-start | bytes 3145736 | tf_op jit(solution)/shard_map/ppermute | solution.py:16
  71.2 18.4 %collective-permute-done.2 = bf16[2,128,2048]{1,2,0:T(8,128)(2,1)} collective-permute-done((bf16[2,128,2048]{1,2,0:T(8,128)(2,1)}, bf16[2,128,2048]{1,2,0:T(8,128)(2,1)}, u32[]{:S(2)}, u32[]{:S(2)}) %collective-permute-start.2) | collective-permute-done | bytes 1048608 | tf_op jit(solution)/shard_map/ppermute | solution.py:16
  89.6 6.0 %collective-permute-start.3 = (bf16[2,128,2048]{1,2,0:T(8,128)(2,1)}, bf16[2,128,2048]{1,2,0:T(8,128)(2,1)}, u32[]{:S(2)}, u32[]{:S(2)}) collective-permute-start(bf16[2,128,2048]{1,2,0:T(8,128)(2,1)} %collective-permute-done.2), channel_id=1, source_target_pairs={{0,1},{1,2},{2,3},{3,4},{4,5},{5,6},{6,7},{8,9},{9,10},{10,11},{11... | collective-permute-start | bytes 3145736 | tf_op jit(solution)/shard_map/ppermute | solution.py:16
  95.6 1.4 scatter_custom_fusion
  97.1 4.3 %collective-permute-start.5 = (bf16[128]{0:T(256)(128)(2,1)S(1)}, bf16[128]{0:T(256)(128)(2,1)S(1)}, u32[]{:S(2)}, u32[]{:S(2)}) collective-permute-start(bf16[128]{0:T(256)(128)(2,1)S(1)} %collective-permute-done.4), channel_id=1, source_target_pairs={{0,1},{1,2},{2,3},{3,4},{4,5},{5,6},{6,7},{8,9},{9,10},{10,11},{11... | collective-permute-start | bytes 776 | tf_op jit(solution)/shard_map/ppermute | solution.py:16
  101.4 13.2 %collective-permute-done.5 = bf16[128]{0:T(256)(128)(2,1)S(1)} collective-permute-done((bf16[128]{0:T(256)(128)(2,1)S(1)}, bf16[128]{0:T(256)(128)(2,1)S(1)}, u32[]{:S(2)}, u32[]{:S(2)}) %collective-permute-start.5) | collective-permute-done | bytes 288 | tf_op jit(solution)/shard_map/ppermute | solution.py:16
  114.6 5.3 %collective-permute-start.6 = (bf16[128]{0:T(256)(128)(2,1)S(1)}, bf16[128]{0:T(256)(128)(2,1)S(1)}, u32[]{:S(2)}, u32[]{:S(2)}) collective-permute-start(bf16[128]{0:T(256)(128)(2,1)S(1)} %collective-permute-done.5), channel_id=1, source_target_pairs={{0,1},{1,2},{2,3},{3,4},{4,5},{5,6},{6,7},{8,9},{9,10},{10,11},{11... | collective-permute-start | bytes 776 | tf_op jit(solution)/shard_map/ppermute | solution.py:16
  119.9 1.3 collective-permute-done.6
  121.2 5.5 %collective-permute-start.7 = (bf16[128]{0:T(256)(128)(2,1)S(1)}, bf16[128]{0:T(256)(128)(2,1)S(1)}, u32[]{:S(2)}, u32[]{:S(2)}) collective-permute-start(bf16[128]{0:T(256)(128)(2,1)S(1)} %collective-permute-done.6), channel_id=1, source_target_pairs={{0,1},{1,2},{2,3},{3,4},{4,5},{5,6},{6,7},{8,9},{9,10},{10,11},{11... | collective-permute-start | bytes 776 | tf_op jit(solution)/shard_map/ppermute | solution.py:16
  129.0 1.4 constant_dynamic-update-slice_fusion.4
  130.4 1.5 constant_dynamic-update-slice_fusion.3
  131.9 1.5 constant_dynamic-update-slice_fusion.2
  135.3 2.4 fusion.36
  139.1 2.5 gather_fusion
  141.6 1.4 broadcast_select_fusion
  142.9 8.1 %all-to-all-start = ((bf16[8,48,2048]{2,1,0:T(8,128)(2,1)}), bf16[8,48,2048]{2,1,0:T(8,128)(2,1)S(1)}, u32[]{:S(2)}, u32[]{:S(2)}) async-start(bf16[8,48,2048]{2,1,0:T(8,128)(2,1)} %broadcast_select_fusion), calls=%async_computation | async-start | bytes 3145728 | tf_op jit(solution)/shard_map/all_to_all | solution.py:108
  151.1 31.3 %all-to-all-done = bf16[8,48,2048]{2,1,0:T(8,128)(2,1)S(1)} async-done(((bf16[8,48,2048]{2,1,0:T(8,128)(2,1)}), bf16[8,48,2048]{2,1,0:T(8,128)(2,1)S(1)}, u32[]{:S(2)}, u32[]{:S(2)}) %all-to-all-start) | async-done | bytes 1572896 | tf_op jit(solution)/shard_map/all_to_all | solution.py:108
  182.4 5.2 %fusion.5 = f32[384,1024]{1,0:T(8,128)} fusion(bf16[384,2048]{1,0:T(8,128)(2,1)S(1)} %bitcast.76, bf16[1,2048,1024]{2,1,0:T(8,128)(2,1)} %all-gather.4.cloned.1.call-done), kind=kOutput, calls=%fused_computation.11 | convolution fusion | flops 1610612736 | bytes 7340032 | tf_op jit(solution)/shard_map/dot_general | solution.py:112
  187.5 8.6 %fusion.8 = bf16[384,2048]{1,0:T(8,128)(2,1)} fusion(bf16[1,1024,2048]{2,1,0:T(8,128)(2,1)} %all-gather.8.cloned.1.call-done, f32[384,1024]{1,0:T(8,128)} %fusion.5, bf16[384,2048]{1,0:T(8,128)(2,1)S(1)} %bitcast.77, bf16[1,2048,1024]{2,1,0:T(8,128)(2,1)} %all-gather.6.cloned.1.call-done), kind=kOutput, calls=%fused_computation.14 | convolution fusion | flops 3224371200 | bytes 13107200 | tf_op jit(solution)/shard_map/dot_general | solution.py:124
  196.1 3.6 %all-to-all-start.1 = ((bf16[8,48,2048]{2,1,0:T(8,128)(2,1)}), bf16[8,48,2048]{2,1,0:T(8,128)(2,1)S(1)}, u32[]{:S(2)}, u32[]{:S(2)}) async-start(bf16[8,48,2048]{2,1,0:T(8,128)(2,1)} %bitcast.75), calls=%async_computation.1 | async-start | bytes 3145728 | tf_op jit(solution)/shard_map/all_to_all | solution.py:130
  200.2 1.3 copy.43
  201.5 33.2 %all-to-all-done.1 = bf16[8,48,2048]{2,1,0:T(8,128)(2,1)S(1)} async-done(((bf16[8,48,2048]{2,1,0:T(8,128)(2,1)}), bf16[8,48,2048]{2,1,0:T(8,128)(2,1)S(1)}, u32[]{:S(2)}, u32[]{:S(2)}) %all-to-all-start.1) | async-done | bytes 1572896 | tf_op jit(solution)/shard_map/all_to_all | solution.py:130
  234.8 1.4 gather_fusion.1
  236.9 1.5 fusion.35
  238.4 1.9 fusion.20
  (73 shorter events, 10.1 us)
Async XLA Ops:
  6.5 36.9 %copy-start.6 = (s32[1,128]{1,0:T(1,128)S(1)}, s32[1,128]{1,0:T(1,128)}, u32[]{:S(2)}) copy-start(s32[1,128]{1,0:T(1,128)} %param.14) | copy-start | bytes 1540
  6.5 63.0 %copy-start.3 = (s32[1,128,2]{1,2,0:T(2,128)S(1)}, s32[1,128,2]{1,2,0:T(2,128)}, u32[]{:S(2)}) copy-start(s32[1,128,2]{1,2,0:T(2,128)} %param.15) | copy-start | bytes 3076
  6.5 64.5 %copy-start.5 = (s32[8]{0:T(128)S(1)}, s32[8]{0:T(128)}, u32[]{:S(2)}) copy-start(s32[8]{0:T(128)} %param.17) | copy-start | bytes 100
  6.5 120.1 %copy-start.1 = (bf16[1,128,2048]{2,1,0:T(8,128)(2,1)S(1)}, bf16[1,128,2048]{2,1,0:T(8,128)(2,1)}, u32[]{:S(2)}) copy-start(bf16[1,128,2048]{2,1,0:T(8,128)(2,1)} %param.11) | copy-start | bytes 1572868
  6.5 144.5 %all-gather.4.cloned.1.call-start = ((), (), s32[]{:S(2)}) async-start(), calls=%async_computation.2 | async-start | bytes 5242880 | tf_op jit(solution)/shard_map/all_gather | solution.py:114
  7.3 180.3 %all-gather.8.cloned.1.call-start = ((), (), s32[]{:S(2)}) async-start(), calls=%async_computation.4 | async-start | bytes 5242880 | tf_op jit(solution)/shard_map/all_gather | solution.py:126
  8.0 179.5 %all-gather.6.cloned.1.call-start = ((), (), s32[]{:S(2)}) async-start(), calls=%async_computation.3 | async-start | bytes 5242880 | tf_op jit(solution)/shard_map/all_gather | solution.py:119
  10.8 27.2 %collective-permute-start = (bf16[2,128,2048]{1,2,0:T(8,128)(2,1)S(1)}, bf16[2,128,2048]{1,2,0:T(8,128)(2,1)S(1)}, u32[]{:S(2)}, u32[]{:S(2)}) collective-permute-start(bf16[2,128,2048]{1,2,0:T(8,128)(2,1)S(1)} %pad_maximum_fusion), channel_id=1, source_target_pairs={{0,1},{1,2},{2,3},{3,4},{4,5},{5,6},{6,7},{8,9},{9,10},{10,11},{11... | collective-permute-start | bytes 3145736 | tf_op jit(solution)/shard_map/ppermute | solution.py:16
  38.1 26.0 %collective-permute-start.1 = (bf16[2,128,2048]{1,2,0:T(8,128)(2,1)S(1)}, bf16[2,128,2048]{1,2,0:T(8,128)(2,1)}, u32[]{:S(2)}, u32[]{:S(2)}) collective-permute-start(bf16[2,128,2048]{1,2,0:T(8,128)(2,1)S(1)} %collective-permute-done), channel_id=1, source_target_pairs={{0,1},{1,2},{2,3},{3,4},{4,5},{5,6},{6,7},{8,9},{9,10},{10,11},{11... | collective-permute-start | bytes 3145736 | tf_op jit(solution)/shard_map/ppermute | solution.py:16
  43.5 53.6 %collective-permute-start.4 = (bf16[128]{0:T(256)(128)(2,1)S(1)}, bf16[128]{0:T(256)(128)(2,1)S(1)}, u32[]{:S(2)}, u32[]{:S(2)}) collective-permute-start(bf16[128]{0:T(256)(128)(2,1)S(1)} %convert_bitcast_fusion), channel_id=1, source_target_pairs={{0,1},{1,2},{2,3},{3,4},{4,5},{5,6},{6,7},{8,9},{9,10},{10,11},{11... | collective-permute-start | bytes 776 | tf_op jit(solution)/shard_map/ppermute | solution.py:16
  64.1 25.5 %collective-permute-start.2 = (bf16[2,128,2048]{1,2,0:T(8,128)(2,1)}, bf16[2,128,2048]{1,2,0:T(8,128)(2,1)}, u32[]{:S(2)}, u32[]{:S(2)}) collective-permute-start(bf16[2,128,2048]{1,2,0:T(8,128)(2,1)} %collective-permute-done.1), channel_id=1, source_target_pairs={{0,1},{1,2},{2,3},{3,4},{4,5},{5,6},{6,7},{8,9},{9,10},{10,11},{11... | collective-permute-start | bytes 3145736 | tf_op jit(solution)/shard_map/ppermute | solution.py:16
  89.6 39.4 %collective-permute-start.3 = (bf16[2,128,2048]{1,2,0:T(8,128)(2,1)}, bf16[2,128,2048]{1,2,0:T(8,128)(2,1)}, u32[]{:S(2)}, u32[]{:S(2)}) collective-permute-start(bf16[2,128,2048]{1,2,0:T(8,128)(2,1)} %collective-permute-done.2), channel_id=1, source_target_pairs={{0,1},{1,2},{2,3},{3,4},{4,5},{5,6},{6,7},{8,9},{9,10},{10,11},{11... | collective-permute-start | bytes 3145736 | tf_op jit(solution)/shard_map/ppermute | solution.py:16
  97.1 17.6 %collective-permute-start.5 = (bf16[128]{0:T(256)(128)(2,1)S(1)}, bf16[128]{0:T(256)(128)(2,1)S(1)}, u32[]{:S(2)}, u32[]{:S(2)}) collective-permute-start(bf16[128]{0:T(256)(128)(2,1)S(1)} %collective-permute-done.4), channel_id=1, source_target_pairs={{0,1},{1,2},{2,3},{3,4},{4,5},{5,6},{6,7},{8,9},{9,10},{10,11},{11... | collective-permute-start | bytes 776 | tf_op jit(solution)/shard_map/ppermute | solution.py:16
  114.6 6.6 %collective-permute-start.6 = (bf16[128]{0:T(256)(128)(2,1)S(1)}, bf16[128]{0:T(256)(128)(2,1)S(1)}, u32[]{:S(2)}, u32[]{:S(2)}) collective-permute-start(bf16[128]{0:T(256)(128)(2,1)S(1)} %collective-permute-done.5), channel_id=1, source_target_pairs={{0,1},{1,2},{2,3},{3,4},{4,5},{5,6},{6,7},{8,9},{9,10},{10,11},{11... | collective-permute-start | bytes 776 | tf_op jit(solution)/shard_map/ppermute | solution.py:16
  121.2 6.6 %collective-permute-start.7 = (bf16[128]{0:T(256)(128)(2,1)S(1)}, bf16[128]{0:T(256)(128)(2,1)S(1)}, u32[]{:S(2)}, u32[]{:S(2)}) collective-permute-start(bf16[128]{0:T(256)(128)(2,1)S(1)} %collective-permute-done.6), channel_id=1, source_target_pairs={{0,1},{1,2},{2,3},{3,4},{4,5},{5,6},{6,7},{8,9},{9,10},{10,11},{11... | collective-permute-start | bytes 776 | tf_op jit(solution)/shard_map/ppermute | solution.py:16
  137.7 1.3 copy-start.2
  142.9 39.4 %all-to-all-start = ((bf16[8,48,2048]{2,1,0:T(8,128)(2,1)}), bf16[8,48,2048]{2,1,0:T(8,128)(2,1)S(1)}, u32[]{:S(2)}, u32[]{:S(2)}) async-start(bf16[8,48,2048]{2,1,0:T(8,128)(2,1)} %broadcast_select_fusion), calls=%async_computation | async-start | bytes 3145728 | tf_op jit(solution)/shard_map/all_to_all | solution.py:108
  187.5 12.4 %copy-start.4 = (f32[1,128,2]{1,2,0:T(2,128)S(1)}, f32[1,128,2]{1,2,0:T(2,128)}, u32[]{:S(2)}) copy-start(f32[1,128,2]{1,2,0:T(2,128)} %param.16) | copy-start | bytes 3076
  196.1 38.6 %all-to-all-start.1 = ((bf16[8,48,2048]{2,1,0:T(8,128)(2,1)}), bf16[8,48,2048]{2,1,0:T(8,128)(2,1)S(1)}, u32[]{:S(2)}, u32[]{:S(2)}) async-start(bf16[8,48,2048]{2,1,0:T(8,128)(2,1)} %bitcast.75), calls=%async_computation.1 | async-start | bytes 3145728 | tf_op jit(solution)/shard_map/all_to_all | solution.py:130
  236.8 1.5 copy-start
Sparse Core Ops, SparseCore 0:
  8.9 37.1 all-gather.3
  47.7 34.4 all-gather.7
  83.8 34.4 all-gather.5
where the time goes:
time: 247 us
  waiting for transfers between devices  139 us (56%)
  starting transfers between devices  52 us (21%)
  local copies, waits for them, and re-layouts  19.2 us (8%)
  matrix products  15.6 us (6%)
  between operations  13.5 us (5%)
  other arithmetic  7.27 us (3%)
    ppermute x8, waiting for transfers between devices, shifted_2(): return lax.ppermute(block, axis, route)  73.3 us
    ppermute x8, starting transfers between devices, shifted_2(): return lax.ppermute(block, axis, route)  40.2 us
    all_to_all x1, waiting for transfers between devices, per_device(): lax.all_to_all(answered, 'expert', split_axis=0, concat_axis=0, tiled=True)  33.2 us
    all_to_all x1, waiting for transfers between devices, per_device(): lax.all_to_all(outgoing, 'expert', split_axis=0, concat_axis=0, tiled=True)  31.3 us
    dot_general x1, matrix products, per_device(): jnp.dot(columns, lax.all_gather(down_weight, 'dp', axis=1, tiled=True)[0]...  8.6 us
    unnamed x27, local copies, waits for them, and re-layouts  8.33 us
    all_to_all x1, starting transfers between devices, per_device(): lax.all_to_all(outgoing, 'expert', split_axis=0, concat_axis=0, tiled=True)  8.13 us
    dot_general x1, matrix products, per_device(): jnp.dot(columns, lax.all_gather(gate_weight, 'dp', axis=1, tiled=True)[0]...  5.17 us
  transfers between devices with their start and end apart: 13, of which 8 were waited for; matrix products, arithmetic and copies ran while one was open for 11% of the time, Pallas kernels for 0%

commit v1 on v0

--- a/solution.py
+++ b/solution.py
@@ -1,13 +1,20 @@
+import functools
 import math
 
 import jax
 import jax.numpy as jnp
 from jax import lax
+from jax.experimental import pallas as pl
+from jax.experimental.pallas import tpu as pltpu
 from jax.sharding import PartitionSpec as P
 
 HEAD_DIM = 128
 TOP = 2
 WINDOW = 512
+META = 16
+LANES = 128
+F32 = jnp.float32
+BF16 = jnp.bfloat16
 
 
 def shifted_2(block, axis, distance):
@@ -47,7 +54,7 @@
     return blocks.reshape(rows_dev, width)
 
 
-def per_device(
+def per_device_general(
     queries,
     keys,
     values,
@@ -137,6 +144,366 @@
     return combined.astype(jnp.bfloat16)[None]
 
 
+def pack_kernel(*refs):
+    out_ref, slots_ref = refs[7:9]
+    copies = [pltpu.make_async_copy(refs[i], refs[9 + i], refs[16].at[i]) for i in range(7)]
+    for number in (3, 4, 5, 6, 0, 1, 2):
+        copies[number].start()
+    q_ref, k_ref, v_ref, docs_ref, index_ref, gates_ref, limits_ref = refs[9:16]
+    rows = q_ref.shape[1]
+    owners, _, part = out_ref.shape
+    experts = limits_ref.shape[1]
+    most = most_of(rows, experts)
+    for number in (3, 4, 5, 6):
+        copies[number].wait()
+    line = lax.broadcasted_iota(jnp.int32, (META, rows), 0)
+    given = jnp.zeros((META, rows), F32)
+    for k in range(TOP):
+        given = jnp.where(line == k, index_ref[k : k + 1].astype(F32), given)
+        given = jnp.where(line == TOP + k, gates_ref[k : k + 1], given)
+    given = jnp.concatenate([given, jnp.zeros((rows - META, rows), F32)], axis=0).T
+    index = [given[:, k : k + 1] for k in range(TOP)]
+    names = lax.broadcasted_iota(jnp.int32, (rows, experts), 1).astype(F32)
+    chosen = [jnp.where(index[k] == names, 1.0, 0.0) for k in range(TOP)]
+    below = lax.broadcasted_iota(jnp.int32, (rows, rows), 1) < lax.broadcasted_iota(jnp.int32, (rows, rows), 0)
+    earlier = jnp.dot(
+        jnp.where(below, 1.0, 0.0).astype(BF16), (chosen[0] + chosen[1]).astype(BF16), preferred_element_type=F32
+    )
+    limits = limits_ref[...].astype(F32)
+    columns = []
+    slots = []
+    weights = []
+    for k in range(TOP):
+        rank = jnp.sum(chosen[k] * earlier, axis=1, keepdims=True)
+        limit = jnp.sum(chosen[k] * limits, axis=1, keepdims=True)
+        slots.append(index[k] * most + rank)
+        columns += [index[k], rank]
+        weights.append(jnp.where(rank < limit, given[:, TOP + k : TOP + k + 1], 0.0))
+    for weight in weights:
+        first = weight.astype(BF16).astype(F32)
+        second = (weight - first).astype(BF16).astype(F32)
+        columns += [first, second, weight - first - second]
+    lane = lax.broadcasted_iota(jnp.int32, (rows, LANES), 1)
+    table = jnp.zeros((rows, LANES), F32)
+    for number, column in enumerate(columns):
+        table = jnp.where(lane == number + 1, column, table)
+    turned = table.T[:META]
+    turned = jnp.where(line == 0, docs_ref[...].astype(F32), turned).astype(BF16)
+    slots_ref[...] = jnp.where(lane == 0, slots[0], jnp.where(lane == 1, slots[1], -1.0))
+    for owner in range(owners):
+        out_ref[owner, TOP_ROWS * rows :, :rows] = turned
+        out_ref[owner, TOP_ROWS * rows :, rows:] = jnp.zeros((META, part - rows), BF16)
+    for which, ref in enumerate((q_ref, k_ref, v_ref)):
+        copies[which].wait()
+        for owner in range(owners):
+            out_ref[owner, which * rows : (which + 1) * rows, :] = ref[0, :, owner * part : (owner + 1) * part]
+
+
+TOP_ROWS = 3
+
+
+def most_of(rows, experts):
+    return max(2, 3 * rows * TOP // (2 * experts))
+
+
+def pack(queries, keys, values, doc_ids, expert_index, gates, capacity, owners):
+    rows, width = queries.shape[1:]
+    part = width // owners
+    vmem = pl.BlockSpec(memory_space=pltpu.VMEM)
+    given = (queries, keys, values, doc_ids, expert_index[0].T, gates[0].T, capacity[None, :])
+    return pl.pallas_call(
+        pack_kernel,
+        out_shape=(
+            jax.ShapeDtypeStruct((owners, TOP_ROWS * rows + META, part), BF16),
+            jax.ShapeDtypeStruct((rows, LANES), F32),
+        ),
+        in_specs=[pl.BlockSpec(memory_space=pltpu.HBM)] * 7,
+        out_specs=(vmem, vmem),
+        scratch_shapes=[pltpu.VMEM(array.shape, array.dtype) for array in given] + [pltpu.SemaphoreType.DMA((7,))],
+        compiler_params=pltpu.CompilerParams(vmem_limit_bytes=60 * 1024 * 1024),
+        name="pack_by_heads",
+    )(*given)
+
+
+def attend_kernel(most, all_ref, out_ref):
+    blocks, _, part = all_ref.shape
+    rows = (all_ref.shape[1] - META) // TOP_ROWS
+    experts = out_ref.shape[0]
+    heads = part // HEAD_DIM
+    reach = (WINDOW - 1) // rows + 1
+    factor = math.log2(math.e) / math.sqrt(HEAD_DIM)
+    apart = lax.broadcasted_iota(jnp.int32, (rows, rows), 0) - lax.broadcasted_iota(jnp.int32, (rows, rows), 1)
+    slot_of = lax.broadcasted_iota(jnp.int32, (experts * most, rows), 0).astype(F32)
+
+    @pl.loop(0, blocks)
+    def _(number):
+        meta = all_ref[number, TOP_ROWS * rows :, :rows].astype(F32)
+        padded = jnp.concatenate([meta, jnp.zeros((rows - META, rows), F32)], axis=0)
+        query_docs = padded.T[:, 0:1]
+        sources = []
+        allowed = []
+        for step in range(reach + 1):
+            source = number - reach + step
+            held = jnp.maximum(source, 0)
+            docs = all_ref[held, TOP_ROWS * rows :, :rows].astype(F32)[0:1]
+            docs = jnp.where(source >= 0, docs, -1.0)
+            mask = query_docs == docs
+            offset = (reach - step) * rows
+            if offset - (rows - 1) < 0:
+                mask = mask & (apart + offset >= 0)
+            if offset + (rows - 1) >= WINDOW:
+                mask = mask & (apart + offset < WINDOW)
+            sources.append(held)
+            allowed.append(mask)
+        done = []
+        for head in range(heads):
+            lanes = slice(head * HEAD_DIM, (head + 1) * HEAD_DIM)
+            query = all_ref[number, 0:rows, lanes]
+            scores = []
+            for held, mask in zip(sources, allowed):
+                key = all_ref[held, rows : 2 * rows, lanes]
+                score = lax.dot_general(query, key, (((1,), (1,)), ((), ())), preferred_element_type=F32)
+                scores.append(jnp.where(mask, score, -1e30))
+            highest = functools.reduce(jnp.maximum, scores)
+            highest = jnp.max(highest, axis=1, keepdims=True)
+            expo = [jnp.exp2((score - highest) * factor) for score in scores]
+            total = jnp.sum(functools.reduce(jnp.add, expo), axis=1, keepdims=True)
+            result = jnp.zeros((rows, HEAD_DIM), F32)
+            for held, weight in zip(sources, expo):
+                value = all_ref[held, 2 * rows : 3 * rows, lanes]
+                result = result + jnp.dot(weight.astype(BF16), value, preferred_element_type=F32)
+            done.append((result / total).astype(BF16))
+        attended = jnp.concatenate(done, axis=1)
+        slots = [meta[1 + 2 * k : 2 + 2 * k] * most + meta[2 + 2 * k : 3 + 2 * k] for k in range(TOP)]
+        picks = (slot_of == slots[0]) | (slot_of == slots[1])
+        routed = jnp.dot(jnp.where(picks, 1.0, 0.0).astype(BF16), attended, preferred_element_type=F32).astype(BF16)
+        for expert in range(experts):
+            out_ref[expert, number] = routed[expert * most : (expert + 1) * most]
+
+
+def attend(gathered, experts, most):
+    blocks, _, part = gathered.shape
+    vmem = pl.BlockSpec(memory_space=pltpu.VMEM)
+    return pl.pallas_call(
+        functools.partial(attend_kernel, most),
+        out_shape=jax.ShapeDtypeStruct((experts, blocks, most, part), BF16),
+        in_specs=[vmem],
+        out_specs=vmem,
+        compiler_params=pltpu.CompilerParams(vmem_limit_bytes=32 * 1024 * 1024),
+        name="attend_and_route",
+    )(gathered)
+
+
+def expert_kernel(
+    pieces, most, place_ref, rows_ref, meta_ref, gain_ref, *refs
+):
+    gate_refs, up_refs, down_refs = refs[:pieces], refs[pieces : 2 * pieces], refs[2 * pieces : 3 * pieces]
+    out_ref, gate_all, up_all, down_all, normed, hidden, sems = refs[3 * pieces :]
+    parts, count, part = rows_ref.shape
+    blocks = meta_ref.shape[0]
+    deep, wide = gate_all.shape[2], gate_all.shape[3]
+    width = parts * part
+    mine, expert = place_ref[0], place_ref[1]
+
+    def gate_copies(step):
+        tile = pl.ds(pl.multiple_of((mine ^ step) * wide, wide), wide)
+        found = []
+        for piece in range(pieces):
+            found.append(
+                pltpu.make_async_copy(gate_refs[piece].at[0, :, tile], gate_all.at[step, piece], sems.at[0, step, piece])
+            )
+            found.append(
+                pltpu.make_async_copy(up_refs[piece].at[0, :, tile], up_all.at[step, piece], sems.at[1, step, piece])
+            )
+        return found
+
+    def down_copy(piece):
+        return pltpu.make_async_copy(down_refs[piece].at[0], down_all.at[piece], sems.at[2, 0, piece])
+
+    for step in range(pieces):
+        for copy in gate_copies(step):
+            copy.start()
+    for piece in range(pieces):
+        down_copy(piece).start()
+
+    squares = jnp.zeros((count, part), F32)
+    for number in range(parts):
+        held = rows_ref[number].astype(F32)
+        squares = squares + held * held
+    inverse = lax.rsqrt(jnp.sum(squares, axis=1, keepdims=True) / width + 1e-05)
+    per_piece = deep // part
+    for number in range(parts):
+        held = rows_ref[number].astype(F32) * inverse * gain_ref[:, number * part : (number + 1) * part]
+        place = number % per_piece
+        normed[number // per_piece, :, place * part : (place + 1) * part] = held.astype(BF16)
+
+    @pl.loop(0, pieces)
+    def _(step):
+        for copy in gate_copies(step):
+            copy.wait()
+        gate = jnp.zeros((count, wide), F32)
+        up = jnp.zeros((count, wide), F32)
+        for piece in range(pieces):
+            held = normed[mine ^ piece]
+            gate = gate + jnp.dot(held, gate_all[step, piece], preferred_element_type=F32)
+            up = up + jnp.dot(held, up_all[step, piece], preferred_element_type=F32)
+        hidden[step] = (gate / (1.0 + jnp.exp(-gate)) * up).astype(BF16)
+
+    for piece in range(pieces):
+        down_copy(piece).wait()
+
+    rows = meta_ref.shape[2] if meta_ref.shape[2] < LANES else LANES
+    slot_of = lax.broadcasted_iota(jnp.int32, (most, rows), 0).astype(F32) + (expert * most).astype(F32)
+    weights, firsts = [], []
+    for number in range(blocks):
+        meta = meta_ref[number, :, :rows].astype(F32)
+        total = jnp.zeros((most, rows), F32)
+        for k in range(TOP):
+            slot = meta[1 + 2 * k : 2 + 2 * k] * most + meta[2 + 2 * k : 3 + 2 * k]
+            at = 1 + 2 * TOP + 3 * k
+            weight = meta[at : at + 1] + meta[at + 1 : at + 2] + meta[at + 2 : at + 3]
+            total = total + jnp.where(slot_of == slot, weight, 0.0)
+            if k == 0:
+                firsts.append(jnp.sum(jnp.where(slot_of == slot, 1.0, 0.0), axis=1, keepdims=True))
+        weights.append(jnp.sum(total, axis=1, keepdims=True))
+    weight = jnp.concatenate(weights, axis=0)
+    first = jnp.concatenate(firsts, axis=0)
+
+    for number in range(parts):
+        lanes = slice(number * part, (number + 1) * part)
+        result = jnp.zeros((count, part), F32)
+        for piece in range(pieces):
+            result = result + jnp.dot(hidden[piece], down_all[piece, :, lanes], preferred_element_type=F32)
+        result = result.astype(BF16).astype(F32) * weight
+        out_ref[:, lanes] = (rows_ref[number].astype(F32) * first + result).astype(BF16)
+
+
+def run_expert(rows, gathered, gain, gates, ups, downs, most):
+    parts, count, part = rows.shape
+    pieces = len(gates)
+    width = parts * part
+    _, deep, hidden = gates[0].shape
+    wide = hidden // pieces
+    blocks, deepest, _ = gathered.shape
+    place = jnp.stack([lax.axis_index("dp"), lax.axis_index("expert")]).astype(jnp.int32)
+    vmem = pl.BlockSpec(memory_space=pltpu.VMEM)
+    anywhere = pl.BlockSpec(memory_space=pltpu.HBM)
+    meta_at = deepest // META - 1
+    grid = pltpu.PrefetchScalarGridSpec(
+        num_scalar_prefetch=1,
+        grid=(1,),
+        in_specs=[
+            pl.BlockSpec((parts, count, part), lambda i, _: (0, 0, 0)),
+            pl.BlockSpec((blocks, META, part), lambda i, _: (0, meta_at, 0)),
+            pl.BlockSpec((1, width), lambda i, _: (0, 0)),
+        ]
+        + [anywhere] * (3 * pieces),
+        out_specs=pl.BlockSpec((count, width), lambda i, _: (0, 0)),
+        scratch_shapes=[
+            pltpu.VMEM((pieces, pieces, deep, wide), BF16),
+            pltpu.VMEM((pieces, pieces, deep, wide), BF16),
+            pltpu.VMEM((pieces, wide, width), BF16),
+            pltpu.VMEM((pieces, count, deep), BF16),
+            pltpu.VMEM((pieces, count, wide), BF16),
+            pltpu.SemaphoreType.DMA((3, pieces, pieces)),
+        ],
+    )
+    return pl.pallas_call(
+        functools.partial(expert_kernel, pieces, most),
+        out_shape=jax.ShapeDtypeStruct((count, width), BF16),
+        grid_spec=grid,
+        compiler_params=pltpu.CompilerParams(vmem_limit_bytes=60 * 1024 * 1024),
+        name="expert_rows",
+    )(place, rows, gathered, gain[None, :], *gates, *ups, *downs)
+
+
+def combine_kernel(rows_ref, slots_ref, out_ref):
+    count = rows_ref.shape[0]
+    rows = slots_ref.shape[0]
+    slot_of = lax.broadcasted_iota(jnp.int32, (rows, count), 1).astype(F32)
+    picks = (slot_of == slots_ref[:, 0:1]) | (slot_of == slots_ref[:, 1:2])
+    picks = jnp.where(picks, 1.0, 0.0).astype(BF16)
+    out_ref[0] = jnp.dot(picks, rows_ref[...], preferred_element_type=F32).astype(BF16)
+
+
+def combine(returned, slots):
+    vmem = pl.BlockSpec(memory_space=pltpu.VMEM)
+    return pl.pallas_call(
+        combine_kernel,
+        out_shape=jax.ShapeDtypeStruct((1, slots.shape[0], returned.shape[1]), BF16),
+        in_specs=[vmem] * 2,
+        out_specs=vmem,
+        compiler_params=pltpu.CompilerParams(vmem_limit_bytes=32 * 1024 * 1024),
+        name="combine_choices",
+    )(returned, slots)
+
+
+def flipped(block, axis, bits):
+    return lax.ppermute(block, axis, [(i, i ^ bits) for i in range(lax.axis_size(axis))])
+
+
+def spread_weight(block, far):
+    size = lax.axis_size("dp")
+    bits = size // 2
+    pieces = {0: block, bits: far}
+    while bits > 1:
+        bits //= 2
+        for number in sorted(pieces):
+            pieces[number | bits] = flipped(pieces[number], "dp", bits)
+    return [pieces[number] for number in range(size)]
+
+
+def per_device(
+    queries,
+    keys,
+    values,
+    doc_ids,
+    expert_index,
+    gates,
+    capacity,
+    norm_gain,
+    gate_weight,
+    up_weight,
+    down_weight,
+):
+    rows, width = queries.shape[1:]
+    experts = lax.axis_size("expert")
+    most = most_of(rows, experts)
+    over = lax.axis_size("dp")
+    gate_far = flipped(gate_weight, "dp", over // 2)
+    up_far = flipped(up_weight, "dp", over // 2)
+    packed, slots = pack(queries, keys, values, doc_ids, expert_index, gates, capacity, experts)
+    gathered = lax.all_to_all(packed, "expert", 0, 0, tiled=True)
+    gathered, gate_far, up_far = lax.optimization_barrier((gathered, gate_far, up_far))
+    gate_pieces = spread_weight(gate_weight, gate_far)
+    up_pieces = spread_weight(up_weight, up_far)
+    down_pieces = spread_weight(down_weight, flipped(down_weight, "dp", over // 2))
+    routed = attend(gathered, experts, most)
+    received = lax.all_to_all(routed, "expert", 0, 0, tiled=True)
+    received = received.reshape(experts, experts * most, width // experts)
+    answered = run_expert(received, gathered, norm_gain, gate_pieces, up_pieces, down_pieces, most)
+    answered = answered.reshape(experts, most, width)
+    returned = lax.all_to_all(answered, "expert", 0, 0, tiled=True)
+    return combine(returned.reshape(experts * most, width), slots)
+
+
+def by_heads(mesh, queries, gate_weight):
+    over, experts = mesh.shape["dp"], mesh.shape["expert"]
+    rows, width = queries.shape[1] // experts, queries.shape[2]
+    hidden = gate_weight.shape[2]
+    return (
+        width % (experts * HEAD_DIM) == 0
+        and rows == LANES
+        and width // experts > rows
+        and (width // over) % (width // experts) == 0
+        and hidden % (over * LANES) == 0
+        and most_of(rows, experts) % 16 == 0
+        and over & (over - 1) == 0
+        and queries.shape[0] == over
+        and gate_weight.shape[0] == experts
+    )
+
+
 def solution(mesh):
     placed = (
         P("dp", "expert", None),
@@ -151,6 +518,11 @@
         P("expert", "dp", None),
         P("expert", "dp", None),
     )
-    return jax.shard_map(
-        per_device, mesh=mesh, in_specs=placed, out_specs=P("dp", "expert", None), check_vma=False
-    )
+
+    def layer(*arrays):
+        step = per_device if by_heads(mesh, arrays[0], arrays[8]) else per_device_general
+        return jax.shard_map(
+            step, mesh=mesh, in_specs=placed, out_specs=P("dp", "expert", None), check_vma=False
+        )(*arrays)
+
+    return layer

time: 247 us -> 164 us (0.66)
  waiting for transfers between devices: 139 us -> 76.8 us
  blocking collectives: 0 us -> 40.7 us
  starting transfers between devices: 52 us -> 17.7 us
  Pallas kernels: 0 us -> 25.7 us
  local copies, waits for them, and re-layouts: 19.2 us -> 2.12 us
  matrix products: 15.6 us -> 0 us
  between operations: 13.5 us -> 0.05 us
  other arithmetic: 7.27 us -> 0.61 us
    all_to_all x2, waiting for transfers between devices: 64.5 us -> 6.29 us  [the longest x1 6.29 us: per_device(): received = lax.all_to_all(routed, 'expert', 0, 0, tiled=True)]
    all_to_all x0 -> x1, blocking collectives: none -> 40.7 us  [per_device(): returned = lax.all_to_all(answered, 'expert', 0, 0, tiled=True)]
    ppermute x8 -> x9, starting transfers between devices: 40.2 us -> 4.64 us  [flipped(): lax.ppermute(block, axis, [(i, i ^ bits) for i in range(lax.axis_size(axi...]
    pallas_call x0 -> x4, Pallas kernels: none -> 25.7 us  [the longest x1 11.2 us: run_expert(): pl.pallas_call(functools.partial(expert_kernel, pieces, most), out_shape=...]
    dot_general x4 -> x0, matrix products: 15.6 us -> none  [the longest x1 8.6 us: per_device(): jnp.dot(columns, lax.all_gather(down_weight, 'dp', axis=1, tiled=True)[0]...]
    unnamed x27 -> x12, local copies, waits for them, and re-layouts: 8.33 us -> 2.12 us
    gather x2 -> x0, local copies, waits for them, and re-layouts: 3.81 us -> none  [the longest x1 2.45 us: per_device(): normed[jnp.maximum(slot_token, 0)]]
    ppermute x8 -> x9, waiting for transfers between devices: 73.3 us -> 70.5 us  [flipped(): lax.ppermute(block, axis, [(i, i ^ bits) for i in range(lax.axis_size(axi...]
  transfers between devices with their start and end apart: 13 -> 11, of which waited for: 8 -> 6; matrix products, arithmetic and copies ran while one was open for 11% -> 0% of each run, Pallas kernels for 0% -> 0%
where the time goes in v1:
time: 164 us
  waiting for transfers between devices  76.8 us (47%)
  blocking collectives  40.7 us (25%)
  Pallas kernels  25.7 us (16%)
  starting transfers between devices  17.7 us (11%)
  local copies, waits for them, and re-layouts  2.12 us (1%)
    ppermute x9, waiting for transfers between devices, flipped(): lax.ppermute(block, axis, [(i, i ^ bits) for i in range(lax.axis_size(axi...  70.5 us
    all_to_all x1, blocking collectives, per_device(): returned = lax.all_to_all(answered, 'expert', 0, 0, tiled=True)  40.7 us
    pallas_call x1, Pallas kernels, run_expert(): pl.pallas_call(functools.partial(expert_kernel, pieces, most), out_shape=...  11.2 us
    pallas_call x1, Pallas kernels, attend(): pl.pallas_call(functools.partial(attend_kernel, most), out_shape=jax.Shap...  10.5 us
    all_to_all x1, starting transfers between devices, per_device(): gathered = lax.all_to_all(packed, 'expert', 0, 0, tiled=True)  7.4 us
    all_to_all x1, waiting for transfers between devices, per_device(): received = lax.all_to_all(routed, 'expert', 0, 0, tiled=True)  6.29 us
    all_to_all x1, starting transfers between devices, per_device(): received = lax.all_to_all(routed, 'expert', 0, 0, tiled=True)  5.65 us
    ppermute x9, starting transfers between devices, flipped(): lax.ppermute(block, axis, [(i, i ^ bits) for i in range(lax.axis_size(axi...  4.64 us
  transfers between devices with their start and end apart: 11, of which 6 were waited for; matrix products, arithmetic and copies ran while one was open for 0% of the time, Pallas kernels for 0%

profile of v1, /device:TPU:0, one launch (start us, length us, event | category | flops | bytes accessed | tf_op | source)
XLA Modules:
  0.0 163.7 jit_solution(8699962558487874391)
XLA Ops:
  0.0 2.7 %pack_by_heads.1 = (bf16[8,400,256]{2,1,0:T(8,128)(2,1)}, f32[128,128]{1,0:T(8,128)}) custom-call(bf16[1,128,2048]{2,1,0:T(8,128)(2,1)} %refs_0_.2, bf16[1,128,2048]{2,1,0:T(8,128)(2,1)} %refs_1_.1, bf16[1,128,2048]{2,1,0:T(8,128)(2,1)} %refs_2_.1, s32[1,128]{1,0:T(1,128)} %refs_3_.1, s32[2,128]{1,0:T(2,128)} %bitcast.17, f32[2,128]{1,0:T(2,128)} %bitcast.18, ...), custom_call_target="tpu_custom_call" | custom-call | tf_op jit(solution)/shard_map/pack_by_heads/pallas_call | solution.py:214
  2.7 0.0 copy-start.3
  2.7 7.4 %all-to-all-start = ((bf16[8,400,256]{2,1,0:T(8,128)(2,1)}), bf16[8,400,256]{2,1,0:T(8,128)(2,1)S(1)}, u32[]{:S(2)}, u32[]{:S(2)}) async-start(bf16[8,400,256]{2,1,0:T(8,128)(2,1)} %get-tuple-element.10), calls=%async_computation | async-start | bytes 3276800 | tf_op jit(solution)/shard_map/all_to_all | solution.py:476
  10.2 1.6 collective-permute-start
  11.7 0.5 collective-permute-start.1
  12.2 24.2 %collective-permute-done.refs_2_ = bf16[1,512,1024]{2,1,0:T(8,128)(2,1)} collective-permute-done((bf16[1,512,1024]{2,1,0:T(8,128)(2,1)S(1)}, bf16[1,512,1024]{2,1,0:T(8,128)(2,1)}, u32[]{:S(2)}, u32[]{:S(2)}) %collective-permute-start) | collective-permute-done | bytes 1048608 | tf_op jit(solution)/shard_map/ppermute | solution.py:442
  36.4 21.0 %collective-permute-done.1.refs_6_ = bf16[1,512,1024]{2,1,0:T(8,128)(2,1)} collective-permute-done((bf16[1,512,1024]{2,1,0:T(8,128)(2,1)}, bf16[1,512,1024]{2,1,0:T(8,128)(2,1)}, u32[]{:S(2)}, u32[]{:S(2)}) %collective-permute-start.1) | collective-permute-done | bytes 1048608 | tf_op jit(solution)/shard_map/ppermute | solution.py:442
  57.4 0.0 all-to-all-done.all_ref.meta_ref
  57.4 10.5 %attend_and_route.1 = bf16[8,8,48,256]{3,2,1,0:T(8,128)(2,1)} custom-call(bf16[8,400,256]{2,1,0:T(8,128)(2,1)S(1)} %all-to-all-done.all_ref.meta_ref), custom_call_target="tpu_custom_call" | custom-call | tf_op jit(solution)/shard_map/attend_and_route/pallas_call | solution.py:287
  68.0 5.7 %all-to-all-start.1 = ((bf16[8,8,48,256]{3,2,1,0:T(8,128)(2,1)}), bf16[8,8,48,256]{3,2,1,0:T(8,128)(2,1)S(1)}, u32[]{:S(2)}, u32[]{:S(2)}) async-start(bf16[8,8,48,256]{3,2,1,0:T(8,128)(2,1)} %attend_and_route.1), calls=%async_computation.1 | async-start | bytes 3145728 | tf_op jit(solution)/shard_map/all_to_all | solution.py:482
  73.6 1.5 collective-permute-start.7
  75.1 0.0 collective-permute-start.2
  75.1 0.5 collective-permute-start.4
  75.6 0.0 collective-permute-start.6
  75.6 21.4 %collective-permute-done.7.refs_10_ = bf16[1,256,2048]{2,1,0:T(8,128)(2,1)} collective-permute-done((bf16[1,256,2048]{2,1,0:T(8,128)(2,1)}, bf16[1,256,2048]{2,1,0:T(8,128)(2,1)}, u32[]{:S(2)}, u32[]{:S(2)}) %collective-permute-start.7) | collective-permute-done | bytes 1048608 | tf_op jit(solution)/shard_map/ppermute | solution.py:442
  97.1 0.0 collective-permute-start.8
  97.1 0.5 collective-permute-start.3
  97.6 0.0 collective-permute-done.2.refs_1_
  97.6 1.0 copy-done.4
  98.5 0.0 collective-permute-start.5
  98.5 0.6 pad_add_fusion.place_ref
  99.1 0.0 collective-permute-done.4.refs_5_
  99.2 0.0 collective-permute-done.6.refs_9_
  99.2 0.9 collective-permute-done.8.refs_11_
  100.1 3.0 %collective-permute-done.3.refs_3_ = bf16[1,512,1024]{2,1,0:T(8,128)(2,1)} collective-permute-done((bf16[1,512,1024]{2,1,0:T(8,128)(2,1)}, bf16[1,512,1024]{2,1,0:T(8,128)(2,1)}, u32[]{:S(2)}, u32[]{:S(2)}) %collective-permute-start.3) | collective-permute-done | bytes 1048608 | tf_op jit(solution)/shard_map/ppermute | solution.py:442
  103.1 0.0 collective-permute-done.5.refs_7_
  103.1 6.3 %all-to-all-done.1 = bf16[8,8,48,256]{3,2,1,0:T(8,128)(2,1)S(1)} async-done(((bf16[8,8,48,256]{3,2,1,0:T(8,128)(2,1)}), bf16[8,8,48,256]{3,2,1,0:T(8,128)(2,1)S(1)}, u32[]{:S(2)}, u32[]{:S(2)}) %all-to-all-start.1) | async-done | bytes 1572896 | tf_op jit(solution)/shard_map/all_to_all | solution.py:482
  109.4 1.1 copy-done.2
  110.5 11.2 %expert_rows.1 = bf16[384,2048]{1,0:T(8,128)(2,1)} custom-call(s32[2]{0:T(128)} %pad_add_fusion.place_ref, bf16[8,384,256]{2,1,0:T(8,128)(2,1)} %bitcast.14, bf16[8,400,256]{2,1,0:T(8,128)(2,1)} %copy-done, f32[1,2048]{1,0:T(1,128)} %bitcast.16, bf16[1,512,1024]{2,1,0:T(8,128)(2,1)} %refs_0_.3, bf16[1,512,1024]{2,1,0:T(8,128)(2,1)} %copy-done.4, ...), custom_call_target="tpu_custom_call" | custom-call | tf_op jit(solution)/shard_map/expert_rows/pallas_call | solution.py:411
  121.7 0.0 copy-start.1
  121.7 40.7 %all_to_all.15 = bf16[8,48,2048]{2,1,0:T(8,128)(2,1)S(1)} all-to-all(bf16[8,48,2048]{2,1,0:T(8,128)(2,1)} %bitcast.15), channel_id=1, replica_groups=mesh['dp'=4,'expert'=8] {'expert'}, dimensions={0} | all-to-all | bytes 3145728 | tf_op jit(solution)/shard_map/all_to_all | solution.py:486
  162.4 1.3 combine_choices.1
  (8 shorter events, 0.0 us)
Async XLA Ops:
  2.7 7.4 %copy-start.3 = (bf16[1,512,1024]{2,1,0:T(8,128)(2,1)S(1)}, bf16[1,512,1024]{2,1,0:T(8,128)(2,1)}, u32[]{:S(2)}) copy-start(bf16[1,512,1024]{2,1,0:T(8,128)(2,1)} %refs_0_.3) | copy-start | bytes 3145732
  2.7 54.7 %all-to-all-start = ((bf16[8,400,256]{2,1,0:T(8,128)(2,1)}), bf16[8,400,256]{2,1,0:T(8,128)(2,1)S(1)}, u32[]{:S(2)}, u32[]{:S(2)}) async-start(bf16[8,400,256]{2,1,0:T(8,128)(2,1)} %get-tuple-element.10), calls=%async_computation | async-start | bytes 3276800 | tf_op jit(solution)/shard_map/all_to_all | solution.py:476
  10.2 26.3 %collective-permute-start = (bf16[1,512,1024]{2,1,0:T(8,128)(2,1)S(1)}, bf16[1,512,1024]{2,1,0:T(8,128)(2,1)}, u32[]{:S(2)}, u32[]{:S(2)}) collective-permute-start(bf16[1,512,1024]{2,1,0:T(8,128)(2,1)S(1)} %copy-done.3), channel_id=1, source_target_pairs={{0,16},{8,24},{16,0},{24,8},{1,17},{9,25},{17,1},{25,9},{2,18},{10... | collective-permute-start | bytes 3145736 | tf_op jit(solution)/shard_map/ppermute | solution.py:442
  11.7 45.7 %collective-permute-start.1 = (bf16[1,512,1024]{2,1,0:T(8,128)(2,1)}, bf16[1,512,1024]{2,1,0:T(8,128)(2,1)}, u32[]{:S(2)}, u32[]{:S(2)}) collective-permute-start(bf16[1,512,1024]{2,1,0:T(8,128)(2,1)} %refs_4_.1), channel_id=1, source_target_pairs={{0,16},{8,24},{16,0},{24,8},{1,17},{9,25},{17,1},{25,9},{2,18},{10... | collective-permute-start | bytes 3145736 | tf_op jit(solution)/shard_map/ppermute | solution.py:442
  57.4 10.5 %copy-start = (bf16[8,400,256]{2,1,0:T(8,128)(2,1)}, bf16[8,400,256]{2,1,0:T(8,128)(2,1)S(1)}, u32[]{:S(2)}) copy-start(bf16[8,400,256]{2,1,0:T(8,128)(2,1)S(1)} %all-to-all-done.all_ref.meta_ref) | copy-start | bytes 4915204
  68.0 41.4 %all-to-all-start.1 = ((bf16[8,8,48,256]{3,2,1,0:T(8,128)(2,1)}), bf16[8,8,48,256]{3,2,1,0:T(8,128)(2,1)S(1)}, u32[]{:S(2)}, u32[]{:S(2)}) async-start(bf16[8,8,48,256]{3,2,1,0:T(8,128)(2,1)} %attend_and_route.1), calls=%async_computation.1 | async-start | bytes 3145728 | tf_op jit(solution)/shard_map/all_to_all | solution.py:482
  73.6 23.4 %collective-permute-start.7 = (bf16[1,256,2048]{2,1,0:T(8,128)(2,1)}, bf16[1,256,2048]{2,1,0:T(8,128)(2,1)}, u32[]{:S(2)}, u32[]{:S(2)}) collective-permute-start(bf16[1,256,2048]{2,1,0:T(8,128)(2,1)} %refs_8_.1), channel_id=1, source_target_pairs={{0,16},{8,24},{16,0},{24,8},{1,17},{9,25},{17,1},{25,9},{2,18},{10... | collective-permute-start | bytes 3145736 | tf_op jit(solution)/shard_map/ppermute | solution.py:442
  75.1 22.4 %collective-permute-start.2 = (bf16[1,512,1024]{2,1,0:T(8,128)(2,1)S(1)}, bf16[1,512,1024]{2,1,0:T(8,128)(2,1)S(1)}, u32[]{:S(2)}, u32[]{:S(2)}) collective-permute-start(bf16[1,512,1024]{2,1,0:T(8,128)(2,1)S(1)} %copy-done.3), channel_id=1, source_target_pairs={{0,8},{8,0},{16,24},{24,16},{1,9},{9,1},{17,25},{25,17},{2,10},{10... | collective-permute-start | bytes 3145736 | tf_op jit(solution)/shard_map/ppermute | solution.py:442
  75.1 24.0 %collective-permute-start.4 = (bf16[1,512,1024]{2,1,0:T(8,128)(2,1)}, bf16[1,512,1024]{2,1,0:T(8,128)(2,1)}, u32[]{:S(2)}, u32[]{:S(2)}) collective-permute-start(bf16[1,512,1024]{2,1,0:T(8,128)(2,1)} %refs_4_.1), channel_id=1, source_target_pairs={{0,8},{8,0},{16,24},{24,16},{1,9},{9,1},{17,25},{25,17},{2,10},{10... | collective-permute-start | bytes 3145736 | tf_op jit(solution)/shard_map/ppermute | solution.py:442
  75.6 23.5 %collective-permute-start.6 = (bf16[1,256,2048]{2,1,0:T(8,128)(2,1)}, bf16[1,256,2048]{2,1,0:T(8,128)(2,1)}, u32[]{:S(2)}, u32[]{:S(2)}) collective-permute-start(bf16[1,256,2048]{2,1,0:T(8,128)(2,1)} %refs_8_.1), channel_id=1, source_target_pairs={{0,8},{8,0},{16,24},{24,16},{1,9},{9,1},{17,25},{25,17},{2,10},{10... | collective-permute-start | bytes 3145736 | tf_op jit(solution)/shard_map/ppermute | solution.py:442
  97.1 3.0 %collective-permute-start.8 = (bf16[1,256,2048]{2,1,0:T(8,128)(2,1)}, bf16[1,256,2048]{2,1,0:T(8,128)(2,1)}, u32[]{:S(2)}, u32[]{:S(2)}) collective-permute-start(bf16[1,256,2048]{2,1,0:T(8,128)(2,1)} %collective-permute-done.7.refs_10_), channel_id=1, source_target_pairs={{0,8},{8,0},{16,24},{24,16},{1,9},{9,1},{17,25},{25,17},{2,10},{10... | collective-permute-start | bytes 3145736 | tf_op jit(solution)/shard_map/ppermute | solution.py:442
  97.1 6.0 %collective-permute-start.3 = (bf16[1,512,1024]{2,1,0:T(8,128)(2,1)}, bf16[1,512,1024]{2,1,0:T(8,128)(2,1)}, u32[]{:S(2)}, u32[]{:S(2)}) collective-permute-start(bf16[1,512,1024]{2,1,0:T(8,128)(2,1)} %collective-permute-done.refs_2_), channel_id=1, source_target_pairs={{0,8},{8,0},{16,24},{24,16},{1,9},{9,1},{17,25},{25,17},{2,10},{10... | collective-permute-start | bytes 3145736 | tf_op jit(solution)/shard_map/ppermute | solution.py:442
  97.6 1.0 copy-start.4
  98.5 4.5 %collective-permute-start.5 = (bf16[1,512,1024]{2,1,0:T(8,128)(2,1)}, bf16[1,512,1024]{2,1,0:T(8,128)(2,1)S(1)}, u32[]{:S(2)}, u32[]{:S(2)}) collective-permute-start(bf16[1,512,1024]{2,1,0:T(8,128)(2,1)} %collective-permute-done.1.refs_6_), channel_id=1, source_target_pairs={{0,8},{8,0},{16,24},{24,16},{1,9},{9,1},{17,25},{25,17},{2,10},{10... | collective-permute-start | bytes 3145736 | tf_op jit(solution)/shard_map/ppermute | solution.py:442
  103.1 6.3 %copy-start.5 = (bf16[1,512,1024]{2,1,0:T(8,128)(2,1)}, bf16[1,512,1024]{2,1,0:T(8,128)(2,1)S(1)}, u32[]{:S(2)}) copy-start(bf16[1,512,1024]{2,1,0:T(8,128)(2,1)S(1)} %collective-permute-done.5.refs_7_) | copy-start | bytes 3145732
  109.4 1.1 copy-start.2
  121.7 40.7 %copy-start.1 = (f32[128,128]{1,0:T(8,128)S(1)}, f32[128,128]{1,0:T(8,128)}, u32[]{:S(2)}) copy-start(f32[128,128]{1,0:T(8,128)} %get-tuple-element.14.slots_ref) | copy-start | bytes 196612

commit v2 on v0

--- a/solution.py
+++ b/solution.py
@@ -1,13 +1,20 @@
+import functools
 import math
 
 import jax
 import jax.numpy as jnp
 from jax import lax
+from jax.experimental import pallas as pl
+from jax.experimental.pallas import tpu as pltpu
 from jax.sharding import PartitionSpec as P
 
 HEAD_DIM = 128
 TOP = 2
 WINDOW = 512
+META = 16
+LANES = 128
+F32 = jnp.float32
+BF16 = jnp.bfloat16
 
 
 def shifted_2(block, axis, distance):
@@ -47,7 +54,7 @@
     return blocks.reshape(rows_dev, width)
 
 
-def per_device(
+def per_device_general(
     queries,
     keys,
     values,
@@ -137,6 +144,487 @@
     return combined.astype(jnp.bfloat16)[None]
 
 
+def pack_kernel(owners, q_ref, k_ref, v_ref, *refs):
+    given, out_refs, slots_ref = refs[:4], refs[4 : 4 + owners], refs[4 + owners]
+    small, packed, sems, small_sems, store_sems = refs[5 + owners : 9 + owners], *refs[9 + owners :]
+    rows = q_ref.shape[1]
+    part = packed.shape[2]
+    me = lax.axis_index("expert")
+    order = list(range(owners // 2, owners)) + list(range(owners // 2))
+    fetches = [pltpu.make_async_copy(given[i], small[i], small_sems.at[i]) for i in range(4)]
+    for fetch in fetches:
+        fetch.start()
+    loads = {}
+    for turn in order:
+        lanes = pl.ds(pl.multiple_of((me ^ turn) * part, part), part)
+        for which, ref in enumerate((q_ref, k_ref, v_ref)):
+            loads[turn, which] = pltpu.make_async_copy(
+                ref.at[0, :, lanes], packed.at[turn, pl.ds(which * rows, rows)], sems.at[turn, which]
+            )
+            loads[turn, which].start()
+    for fetch in fetches:
+        fetch.wait()
+    docs_ref, index_ref, gates_ref, limits_ref = small
+    experts = limits_ref.shape[1]
+    most = most_of(rows, experts)
+    line = lax.broadcasted_iota(jnp.int32, (META, rows), 0)
+    given = jnp.zeros((META, rows), F32)
+    for k in range(TOP):
+        given = jnp.where(line == k, index_ref[k : k + 1].astype(F32), given)
+        given = jnp.where(line == TOP + k, gates_ref[k : k + 1], given)
+    given = jnp.concatenate([given, jnp.zeros((rows - META, rows), F32)], axis=0).T
+    index = [given[:, k : k + 1] for k in range(TOP)]
+    names = lax.broadcasted_iota(jnp.int32, (rows, experts), 1).astype(F32)
+    chosen = [jnp.where(index[k] == names, 1.0, 0.0) for k in range(TOP)]
+    below = lax.broadcasted_iota(jnp.int32, (rows, rows), 1) < lax.broadcasted_iota(jnp.int32, (rows, rows), 0)
+    earlier = jnp.dot(
+        jnp.where(below, 1.0, 0.0).astype(BF16), (chosen[0] + chosen[1]).astype(BF16), preferred_element_type=F32
+    )
+    limits = limits_ref[...].astype(F32)
+    columns = []
+    slots = []
+    weights = []
+    for k in range(TOP):
+        rank = jnp.sum(chosen[k] * earlier, axis=1, keepdims=True)
+        limit = jnp.sum(chosen[k] * limits, axis=1, keepdims=True)
+        slots.append(index[k] * most + rank)
+        columns += [index[k], rank]
+        weights.append(jnp.where(rank < limit, given[:, TOP + k : TOP + k + 1], 0.0))
+    for weight in weights:
+        first = weight.astype(BF16).astype(F32)
+        second = (weight - first).astype(BF16).astype(F32)
+        columns += [first, second, weight - first - second]
+    lane = lax.broadcasted_iota(jnp.int32, (rows, LANES), 1)
+    table = jnp.zeros((rows, LANES), F32)
+    for number, column in enumerate(columns):
+        table = jnp.where(lane == number + 1, column, table)
+    turned = table.T[:META]
+    turned = jnp.where(line == 0, docs_ref[...].astype(F32), turned).astype(BF16)
+    slots_ref[...] = jnp.where(lane == 0, slots[0], jnp.where(lane == 1, slots[1], -1.0))
+    stores = []
+    for turn in order:
+        packed[turn, TOP_ROWS * rows :, :rows] = turned
+        packed[turn, TOP_ROWS * rows :, rows:] = jnp.zeros((META, part - rows), BF16)
+        for which in range(TOP_ROWS):
+            loads[turn, which].wait()
+        stores.append(pltpu.make_async_copy(packed.at[turn], out_refs[turn], store_sems.at[turn]))
+        stores[-1].start()
+    for store in stores:
+        store.wait()
+
+
+TOP_ROWS = 3
+VMEM_BYTES = 65400 * 1024
+ANYWHERE = pl.BlockSpec(memory_space=pl.ANY)
+
+
+def most_of(rows, experts):
+    return max(2, 3 * rows * TOP // (2 * experts))
+
+
+def pack(queries, keys, values, doc_ids, expert_index, gates, capacity, owners):
+    rows, width = queries.shape[1:]
+    part = width // owners
+    deep = TOP_ROWS * rows + META
+    small = (doc_ids, expert_index[0].T, gates[0].T, capacity[None, :])
+    result = pl.pallas_call(
+        functools.partial(pack_kernel, owners),
+        out_shape=[jax.ShapeDtypeStruct((deep, part), BF16)] * owners + [jax.ShapeDtypeStruct((rows, LANES), F32)],
+        in_specs=[ANYWHERE] * 7,
+        out_specs=[ANYWHERE] * owners + [pl.BlockSpec(memory_space=pltpu.VMEM)],
+        scratch_shapes=[pltpu.VMEM(array.shape, array.dtype) for array in small]
+        + [
+            pltpu.VMEM((owners, deep, part), BF16),
+            pltpu.SemaphoreType.DMA((owners, TOP_ROWS)),
+            pltpu.SemaphoreType.DMA((4,)),
+            pltpu.SemaphoreType.DMA((owners,)),
+        ],
+        compiler_params=pltpu.CompilerParams(vmem_limit_bytes=VMEM_BYTES),
+        name="pack_by_heads",
+    )(queries, keys, values, *small)
+    return result[:owners], result[owners]
+
+
+def attend_kernel(most, count, *refs):
+    in_refs, out_refs = refs[:count], refs[count : 2 * count]
+    queries, keys, values, wide_values, docs, slots_of, routed, load_sems, store_sems = refs[2 * count :]
+    me = lax.axis_index("expert")
+    experts = count
+    part = queries.shape[2]
+    rows = keys.shape[1]
+    reach = keys.shape[0] - count
+    heads = part // HEAD_DIM
+    factor = math.log2(math.e) / math.sqrt(HEAD_DIM)
+    loads = []
+    for turn in range(count):
+        source = me ^ turn
+        loads += [
+            pltpu.make_async_copy(
+                in_refs[turn].at[pl.ds(2 * rows, rows + META)], values.at[reach + source], load_sems.at[turn, 0]
+            ),
+            pltpu.make_async_copy(in_refs[turn].at[pl.ds(rows, rows)], keys.at[reach + source], load_sems.at[turn, 1]),
+            pltpu.make_async_copy(in_refs[turn].at[pl.ds(0, rows)], queries.at[source], load_sems.at[turn, 2]),
+        ]
+    for load in loads[0::3] + loads[1::3] + loads[2::3]:
+        load.start()
+    for number in range(reach):
+        keys[number] = jnp.zeros((rows, part), BF16)
+        for head in range(heads):
+            wide_values[head, number] = jnp.zeros((rows, 2 * HEAD_DIM), BF16)
+        docs[number] = jnp.full((8, rows), -1.0, F32)
+    for load in loads[0::3]:
+        load.wait()
+
+    @pl.loop(reach, reach + count, unroll=True)
+    def _(number):
+        for head in range(heads):
+            wide_values[head, number, :, :HEAD_DIM] = values[number, :rows, head * HEAD_DIM : (head + 1) * HEAD_DIM]
+            wide_values[head, number, :, HEAD_DIM:] = jnp.ones((rows, HEAD_DIM), BF16)
+        meta = values[number, rows:, :rows].astype(F32)
+        docs[number] = jnp.broadcast_to(meta[0:1], (8, rows))
+        for k in range(TOP):
+            slots_of[number, k : k + 1] = meta[1 + 2 * k : 2 + 2 * k] * most + meta[2 + 2 * k : 3 + 2 * k]
+
+    for load in loads[1::3] + loads[2::3]:
+        load.wait()
+    lower = lax.broadcasted_iota(jnp.int32, (rows, rows), 1) <= lax.broadcasted_iota(jnp.int32, (rows, rows), 0)
+    slot_at = lax.broadcasted_iota(jnp.int32, (experts * most, rows), 0).astype(F32)
+    nothing = jnp.zeros((rows, rows), BF16)
+
+    def one_pair(pair):
+        at = pair * 2
+        allowed = []
+        for side in range(2):
+            square = jnp.broadcast_to(docs[at + side + reach, 0:1], (rows, rows))
+            query_docs = square.T
+            masks = []
+            for step in range(reach):
+                key_docs = docs[at + side + step, 0:1]
+                if step == 0:
+                    key_docs = jnp.where(lower, square, key_docs)
+                masks.append(query_docs == key_docs)
+            allowed.append(masks)
+        done = []
+        for head in range(heads):
+            lanes = slice(head * HEAD_DIM, (head + 1) * HEAD_DIM)
+            query = queries[pl.ds(at, 2), :, lanes].reshape(2 * rows, HEAD_DIM)
+            key = keys[pl.ds(at, reach + 2), :, lanes].reshape((reach + 2) * rows, HEAD_DIM)
+            scores = lax.dot_general(query, key, (((1,), (1,)), ((), ())), preferred_element_type=F32)
+            lines = []
+            for side in range(2):
+                here = scores[side * rows : (side + 1) * rows]
+                cut = [here[:, (side + step) * rows : (side + step + 1) * rows] for step in range(reach + 1)]
+                cut = [jnp.where(lower, cut[reach], cut[0])] + cut[1:reach]
+                cut = [jnp.where(mask, score, -1e30) for mask, score in zip(allowed[side], cut)]
+                highest = jnp.max(functools.reduce(jnp.maximum, cut), axis=1, keepdims=True)
+                expo = [jnp.exp2((score - highest) * factor) for score in cut]
+                last = jnp.where(lower, expo[0], 0.0).astype(BF16)
+                expo = [jnp.where(lower, 0.0, expo[0]).astype(BF16)] + [e.astype(BF16) for e in expo[1:]] + [last]
+                lines.append(jnp.concatenate([nothing] * side + expo + [nothing] * (1 - side), axis=1))
+            weight = jnp.concatenate(lines, axis=0)
+            value = wide_values[head, pl.ds(at, reach + 2)].reshape((reach + 2) * rows, 2 * HEAD_DIM)
+            result = jnp.dot(weight, value, preferred_element_type=F32)
+            done.append((result[:, :HEAD_DIM] / result[:, HEAD_DIM:]).astype(BF16))
+        attended = jnp.concatenate(done, axis=1)
+        for side in range(2):
+            slots = slots_of[at + side + reach]
+            picks = (slot_at == slots[0:1]) | (slot_at == slots[1:2])
+            picks = jnp.where(picks, 1.0, 0.0).astype(BF16)
+            sent = jnp.dot(picks, attended[side * rows : (side + 1) * rows], preferred_element_type=F32).astype(BF16)
+            for expert in range(experts):
+                routed[expert, at + side] = sent[expert * most : (expert + 1) * most]
+
+    half = count // 2
+    stores = []
+    for group in range(2):
+        pl.loop(group * half // 2, (group + 1) * half // 2, unroll=True)(one_pair)
+        for turn in range(count):
+            some = pl.ds(group * half, half)
+            stores.append(
+                pltpu.make_async_copy(routed.at[me ^ turn, some], out_refs[turn].at[some], store_sems.at[turn, group])
+            )
+            stores[-1].start()
+    for store in stores:
+        store.wait()
+
+
+def attend(gathered, most):
+    count = len(gathered)
+    deepest, part = gathered[0].shape
+    rows = (deepest - META) // TOP_ROWS
+    reach = WINDOW // rows
+    total = reach + count
+    return pl.pallas_call(
+        functools.partial(attend_kernel, most, count),
+        out_shape=[jax.ShapeDtypeStruct((count, most, part), BF16)] * count,
+        in_specs=[ANYWHERE] * count,
+        out_specs=[ANYWHERE] * count,
+        scratch_shapes=[
+            pltpu.VMEM((count, rows, part), BF16),
+            pltpu.VMEM((total, rows, part), BF16),
+            pltpu.VMEM((total, rows + META, part), BF16),
+            pltpu.VMEM((part // HEAD_DIM, total, rows, 2 * HEAD_DIM), BF16),
+            pltpu.VMEM((total, 8, rows), F32),
+            pltpu.VMEM((total, 8, rows), F32),
+            pltpu.VMEM((count, count, most, part), BF16),
+            pltpu.SemaphoreType.DMA((count, 3)),
+            pltpu.SemaphoreType.DMA((count, 2)),
+        ],
+        compiler_params=pltpu.CompilerParams(vmem_limit_bytes=VMEM_BYTES),
+        name="attend_and_route",
+    )(*gathered)
+
+
+def expert_kernel(pieces, blocks, gain_ref, *refs):
+    row_refs, meta_refs, refs = refs[:blocks], refs[blocks : 2 * blocks], refs[2 * blocks :]
+    gate_refs, up_refs, down_refs = refs[:pieces], refs[pieces : 2 * pieces], refs[2 * pieces : 3 * pieces]
+    refs = refs[3 * pieces :]
+    out_refs, refs = refs[:blocks], refs[blocks:]
+    held_rows, meta_all, gate_all, up_all, down_all, normed, hidden, answers = refs[:8]
+    sems, row_sems, store_sems = refs[8:]
+    parts, count, part = held_rows.shape
+    most = answers.shape[1]
+    wide = gate_all.shape[3]
+    width = parts * part
+    mine, expert = lax.axis_index("dp"), lax.axis_index("expert")
+    loads = []
+    for turn in range(blocks):
+        source = expert ^ turn
+        loads += [
+            pltpu.make_async_copy(row_refs[turn], held_rows.at[source], row_sems.at[turn, 0]),
+            pltpu.make_async_copy(
+                meta_refs[turn].at[pl.ds(meta_refs[turn].shape[0] - META, META)], meta_all.at[source], row_sems.at[turn, 1]
+            ),
+        ]
+
+    def tile_copies(step):
+        tile = pl.ds(pl.multiple_of((mine ^ step) * wide, wide), wide)
+        found = []
+        for which, (held, weights) in enumerate(((gate_all, gate_refs), (up_all, up_refs))):
+            for number in range(pieces):
+                source, target = weights[number].at[0, :, tile], held.at[step, mine ^ number]
+                found.append(pltpu.make_async_copy(source, target, sems.at[which, step, number]))
+        return found
+
+    def down_copy(step):
+        return pltpu.make_async_copy(down_refs[step].at[0], down_all.at[step], sems.at[2, 0, step])
+
+    for load in loads:
+        load.start()
+    for load in loads:
+        load.wait()
+    for step in range(pieces):
+        for copy in tile_copies(step):
+            copy.start()
+    for step in range(pieces):
+        down_copy(step).start()
+
+    squares = jnp.zeros((count, part), F32)
+    for number in range(parts):
+        held = held_rows[number].astype(F32)
+        squares = squares + held * held
+    inverse = lax.rsqrt(jnp.sum(squares, axis=1, keepdims=True) / width + 1e-05)
+    for number in range(parts):
+        lanes = slice(number * part, (number + 1) * part)
+        normed[:, lanes] = (held_rows[number].astype(F32) * inverse * gain_ref[:, lanes]).astype(BF16)
+
+    @pl.loop(0, pieces)
+    def _(step):
+        for copy in tile_copies(step):
+            copy.wait()
+        held = normed[...]
+        gate = jnp.dot(held, gate_all[step].reshape(width, wide), preferred_element_type=F32)
+        up = jnp.dot(held, up_all[step].reshape(width, wide), preferred_element_type=F32)
+        hidden[step] = (gate / (1.0 + jnp.exp(-gate)) * up).astype(BF16)
+
+    for piece in range(pieces):
+        down_copy(piece).wait()
+
+    rows = LANES
+    slot_of = lax.broadcasted_iota(jnp.int32, (most, rows), 0).astype(F32) + (expert * most).astype(F32)
+    weights, firsts = [], []
+    for number in range(blocks):
+        meta = meta_all[number, :, :rows].astype(F32)
+        total = jnp.zeros((most, rows), F32)
+        for k in range(TOP):
+            slot = meta[1 + 2 * k : 2 + 2 * k] * most + meta[2 + 2 * k : 3 + 2 * k]
+            at = 1 + 2 * TOP + 3 * k
+            weight = meta[at : at + 1] + meta[at + 1 : at + 2] + meta[at + 2 : at + 3]
+            total = total + jnp.where(slot_of == slot, weight, 0.0)
+            if k == 0:
+                firsts.append(jnp.sum(jnp.where(slot_of == slot, 1.0, 0.0), axis=1, keepdims=True))
+        weights.append(jnp.sum(total, axis=1, keepdims=True))
+    weight = jnp.concatenate(weights, axis=0)
+    first = jnp.concatenate(firsts, axis=0)
+
+    stores = []
+    for number in range(parts):
+        lanes = slice(number * part, (number + 1) * part)
+        result = jnp.zeros((count, part), F32)
+        for piece in range(pieces):
+            result = result + jnp.dot(hidden[piece], down_all[piece, :, lanes], preferred_element_type=F32)
+        result = result.astype(BF16).astype(F32) * weight
+        result = (held_rows[number].astype(F32) * first + result).astype(BF16)
+        for source in range(blocks):
+            answers[source, :, lanes] = result[source * most : (source + 1) * most]
+        if number % 2 == 1:
+            for turn in range(blocks):
+                some = pl.ds((number - 1) * part, 2 * part)
+                stores.append(
+                    pltpu.make_async_copy(
+                        answers.at[expert ^ turn, :, some], out_refs[turn].at[:, some], store_sems.at[turn, number // 2]
+                    )
+                )
+                stores[-1].start()
+    for store in stores:
+        store.wait()
+
+
+def run_expert(rows, gathered, gain, gates, ups, downs, most):
+    blocks = len(rows)
+    count, part = rows[0].shape
+    width = blocks * part
+    pieces = len(downs)
+    wide = downs[1].shape[1]
+    deep = width // pieces
+    return pl.pallas_call(
+        functools.partial(expert_kernel, pieces, blocks),
+        out_shape=[jax.ShapeDtypeStruct((most, width), BF16)] * blocks,
+        in_specs=[pl.BlockSpec(memory_space=pltpu.VMEM)]
+        + [ANYWHERE] * (2 * blocks + 3 * pieces),
+        out_specs=[ANYWHERE] * blocks,
+        scratch_shapes=[
+            pltpu.VMEM((blocks, count, part), BF16),
+            pltpu.VMEM((blocks, META, part), BF16),
+            pltpu.VMEM((pieces, pieces, deep, wide), BF16),
+            pltpu.VMEM((pieces, pieces, deep, wide), BF16),
+            pltpu.VMEM((pieces, wide, width), BF16),
+            pltpu.VMEM((count, width), BF16),
+            pltpu.VMEM((pieces, count, wide), BF16),
+            pltpu.VMEM((blocks, most, width), BF16),
+            pltpu.SemaphoreType.DMA((3, pieces, pieces)),
+            pltpu.SemaphoreType.DMA((blocks, 2)),
+            pltpu.SemaphoreType.DMA((blocks, blocks // 2)),
+        ],
+        compiler_params=pltpu.CompilerParams(vmem_limit_bytes=VMEM_BYTES),
+        name="expert_rows",
+    )(gain[None, :], *rows, *gathered, *gates, *ups, *downs)
+
+
+def combine_kernel(blocks, slots_ref, own_ref, *refs):
+    row_refs, out_ref, own, slots, sems = refs[: blocks - 1], *refs[blocks - 1 :]
+    loads = [
+        pltpu.make_async_copy(slots_ref, slots, sems.at[0]),
+        pltpu.make_async_copy(own_ref, own, sems.at[1]),
+    ]
+    for load in loads:
+        load.start()
+    most = own.shape[0]
+    rows = slots.shape[0]
+    column = lax.broadcasted_iota(jnp.int32, (rows, blocks * most), 1)
+    slot_of = (((column // most) ^ lax.axis_index("expert")) * most + column % most).astype(F32)
+    loads[0].wait()
+    picks = (slot_of == slots[:, 0:1]) | (slot_of == slots[:, 1:2])
+    picks = jnp.where(picks, 1.0, 0.0).astype(BF16)
+    loads[1].wait()
+    held = jnp.concatenate([own[...]] + [ref[...] for ref in row_refs], axis=0)
+    out_ref[0] = jnp.dot(picks, held, preferred_element_type=F32).astype(BF16)
+
+
+def combine(returned, slots):
+    blocks = len(returned)
+    most, width = returned[0].shape
+    vmem = pl.BlockSpec(memory_space=pltpu.VMEM)
+    return pl.pallas_call(
+        functools.partial(combine_kernel, blocks),
+        out_shape=jax.ShapeDtypeStruct((1, slots.shape[0], width), BF16),
+        in_specs=[pl.BlockSpec(memory_space=pltpu.HBM)] * 2 + [vmem] * (blocks - 1),
+        out_specs=vmem,
+        scratch_shapes=[
+            pltpu.VMEM(returned[0].shape, BF16),
+            pltpu.VMEM(slots.shape, F32),
+            pltpu.SemaphoreType.DMA((2,)),
+        ],
+        compiler_params=pltpu.CompilerParams(vmem_limit_bytes=24 * 1024 * 1024),
+        name="combine_choices",
+    )(slots, *returned)
+
+
+def flipped(block, axis, bits):
+    return lax.ppermute(block, axis, [(i, i ^ bits) for i in range(lax.axis_size(axis))])
+
+
+def exchange(blocks):
+    count = len(blocks)
+    moved = {turn: flipped(blocks[turn], "expert", turn) for turn in range(count - 1, 0, -1)}
+    return [blocks[0]] + [moved[turn] for turn in range(1, count)]
+
+
+def per_device(
+    queries,
+    keys,
+    values,
+    doc_ids,
+    expert_index,
+    gates,
+    capacity,
+    norm_gain,
+    gate_weight,
+    up_weight,
+    down_weight,
+):
+    rows, width = queries.shape[1:]
+    experts = lax.axis_size("expert")
+    most = most_of(rows, experts)
+    over = lax.axis_size("dp")
+    weights = [gate_weight, up_weight, down_weight]
+    gate, up, down = ({0: block} for block in weights)
+    for number in range(2, over, 2):
+        gate[number] = flipped(gate_weight, "dp", number)
+    packed, slots = pack(queries, keys, values, doc_ids, expert_index, gates, capacity, experts)
+    gathered = exchange(packed)
+    gathered, gate, up, down = lax.optimization_barrier((gathered, gate, up, down))
+    for pieces in (gate, up, down):
+        for number in list(pieces):
+            pieces[number + 1] = flipped(pieces[number], "dp", 1)
+    for number in range(2, over, 2):
+        up[number] = flipped(up_weight, "dp", number)
+    routed = list(attend(gathered, most))
+    routed, gate, up, down = lax.optimization_barrier((routed, gate, up, down))
+    for number in range(2, over, 2):
+        down[number] = flipped(down[0], "dp", number)
+    received = exchange(routed)
+    received, up, down = lax.optimization_barrier((received, up, down))
+    for pieces in (up, down):
+        for number in range(2, over, 2):
+            pieces[number + 1] = flipped(pieces[number], "dp", 1)
+    gate, up, down = ([pieces[number] for number in range(over)] for pieces in (gate, up, down))
+    received = [block.reshape(experts * most, width // experts) for block in received]
+    answered = run_expert(received, gathered, norm_gain, gate, up, down, most)
+    return combine(exchange(answered), slots)
+
+
+def by_heads(mesh, queries, gate_weight):
+    over, experts = mesh.shape["dp"], mesh.shape["expert"]
+    rows, width = queries.shape[1] // experts, queries.shape[2]
+    hidden = gate_weight.shape[2]
+    return (
+        width % (experts * HEAD_DIM) == 0
+        and rows == LANES
+        and WINDOW % rows == 0
+        and experts % 4 == 0
+        and experts & (experts - 1) == 0
+        and width // experts > rows
+        and (width // over) % (width // experts) == 0
+        and hidden % (over * LANES) == 0
+        and most_of(rows, experts) % 16 == 0
+        and over > 2
+        and over & (over - 1) == 0
+        and queries.shape[0] == over
+        and gate_weight.shape[0] == experts
+    )
+
+
 def solution(mesh):
     placed = (
         P("dp", "expert", None),
@@ -151,6 +639,11 @@
         P("expert", "dp", None),
         P("expert", "dp", None),
     )
-    return jax.shard_map(
-        per_device, mesh=mesh, in_specs=placed, out_specs=P("dp", "expert", None), check_vma=False
-    )
+
+    def layer(*arrays):
+        step = per_device if by_heads(mesh, arrays[0], arrays[8]) else per_device_general
+        return jax.shard_map(
+            step, mesh=mesh, in_specs=placed, out_specs=P("dp", "expert", None), check_vma=False
+        )(*arrays)
+
+    return layer

time: 247 us -> 155 us (0.63)
  the two profiles are of different devices: /device:TPU:0 before, /device:TPU:8 now
where the time goes in v2:
time: 155 us
  waiting for transfers between devices  95.1 us (61%)
  starting transfers between devices  33.2 us (21%)
  Pallas kernels  24.1 us (16%)
  local copies, waits for them, and re-layouts  1.88 us (1%)
    ppermute x30, waiting for transfers between devices, flipped(): lax.ppermute(block, axis, [(i, i ^ bits) for i in range(lax.axis_size(axi...  95.1 us
    ppermute x30, starting transfers between devices, flipped(): lax.ppermute(block, axis, [(i, i ^ bits) for i in range(lax.axis_size(axi...  33.2 us
    pallas_call x1, Pallas kernels, run_expert(): pl.pallas_call(functools.partial(expert_kernel, pieces, blocks), out_shap...  11.4 us
    pallas_call x1, Pallas kernels, attend(): pl.pallas_call(functools.partial(attend_kernel, most, count), out_shape=[...  7.01 us
    pallas_call x1, Pallas kernels, pack(): pl.pallas_call(functools.partial(pack_kernel, owners), out_shape=[jax.Sha...  3.99 us
  transfers between devices with their start and end apart: 30, of which 22 were waited for; matrix products, arithmetic and copies ran while one was open for 0% of the time, Pallas kernels for 7%

profile of v2, /device:TPU:8, one launch (start us, length us, event | category | flops | bytes accessed | tf_op | source)
XLA Modules:
  0.0 154.5 jit_solution(18383144890097445463)
XLA Ops:
  0.0 1.5 collective-permute-start.7
  1.5 4.0 %pack_by_heads.1 = (bf16[400,256]{1,0:T(8,128)(2,1)}, bf16[400,256]{1,0:T(8,128)(2,1)}, bf16[400,256]{1,0:T(8,128)(2,1)}, bf16[400,256]{1,0:T(8,128)(2,1)}, bf16...) custom-call(bf16[1,128,2048]{2,1,0:T(8,128)(2,1)} %q_ref.1, ...), custom_call_target="tpu_custom_call" | custom-call | tf_op jit(solution)/shard_map/pack_by_heads/pallas_call | solution.py:230
  5.5 1.6 %collective-permute-start = (bf16[400,256]{1,0:T(8,128)(2,1)}, bf16[400,256]{1,0:T(8,128)(2,1)}, u32[]{:S(2)}, u32[]{:S(2)}) collective-permute-start(bf16[400,256]{1,0:T(8,128)(2,1)} %get-tuple-element.75), channel_id=1, source_target_pairs={{0,1},{1,0},{2,3},{3,2},{4,5},{5,4},{6,7},{7,6},{8,9},{9,8},{10,11... | collective-permute-start | bytes 614408 | tf_op jit(solution)/shard_map/ppermute | solution.py:554
  7.5 1.5 %collective-permute-start.2 = (bf16[400,256]{1,0:T(8,128)(2,1)}, bf16[400,256]{1,0:T(8,128)(2,1)}, u32[]{:S(2)}, u32[]{:S(2)}) collective-permute-start(bf16[400,256]{1,0:T(8,128)(2,1)} %get-tuple-element.77), channel_id=1, source_target_pairs={{0,3},{1,2},{2,1},{3,0},{4,7},{5,6},{6,5},{7,4},{8,11},{9,10},{10,... | collective-permute-start | bytes 614408 | tf_op jit(solution)/shard_map/ppermute | solution.py:554
  9.1 2.6 %collective-permute-start.3 = (bf16[400,256]{1,0:T(8,128)(2,1)}, bf16[400,256]{1,0:T(8,128)(2,1)}, u32[]{:S(2)}, u32[]{:S(2)}) collective-permute-start(bf16[400,256]{1,0:T(8,128)(2,1)} %get-tuple-element.78), channel_id=1, source_target_pairs={{0,4},{1,5},{2,6},{3,7},{4,0},{5,1},{6,2},{7,3},{8,12},{9,13},{10,... | collective-permute-start | bytes 614408 | tf_op jit(solution)/shard_map/ppermute | solution.py:554
  13.0 2.9 %collective-permute-start.4 = (bf16[400,256]{1,0:T(8,128)(2,1)}, bf16[400,256]{1,0:T(8,128)(2,1)}, u32[]{:S(2)}, u32[]{:S(2)}) collective-permute-start(bf16[400,256]{1,0:T(8,128)(2,1)} %get-tuple-element.79), channel_id=1, source_target_pairs={{0,5},{1,4},{2,7},{3,6},{4,1},{5,0},{6,3},{7,2},{8,13},{9,12},{10,... | collective-permute-start | bytes 614408 | tf_op jit(solution)/shard_map/ppermute | solution.py:554
  16.0 5.0 %collective-permute-done.1.refs_2_.refs_10_ = bf16[400,256]{1,0:T(8,128)(2,1)} collective-permute-done((bf16[400,256]{1,0:T(8,128)(2,1)}, bf16[400,256]{1,0:T(8,128)(2,1)}, u32[]{:S(2)}, u32[]{:S(2)}) %collective-permute-start.1) | collective-permute-done | bytes 204832 | tf_op jit(solution)/shard_map/ppermute | solution.py:554
  25.8 12.5 %collective-permute-done.4.refs_5_.refs_13_ = bf16[400,256]{1,0:T(8,128)(2,1)} collective-permute-done((bf16[400,256]{1,0:T(8,128)(2,1)}, bf16[400,256]{1,0:T(8,128)(2,1)}, u32[]{:S(2)}, u32[]{:S(2)}) %collective-permute-start.4) | collective-permute-done | bytes 204832 | tf_op jit(solution)/shard_map/ppermute | solution.py:554
  38.3 5.2 %collective-permute-done.5.refs_6_.refs_14_ = bf16[400,256]{1,0:T(8,128)(2,1)} collective-permute-done((bf16[400,256]{1,0:T(8,128)(2,1)}, bf16[400,256]{1,0:T(8,128)(2,1)}, u32[]{:S(2)}, u32[]{:S(2)}) %collective-permute-start.5) | collective-permute-done | bytes 204832 | tf_op jit(solution)/shard_map/ppermute | solution.py:554
  43.5 3.2 %collective-permute-done.6.refs_7_.refs_15_ = bf16[400,256]{1,0:T(8,128)(2,1)} collective-permute-done((bf16[400,256]{1,0:T(8,128)(2,1)}, bf16[400,256]{1,0:T(8,128)(2,1)}, u32[]{:S(2)}, u32[]{:S(2)}) %collective-permute-start.6) | collective-permute-done | bytes 204832 | tf_op jit(solution)/shard_map/ppermute | solution.py:554
  47.7 7.0 %attend_and_route.1 = (bf16[8,48,256]{2,1,0:T(8,128)(2,1)}, bf16[8,48,256]{2,1,0:T(8,128)(2,1)}, bf16[8,48,256]{2,1,0:T(8,128)(2,1)}, bf16[8,48,256]{2,1,0:T(8,1...) custom-call(bf16[400,256]{1,0:T(8,128)(2,1)} %get-tuple-element.82.r, ...), custom_call_target="tpu_custom_call" | custom-call | tf_op jit(solution)/shard_map/attend_and_route/pallas_call | solution.py:357
  56.1 2.7 %collective-permute-start.15 = (bf16[8,48,256]{2,1,0:T(8,128)(2,1)}, bf16[8,48,256]{2,1,0:T(8,128)(2,1)S(1)}, u32[]{:S(2)}, u32[]{:S(2)}) collective-permute-start(bf16[8,48,256]{2,1,0:T(8,128)(2,1)} %get-tuple-element.105), channel_id=1, source_target_pairs={{0,3},{1,2},{2,1},{3,0},{4,7},{5,6},{6,5},{7,4},{8,11},{9,10},{10,... | collective-permute-start | bytes 589832 | tf_op jit(solution)/shard_map/ppermute | solution.py:554
  58.8 2.1 %collective-permute-start.16 = (bf16[8,48,256]{2,1,0:T(8,128)(2,1)}, bf16[8,48,256]{2,1,0:T(8,128)(2,1)S(1)}, u32[]{:S(2)}, u32[]{:S(2)}) collective-permute-start(bf16[8,48,256]{2,1,0:T(8,128)(2,1)} %get-tuple-element.106), channel_id=1, source_target_pairs={{0,4},{1,5},{2,6},{3,7},{4,0},{5,1},{6,2},{7,3},{8,12},{9,13},{10,... | collective-permute-start | bytes 589832 | tf_op jit(solution)/shard_map/ppermute | solution.py:554
  61.0 1.5 collective-permute-done.13
  62.5 5.5 %collective-permute-done.14 = bf16[8,48,256]{2,1,0:T(8,128)(2,1)S(1)} collective-permute-done((bf16[8,48,256]{2,1,0:T(8,128)(2,1)}, bf16[8,48,256]{2,1,0:T(8,128)(2,1)S(1)}, u32[]{:S(2)}, u32[]{:S(2)}) %collective-permute-start.14) | collective-permute-done | bytes 196640 | tf_op jit(solution)/shard_map/ppermute | solution.py:554
  69.5 2.5 %collective-permute-done.15 = bf16[8,48,256]{2,1,0:T(8,128)(2,1)S(1)} collective-permute-done((bf16[8,48,256]{2,1,0:T(8,128)(2,1)}, bf16[8,48,256]{2,1,0:T(8,128)(2,1)S(1)}, u32[]{:S(2)}, u32[]{:S(2)}) %collective-permute-start.15) | collective-permute-done | bytes 196640 | tf_op jit(solution)/shard_map/ppermute | solution.py:554
  71.9 2.2 %collective-permute-start.19 = (bf16[8,48,256]{2,1,0:T(8,128)(2,1)}, bf16[8,48,256]{2,1,0:T(8,128)(2,1)S(1)}, u32[]{:S(2)}, u32[]{:S(2)}) collective-permute-start(bf16[8,48,256]{2,1,0:T(8,128)(2,1)} %get-tuple-element.109), channel_id=1, source_target_pairs={{0,7},{1,6},{2,5},{3,4},{4,3},{5,2},{6,1},{7,0},{8,15},{9,14},{10,... | collective-permute-start | bytes 589832 | tf_op jit(solution)/shard_map/ppermute | solution.py:554
  74.2 9.2 %collective-permute-done.16 = bf16[8,48,256]{2,1,0:T(8,128)(2,1)S(1)} collective-permute-done((bf16[8,48,256]{2,1,0:T(8,128)(2,1)}, bf16[8,48,256]{2,1,0:T(8,128)(2,1)S(1)}, u32[]{:S(2)}, u32[]{:S(2)}) %collective-permute-start.16) | collective-permute-done | bytes 196640 | tf_op jit(solution)/shard_map/ppermute | solution.py:554
  83.4 4.4 %collective-permute-done.17 = bf16[8,48,256]{2,1,0:T(8,128)(2,1)S(1)} collective-permute-done((bf16[8,48,256]{2,1,0:T(8,128)(2,1)}, bf16[8,48,256]{2,1,0:T(8,128)(2,1)S(1)}, u32[]{:S(2)}, u32[]{:S(2)}) %collective-permute-start.17) | collective-permute-done | bytes 196640 | tf_op jit(solution)/shard_map/ppermute | solution.py:554
  87.7 4.6 %collective-permute-done.18 = bf16[8,48,256]{2,1,0:T(8,128)(2,1)S(1)} collective-permute-done((bf16[8,48,256]{2,1,0:T(8,128)(2,1)}, bf16[8,48,256]{2,1,0:T(8,128)(2,1)S(1)}, u32[]{:S(2)}, u32[]{:S(2)}) %collective-permute-start.18) | collective-permute-done | bytes 196640 | tf_op jit(solution)/shard_map/ppermute | solution.py:554
  92.3 2.9 %collective-permute-done.19 = bf16[8,48,256]{2,1,0:T(8,128)(2,1)S(1)} collective-permute-done((bf16[8,48,256]{2,1,0:T(8,128)(2,1)}, bf16[8,48,256]{2,1,0:T(8,128)(2,1)S(1)}, u32[]{:S(2)}, u32[]{:S(2)}) %collective-permute-start.19) | collective-permute-done | bytes 196640 | tf_op jit(solution)/shard_map/ppermute | solution.py:554
  95.8 3.1 %collective-permute-done.21.refs_23_ = bf16[1,512,1024]{2,1,0:T(8,128)(2,1)S(1)} collective-permute-done((bf16[1,512,1024]{2,1,0:T(8,128)(2,1)}, bf16[1,512,1024]{2,1,0:T(8,128)(2,1)S(1)}, u32[]{:S(2)}, u32[]{:S(2)}) %collective-permute-start.21) | collective-permute-done | bytes 1048608 | tf_op jit(solution)/shard_map/ppermute | solution.py:554
  100.4 11.4 %expert_rows.1 = (bf16[48,2048]{1,0:T(8,128)(2,1)}, bf16[48,2048]{1,0:T(8,128)(2,1)}, bf16[48,2048]{1,0:T(8,128)(2,1)}, bf16[48,2048]{1,0:T(8,128)(2,1)}, bf16[4...) custom-call(f32[1,2048]{1,0:T(1,128)} %bitcast.24, ...), custom_call_target="tpu_custom_call" | custom-call | tf_op jit(solution)/shard_map/expert_rows/pallas_call | solution.py:490
  111.8 1.6 %collective-permute-start.23 = (bf16[48,2048]{1,0:T(8,128)(2,1)}, bf16[48,2048]{1,0:T(8,128)(2,1)S(1)}, u32[]{:S(2)}, u32[]{:S(2)}) collective-permute-start(bf16[48,2048]{1,0:T(8,128)(2,1)} %get-tuple-element.134), channel_id=1, source_target_pairs={{0,1},{1,0},{2,3},{3,2},{4,5},{5,4},{6,7},{7,6},{8,9},{9,8},{10,11... | collective-permute-start | bytes 589832 | tf_op jit(solution)/shard_map/ppermute | solution.py:554
  113.4 2.0 %collective-permute-start.25 = (bf16[48,2048]{1,0:T(8,128)(2,1)}, bf16[48,2048]{1,0:T(8,128)(2,1)S(1)}, u32[]{:S(2)}, u32[]{:S(2)}) collective-permute-start(bf16[48,2048]{1,0:T(8,128)(2,1)} %get-tuple-element.136), channel_id=1, source_target_pairs={{0,3},{1,2},{2,1},{3,0},{4,7},{5,6},{6,5},{7,4},{8,11},{9,10},{10,... | collective-permute-start | bytes 589832 | tf_op jit(solution)/shard_map/ppermute | solution.py:554
  116.3 2.9 %collective-permute-start.27 = (bf16[48,2048]{1,0:T(8,128)(2,1)}, bf16[48,2048]{1,0:T(8,128)(2,1)S(1)}, u32[]{:S(2)}, u32[]{:S(2)}) collective-permute-start(bf16[48,2048]{1,0:T(8,128)(2,1)} %get-tuple-element.138), channel_id=1, source_target_pairs={{0,5},{1,4},{2,7},{3,6},{4,1},{5,0},{6,3},{7,2},{8,13},{9,12},{10,... | collective-permute-start | bytes 589832 | tf_op jit(solution)/shard_map/ppermute | solution.py:554
  120.7 6.1 %collective-permute-done.24.refs_1_ = bf16[48,2048]{1,0:T(8,128)(2,1)S(1)} collective-permute-done((bf16[48,2048]{1,0:T(8,128)(2,1)}, bf16[48,2048]{1,0:T(8,128)(2,1)S(1)}, u32[]{:S(2)}, u32[]{:S(2)}) %collective-permute-start.24) | collective-permute-done | bytes 196640 | tf_op jit(solution)/shard_map/ppermute | solution.py:554
  126.8 3.4 %collective-permute-done.25.refs_2_ = bf16[48,2048]{1,0:T(8,128)(2,1)S(1)} collective-permute-done((bf16[48,2048]{1,0:T(8,128)(2,1)}, bf16[48,2048]{1,0:T(8,128)(2,1)S(1)}, u32[]{:S(2)}, u32[]{:S(2)}) %collective-permute-start.25) | collective-permute-done | bytes 196640 | tf_op jit(solution)/shard_map/ppermute | solution.py:554
  130.8 12.2 %collective-permute-done.27.refs_4_ = bf16[48,2048]{1,0:T(8,128)(2,1)S(1)} collective-permute-done((bf16[48,2048]{1,0:T(8,128)(2,1)}, bf16[48,2048]{1,0:T(8,128)(2,1)S(1)}, u32[]{:S(2)}, u32[]{:S(2)}) %collective-permute-start.27) | collective-permute-done | bytes 196640 | tf_op jit(solution)/shard_map/ppermute | solution.py:554
  143.0 4.7 %collective-permute-done.28.refs_5_ = bf16[48,2048]{1,0:T(8,128)(2,1)S(1)} collective-permute-done((bf16[48,2048]{1,0:T(8,128)(2,1)}, bf16[48,2048]{1,0:T(8,128)(2,1)S(1)}, u32[]{:S(2)}, u32[]{:S(2)}) %collective-permute-start.28) | collective-permute-done | bytes 196640 | tf_op jit(solution)/shard_map/ppermute | solution.py:554
  147.8 4.1 %collective-permute-done.29.refs_6_ = bf16[48,2048]{1,0:T(8,128)(2,1)S(1)} collective-permute-done((bf16[48,2048]{1,0:T(8,128)(2,1)}, bf16[48,2048]{1,0:T(8,128)(2,1)S(1)}, u32[]{:S(2)}, u32[]{:S(2)}) %collective-permute-start.29) | collective-permute-done | bytes 196640 | tf_op jit(solution)/shard_map/ppermute | solution.py:554
  152.8 1.7 %combine_choices.1 = bf16[1,128,2048]{2,1,0:T(8,128)(2,1)} custom-call(f32[128,128]{1,0:T(8,128)S(1)} %copy-done.1, bf16[48,2048]{1,0:T(8,128)(2,1)S(1)} %copy-done, bf16[48,2048]{1,0:T(8,128)(2,1)S(1)} %collective-permute-done.23.refs_0_, bf16[48,2048]{1,0:T(8,128)(2,1)S(1)} %collective-permute-done.24.refs_1_, ...), custom_call_target="tpu_custom_call" | custom-call | tf_op jit(solution)/shard_map/combine_choices/pallas_call | solution.py:538
  (56 shorter events, 16.6 us)
Async XLA Ops:
  0.0 46.7 %collective-permute-start.7 = (bf16[1,512,1024]{2,1,0:T(8,128)(2,1)}, bf16[1,512,1024]{2,1,0:T(8,128)(2,1)}, u32[]{:S(2)}, u32[]{:S(2)}) collective-permute-start(bf16[1,512,1024]{2,1,0:T(8,128)(2,1)} %refs_16_), channel_id=1, source_target_pairs={{0,16},{8,24},{16,0},{24,8},{1,17},{9,25},{17,1},{25,9},{2,18},{10... | collective-permute-start | bytes 3145736 | tf_op jit(solution)/shard_map/ppermute | solution.py:554
  5.5 7.5 %collective-permute-start = (bf16[400,256]{1,0:T(8,128)(2,1)}, bf16[400,256]{1,0:T(8,128)(2,1)}, u32[]{:S(2)}, u32[]{:S(2)}) collective-permute-start(bf16[400,256]{1,0:T(8,128)(2,1)} %get-tuple-element.75), channel_id=1, source_target_pairs={{0,1},{1,0},{2,3},{3,2},{4,5},{5,4},{6,7},{7,6},{8,9},{9,8},{10,11... | collective-permute-start | bytes 614408 | tf_op jit(solution)/shard_map/ppermute | solution.py:554
  7.1 13.9 %collective-permute-start.1 = (bf16[400,256]{1,0:T(8,128)(2,1)}, bf16[400,256]{1,0:T(8,128)(2,1)}, u32[]{:S(2)}, u32[]{:S(2)}) collective-permute-start(bf16[400,256]{1,0:T(8,128)(2,1)} %get-tuple-element.76), channel_id=1, source_target_pairs={{0,2},{1,3},{2,0},{3,1},{4,6},{5,7},{6,4},{7,5},{8,10},{9,11},{10,... | collective-permute-start | bytes 614408 | tf_op jit(solution)/shard_map/ppermute | solution.py:554
  7.5 16.0 %collective-permute-start.2 = (bf16[400,256]{1,0:T(8,128)(2,1)}, bf16[400,256]{1,0:T(8,128)(2,1)}, u32[]{:S(2)}, u32[]{:S(2)}) collective-permute-start(bf16[400,256]{1,0:T(8,128)(2,1)} %get-tuple-element.77), channel_id=1, source_target_pairs={{0,3},{1,2},{2,1},{3,0},{4,7},{5,6},{6,5},{7,4},{8,11},{9,10},{10,... | collective-permute-start | bytes 614408 | tf_op jit(solution)/shard_map/ppermute | solution.py:554
  9.1 16.2 %collective-permute-start.3 = (bf16[400,256]{1,0:T(8,128)(2,1)}, bf16[400,256]{1,0:T(8,128)(2,1)}, u32[]{:S(2)}, u32[]{:S(2)}) collective-permute-start(bf16[400,256]{1,0:T(8,128)(2,1)} %get-tuple-element.78), channel_id=1, source_target_pairs={{0,4},{1,5},{2,6},{3,7},{4,0},{5,1},{6,2},{7,3},{8,12},{9,13},{10,... | collective-permute-start | bytes 614408 | tf_op jit(solution)/shard_map/ppermute | solution.py:554
  13.0 25.3 %collective-permute-start.4 = (bf16[400,256]{1,0:T(8,128)(2,1)}, bf16[400,256]{1,0:T(8,128)(2,1)}, u32[]{:S(2)}, u32[]{:S(2)}) collective-permute-start(bf16[400,256]{1,0:T(8,128)(2,1)} %get-tuple-element.79), channel_id=1, source_target_pairs={{0,5},{1,4},{2,7},{3,6},{4,1},{5,0},{6,3},{7,2},{8,13},{9,12},{10,... | collective-permute-start | bytes 614408 | tf_op jit(solution)/shard_map/ppermute | solution.py:554
  20.9 22.6 %collective-permute-start.5 = (bf16[400,256]{1,0:T(8,128)(2,1)}, bf16[400,256]{1,0:T(8,128)(2,1)}, u32[]{:S(2)}, u32[]{:S(2)}) collective-permute-start(bf16[400,256]{1,0:T(8,128)(2,1)} %get-tuple-element.80), channel_id=1, source_target_pairs={{0,6},{1,7},{2,4},{3,5},{4,2},{5,3},{6,0},{7,1},{8,14},{9,15},{10,... | collective-permute-start | bytes 614408 | tf_op jit(solution)/shard_map/ppermute | solution.py:554
  23.6 23.1 %collective-permute-start.6 = (bf16[400,256]{1,0:T(8,128)(2,1)}, bf16[400,256]{1,0:T(8,128)(2,1)}, u32[]{:S(2)}, u32[]{:S(2)}) collective-permute-start(bf16[400,256]{1,0:T(8,128)(2,1)} %get-tuple-element.81), channel_id=1, source_target_pairs={{0,7},{1,6},{2,5},{3,4},{4,3},{5,2},{6,1},{7,0},{8,15},{9,14},{10,... | collective-permute-start | bytes 614408 | tf_op jit(solution)/shard_map/ppermute | solution.py:554
  25.3 29.4 %collective-permute-start.11 = (bf16[1,512,1024]{2,1,0:T(8,128)(2,1)}, bf16[1,512,1024]{2,1,0:T(8,128)(2,1)}, u32[]{:S(2)}, u32[]{:S(2)}) collective-permute-start(bf16[1,512,1024]{2,1,0:T(8,128)(2,1)} %refs_20_), channel_id=1, source_target_pairs={{0,16},{8,24},{16,0},{24,8},{1,17},{9,25},{17,1},{25,9},{2,18},{10... | collective-permute-start | bytes 3145736 | tf_op jit(solution)/shard_map/ppermute | solution.py:554
  46.7 8.1 %collective-permute-start.8 = (bf16[1,512,1024]{2,1,0:T(8,128)(2,1)}, bf16[1,512,1024]{2,1,0:T(8,128)(2,1)}, u32[]{:S(2)}, u32[]{:S(2)}) collective-permute-start(bf16[1,512,1024]{2,1,0:T(8,128)(2,1)} %refs_16_), channel_id=1, source_target_pairs={{0,8},{8,0},{16,24},{24,16},{1,9},{9,1},{17,25},{25,17},{2,10},{10... | collective-permute-start | bytes 3145736 | tf_op jit(solution)/shard_map/ppermute | solution.py:554
  46.7 8.1 %collective-permute-start.9 = (bf16[1,512,1024]{2,1,0:T(8,128)(2,1)}, bf16[1,512,1024]{2,1,0:T(8,128)(2,1)}, u32[]{:S(2)}, u32[]{:S(2)}) collective-permute-start(bf16[1,512,1024]{2,1,0:T(8,128)(2,1)} %collective-permute-done.7.refs_18_), channel_id=1, source_target_pairs={{0,8},{8,0},{16,24},{24,16},{1,9},{9,1},{17,25},{25,17},{2,10},{10... | collective-permute-start | bytes 3145736 | tf_op jit(solution)/shard_map/ppermute | solution.py:554
  47.2 7.6 %collective-permute-start.10 = (bf16[1,512,1024]{2,1,0:T(8,128)(2,1)}, bf16[1,512,1024]{2,1,0:T(8,128)(2,1)}, u32[]{:S(2)}, u32[]{:S(2)}) collective-permute-start(bf16[1,512,1024]{2,1,0:T(8,128)(2,1)} %refs_20_), channel_id=1, source_target_pairs={{0,8},{8,0},{16,24},{24,16},{1,9},{9,1},{17,25},{25,17},{2,10},{10... | collective-permute-start | bytes 3145736 | tf_op jit(solution)/shard_map/ppermute | solution.py:554
  47.2 7.6 %collective-permute-start.12 = (bf16[1,256,2048]{2,1,0:T(8,128)(2,1)}, bf16[1,256,2048]{2,1,0:T(8,128)(2,1)}, u32[]{:S(2)}, u32[]{:S(2)}) collective-permute-start(bf16[1,256,2048]{2,1,0:T(8,128)(2,1)} %refs_24_), channel_id=1, source_target_pairs={{0,8},{8,0},{16,24},{24,16},{1,9},{9,1},{17,25},{25,17},{2,10},{10... | collective-permute-start | bytes 3145736 | tf_op jit(solution)/shard_map/ppermute | solution.py:554
  54.8 40.4 %collective-permute-start.20 = (bf16[1,256,2048]{2,1,0:T(8,128)(2,1)}, bf16[1,256,2048]{2,1,0:T(8,128)(2,1)S(1)}, u32[]{:S(2)}, u32[]{:S(2)}) collective-permute-start(bf16[1,256,2048]{2,1,0:T(8,128)(2,1)} %refs_24_), channel_id=1, source_target_pairs={{0,16},{8,24},{16,0},{24,8},{1,17},{9,25},{17,1},{25,9},{2,18},{10... | collective-permute-start | bytes 3145736 | tf_op jit(solution)/shard_map/ppermute | solution.py:554
  55.3 7.1 %collective-permute-start.13 = (bf16[8,48,256]{2,1,0:T(8,128)(2,1)}, bf16[8,48,256]{2,1,0:T(8,128)(2,1)S(1)}, u32[]{:S(2)}, u32[]{:S(2)}) collective-permute-start(bf16[8,48,256]{2,1,0:T(8,128)(2,1)} %get-tuple-element.103), channel_id=1, source_target_pairs={{0,1},{1,0},{2,3},{3,2},{4,5},{5,4},{6,7},{7,6},{8,9},{9,8},{10,11... | collective-permute-start | bytes 589832 | tf_op jit(solution)/shard_map/ppermute | solution.py:554
  56.1 11.9 %collective-permute-start.14 = (bf16[8,48,256]{2,1,0:T(8,128)(2,1)}, bf16[8,48,256]{2,1,0:T(8,128)(2,1)S(1)}, u32[]{:S(2)}, u32[]{:S(2)}) collective-permute-start(bf16[8,48,256]{2,1,0:T(8,128)(2,1)} %get-tuple-element.104), channel_id=1, source_target_pairs={{0,2},{1,3},{2,0},{3,1},{4,6},{5,7},{6,4},{7,5},{8,10},{9,11},{10,... | collective-permute-start | bytes 589832 | tf_op jit(solution)/shard_map/ppermute | solution.py:554
  56.1 15.8 %collective-permute-start.15 = (bf16[8,48,256]{2,1,0:T(8,128)(2,1)}, bf16[8,48,256]{2,1,0:T(8,128)(2,1)S(1)}, u32[]{:S(2)}, u32[]{:S(2)}) collective-permute-start(bf16[8,48,256]{2,1,0:T(8,128)(2,1)} %get-tuple-element.105), channel_id=1, source_target_pairs={{0,3},{1,2},{2,1},{3,0},{4,7},{5,6},{6,5},{7,4},{8,11},{9,10},{10,... | collective-permute-start | bytes 589832 | tf_op jit(solution)/shard_map/ppermute | solution.py:554
  58.8 24.5 %collective-permute-start.16 = (bf16[8,48,256]{2,1,0:T(8,128)(2,1)}, bf16[8,48,256]{2,1,0:T(8,128)(2,1)S(1)}, u32[]{:S(2)}, u32[]{:S(2)}) collective-permute-start(bf16[8,48,256]{2,1,0:T(8,128)(2,1)} %get-tuple-element.106), channel_id=1, source_target_pairs={{0,4},{1,5},{2,6},{3,7},{4,0},{5,1},{6,2},{7,3},{8,12},{9,13},{10,... | collective-permute-start | bytes 589832 | tf_op jit(solution)/shard_map/ppermute | solution.py:554
  62.5 36.9 %copy-start.5 = (bf16[8,48,256]{2,1,0:T(8,128)(2,1)}, bf16[8,48,256]{2,1,0:T(8,128)(2,1)S(1)}, u32[]{:S(2)}) copy-start(bf16[8,48,256]{2,1,0:T(8,128)(2,1)S(1)} %collective-permute-done.13) | copy-start | bytes 589828
  62.5 25.2 %collective-permute-start.17 = (bf16[8,48,256]{2,1,0:T(8,128)(2,1)}, bf16[8,48,256]{2,1,0:T(8,128)(2,1)S(1)}, u32[]{:S(2)}, u32[]{:S(2)}) collective-permute-start(bf16[8,48,256]{2,1,0:T(8,128)(2,1)} %get-tuple-element.107), channel_id=1, source_target_pairs={{0,5},{1,4},{2,7},{3,6},{4,1},{5,0},{6,3},{7,2},{8,13},{9,12},{10,... | collective-permute-start | bytes 589832 | tf_op jit(solution)/shard_map/ppermute | solution.py:554
  68.0 24.3 %collective-permute-start.18 = (bf16[8,48,256]{2,1,0:T(8,128)(2,1)}, bf16[8,48,256]{2,1,0:T(8,128)(2,1)S(1)}, u32[]{:S(2)}, u32[]{:S(2)}) collective-permute-start(bf16[8,48,256]{2,1,0:T(8,128)(2,1)} %get-tuple-element.108), channel_id=1, source_target_pairs={{0,6},{1,7},{2,4},{3,5},{4,2},{5,3},{6,0},{7,1},{8,14},{9,15},{10,... | collective-permute-start | bytes 589832 | tf_op jit(solution)/shard_map/ppermute | solution.py:554
  71.9 23.3 %collective-permute-start.19 = (bf16[8,48,256]{2,1,0:T(8,128)(2,1)}, bf16[8,48,256]{2,1,0:T(8,128)(2,1)S(1)}, u32[]{:S(2)}, u32[]{:S(2)}) collective-permute-start(bf16[8,48,256]{2,1,0:T(8,128)(2,1)} %get-tuple-element.109), channel_id=1, source_target_pairs={{0,7},{1,6},{2,5},{3,4},{4,3},{5,2},{6,1},{7,0},{8,15},{9,14},{10,... | collective-permute-start | bytes 589832 | tf_op jit(solution)/shard_map/ppermute | solution.py:554
  95.2 3.6 %collective-permute-start.21 = (bf16[1,512,1024]{2,1,0:T(8,128)(2,1)}, bf16[1,512,1024]{2,1,0:T(8,128)(2,1)S(1)}, u32[]{:S(2)}, u32[]{:S(2)}) collective-permute-start(bf16[1,512,1024]{2,1,0:T(8,128)(2,1)} %collective-permute-done.11.refs_22_), channel_id=1, source_target_pairs={{0,8},{8,0},{16,24},{24,16},{1,9},{9,1},{17,25},{25,17},{2,10},{10... | collective-permute-start | bytes 3145736 | tf_op jit(solution)/shard_map/ppermute | solution.py:554
  95.3 4.1 %collective-permute-start.22 = (bf16[1,256,2048]{2,1,0:T(8,128)(2,1)S(1)}, bf16[1,256,2048]{2,1,0:T(8,128)(2,1)S(1)}, u32[]{:S(2)}, u32[]{:S(2)}) collective-permute-start(bf16[1,256,2048]{2,1,0:T(8,128)(2,1)S(1)} %collective-permute-done.20.refs_26_), channel_id=1, source_target_pairs={{0,8},{8,0},{16,24},{24,16},{1,9},{9,1},{17,25},{25,17},{2,10},{10... | collective-permute-start | bytes 3145736 | tf_op jit(solution)/shard_map/ppermute | solution.py:554
  100.4 51.5 %copy-start.1 = (f32[128,128]{1,0:T(8,128)S(1)}, f32[128,128]{1,0:T(8,128)}, u32[]{:S(2)}) copy-start(f32[128,128]{1,0:T(8,128)} %get-tuple-element.73.slots_ref) | copy-start | bytes 196612
  111.8 7.4 %collective-permute-start.23 = (bf16[48,2048]{1,0:T(8,128)(2,1)}, bf16[48,2048]{1,0:T(8,128)(2,1)S(1)}, u32[]{:S(2)}, u32[]{:S(2)}) collective-permute-start(bf16[48,2048]{1,0:T(8,128)(2,1)} %get-tuple-element.134), channel_id=1, source_target_pairs={{0,1},{1,0},{2,3},{3,2},{4,5},{5,4},{6,7},{7,6},{8,9},{9,8},{10,11... | collective-permute-start | bytes 589832 | tf_op jit(solution)/shard_map/ppermute | solution.py:554
  113.4 13.4 %collective-permute-start.24 = (bf16[48,2048]{1,0:T(8,128)(2,1)}, bf16[48,2048]{1,0:T(8,128)(2,1)S(1)}, u32[]{:S(2)}, u32[]{:S(2)}) collective-permute-start(bf16[48,2048]{1,0:T(8,128)(2,1)} %get-tuple-element.135), channel_id=1, source_target_pairs={{0,2},{1,3},{2,0},{3,1},{4,6},{5,7},{6,4},{7,5},{8,10},{9,11},{10,... | collective-permute-start | bytes 589832 | tf_op jit(solution)/shard_map/ppermute | solution.py:554
  113.4 16.8 %collective-permute-start.25 = (bf16[48,2048]{1,0:T(8,128)(2,1)}, bf16[48,2048]{1,0:T(8,128)(2,1)S(1)}, u32[]{:S(2)}, u32[]{:S(2)}) collective-permute-start(bf16[48,2048]{1,0:T(8,128)(2,1)} %get-tuple-element.136), channel_id=1, source_target_pairs={{0,3},{1,2},{2,1},{3,0},{4,7},{5,6},{6,5},{7,4},{8,11},{9,10},{10,... | collective-permute-start | bytes 589832 | tf_op jit(solution)/shard_map/ppermute | solution.py:554
  115.4 15.4 %collective-permute-start.26 = (bf16[48,2048]{1,0:T(8,128)(2,1)}, bf16[48,2048]{1,0:T(8,128)(2,1)S(1)}, u32[]{:S(2)}, u32[]{:S(2)}) collective-permute-start(bf16[48,2048]{1,0:T(8,128)(2,1)} %get-tuple-element.137), channel_id=1, source_target_pairs={{0,4},{1,5},{2,6},{3,7},{4,0},{5,1},{6,2},{7,3},{8,12},{9,13},{10,... | collective-permute-start | bytes 589832 | tf_op jit(solution)/shard_map/ppermute | solution.py:554
  116.3 26.7 %collective-permute-start.27 = (bf16[48,2048]{1,0:T(8,128)(2,1)}, bf16[48,2048]{1,0:T(8,128)(2,1)S(1)}, u32[]{:S(2)}, u32[]{:S(2)}) collective-permute-start(bf16[48,2048]{1,0:T(8,128)(2,1)} %get-tuple-element.138), channel_id=1, source_target_pairs={{0,5},{1,4},{2,7},{3,6},{4,1},{5,0},{6,3},{7,2},{8,13},{9,12},{10,... | collective-permute-start | bytes 589832 | tf_op jit(solution)/shard_map/ppermute | solution.py:554
  119.2 28.5 %collective-permute-start.28 = (bf16[48,2048]{1,0:T(8,128)(2,1)}, bf16[48,2048]{1,0:T(8,128)(2,1)S(1)}, u32[]{:S(2)}, u32[]{:S(2)}) collective-permute-start(bf16[48,2048]{1,0:T(8,128)(2,1)} %get-tuple-element.139), channel_id=1, source_target_pairs={{0,6},{1,7},{2,4},{3,5},{4,2},{5,3},{6,0},{7,1},{8,14},{9,15},{10,... | collective-permute-start | bytes 589832 | tf_op jit(solution)/shard_map/ppermute | solution.py:554
  126.8 25.1 %collective-permute-start.29 = (bf16[48,2048]{1,0:T(8,128)(2,1)}, bf16[48,2048]{1,0:T(8,128)(2,1)S(1)}, u32[]{:S(2)}, u32[]{:S(2)}) collective-permute-start(bf16[48,2048]{1,0:T(8,128)(2,1)} %get-tuple-element.140), channel_id=1, source_target_pairs={{0,7},{1,6},{2,5},{3,4},{4,3},{5,2},{6,1},{7,0},{8,15},{9,14},{10,... | collective-permute-start | bytes 589832 | tf_op jit(solution)/shard_map/ppermute | solution.py:554
  (10 other events, 105.4 us)

commit v3 on v2

--- a/solution.py
+++ b/solution.py
@@ -146,22 +146,18 @@
 
 def pack_kernel(owners, q_ref, k_ref, v_ref, *refs):
     given, out_refs, slots_ref = refs[:4], refs[4 : 4 + owners], refs[4 + owners]
-    small, packed, sems, small_sems, store_sems = refs[5 + owners : 9 + owners], *refs[9 + owners :]
+    small, held, packed, sems, store_sems = refs[5 + owners : 9 + owners], *refs[9 + owners :]
     rows = q_ref.shape[1]
     part = packed.shape[2]
     me = lax.axis_index("expert")
     order = list(range(owners // 2, owners)) + list(range(owners // 2))
-    fetches = [pltpu.make_async_copy(given[i], small[i], small_sems.at[i]) for i in range(4)]
-    for fetch in fetches:
+    fetches = [pltpu.make_async_copy(given[i], small[i], sems.at[i]) for i in range(4)]
+    loads = [
+        pltpu.make_async_copy(ref.at[0], held.at[which], sems.at[4 + which])
+        for which, ref in enumerate((q_ref, k_ref, v_ref))
+    ]
+    for fetch in fetches + loads:
         fetch.start()
-    loads = {}
-    for turn in order:
-        lanes = pl.ds(pl.multiple_of((me ^ turn) * part, part), part)
-        for which, ref in enumerate((q_ref, k_ref, v_ref)):
-            loads[turn, which] = pltpu.make_async_copy(
-                ref.at[0, :, lanes], packed.at[turn, pl.ds(which * rows, rows)], sems.at[turn, which]
-            )
-            loads[turn, which].start()
     for fetch in fetches:
         fetch.wait()
     docs_ref, index_ref, gates_ref, limits_ref = small
@@ -201,12 +197,15 @@
     turned = table.T[:META]
     turned = jnp.where(line == 0, docs_ref[...].astype(F32), turned).astype(BF16)
     slots_ref[...] = jnp.where(lane == 0, slots[0], jnp.where(lane == 1, slots[1], -1.0))
+    for load in loads:
+        load.wait()
     stores = []
     for turn in order:
+        lanes = pl.ds(pl.multiple_of((me ^ turn) * part, part), part)
+        for which in range(TOP_ROWS):
+            packed[turn, which * rows : (which + 1) * rows, :] = held[which, :, lanes]
         packed[turn, TOP_ROWS * rows :, :rows] = turned
         packed[turn, TOP_ROWS * rows :, rows:] = jnp.zeros((META, part - rows), BF16)
-        for which in range(TOP_ROWS):
-            loads[turn, which].wait()
         stores.append(pltpu.make_async_copy(packed.at[turn], out_refs[turn], store_sems.at[turn]))
         stores[-1].start()
     for store in stores:
@@ -234,9 +233,9 @@
         out_specs=[ANYWHERE] * owners + [pl.BlockSpec(memory_space=pltpu.VMEM)],
         scratch_shapes=[pltpu.VMEM(array.shape, array.dtype) for array in small]
         + [
+            pltpu.VMEM((TOP_ROWS, rows, width), BF16),
             pltpu.VMEM((owners, deep, part), BF16),
-            pltpu.SemaphoreType.DMA((owners, TOP_ROWS)),
-            pltpu.SemaphoreType.DMA((4,)),
+            pltpu.SemaphoreType.DMA((7,)),
             pltpu.SemaphoreType.DMA((owners,)),
         ],
         compiler_params=pltpu.CompilerParams(vmem_limit_bytes=VMEM_BYTES),
@@ -247,46 +246,41 @@
 
 def attend_kernel(most, count, *refs):
     in_refs, out_refs = refs[:count], refs[count : 2 * count]
-    queries, keys, values, wide_values, docs, slots_of, routed, load_sems, store_sems = refs[2 * count :]
+    held, keys, wide_values, docs, slots_of, routed, load_sems, store_sems = refs[2 * count :]
     me = lax.axis_index("expert")
     experts = count
-    part = queries.shape[2]
+    part = keys.shape[2]
     rows = keys.shape[1]
     reach = keys.shape[0] - count
     heads = part // HEAD_DIM
     factor = math.log2(math.e) / math.sqrt(HEAD_DIM)
     loads = []
     for turn in range(count):
-        source = me ^ turn
-        loads += [
-            pltpu.make_async_copy(
-                in_refs[turn].at[pl.ds(2 * rows, rows + META)], values.at[reach + source], load_sems.at[turn, 0]
-            ),
-            pltpu.make_async_copy(in_refs[turn].at[pl.ds(rows, rows)], keys.at[reach + source], load_sems.at[turn, 1]),
-            pltpu.make_async_copy(in_refs[turn].at[pl.ds(0, rows)], queries.at[source], load_sems.at[turn, 2]),
-        ]
-    for load in loads[0::3] + loads[1::3] + loads[2::3]:
+        loads.append(pltpu.make_async_copy(in_refs[turn], held.at[me ^ turn], load_sems.at[turn]))
+    for load in loads:
         load.start()
     for number in range(reach):
         keys[number] = jnp.zeros((rows, part), BF16)
         for head in range(heads):
             wide_values[head, number] = jnp.zeros((rows, 2 * HEAD_DIM), BF16)
         docs[number] = jnp.full((8, rows), -1.0, F32)
-    for load in loads[0::3]:
+    for number in range(reach, reach + count):
+        for head in range(heads):
+            wide_values[head, number, :, HEAD_DIM:] = jnp.ones((rows, HEAD_DIM), BF16)
+    for load in loads:
         load.wait()
 
-    @pl.loop(reach, reach + count, unroll=True)
+    @pl.loop(0, count, unroll=True)
     def _(number):
+        keys[reach + number] = held[number, rows : 2 * rows]
         for head in range(heads):
-            wide_values[head, number, :, :HEAD_DIM] = values[number, :rows, head * HEAD_DIM : (head + 1) * HEAD_DIM]
-            wide_values[head, number, :, HEAD_DIM:] = jnp.ones((rows, HEAD_DIM), BF16)
-        meta = values[number, rows:, :rows].astype(F32)
-        docs[number] = jnp.broadcast_to(meta[0:1], (8, rows))
+            lanes = slice(head * HEAD_DIM, (head + 1) * HEAD_DIM)
+            wide_values[head, reach + number, :, :HEAD_DIM] = held[number, 2 * rows : 3 * rows, lanes]
+        meta = held[number, TOP_ROWS * rows :, :rows].astype(F32)
+        docs[reach + number] = jnp.broadcast_to(meta[0:1], (8, rows))
         for k in range(TOP):
             slots_of[number, k : k + 1] = meta[1 + 2 * k : 2 + 2 * k] * most + meta[2 + 2 * k : 3 + 2 * k]
 
-    for load in loads[1::3] + loads[2::3]:
-        load.wait()
     lower = lax.broadcasted_iota(jnp.int32, (rows, rows), 1) <= lax.broadcasted_iota(jnp.int32, (rows, rows), 0)
     slot_at = lax.broadcasted_iota(jnp.int32, (experts * most, rows), 0).astype(F32)
     nothing = jnp.zeros((rows, rows), BF16)
@@ -307,7 +301,7 @@
         done = []
         for head in range(heads):
             lanes = slice(head * HEAD_DIM, (head + 1) * HEAD_DIM)
-            query = queries[pl.ds(at, 2), :, lanes].reshape(2 * rows, HEAD_DIM)
+            query = held[pl.ds(at, 2), :rows, lanes].reshape(2 * rows, HEAD_DIM)
             key = keys[pl.ds(at, reach + 2), :, lanes].reshape((reach + 2) * rows, HEAD_DIM)
             scores = lax.dot_general(query, key, (((1,), (1,)), ((), ())), preferred_element_type=F32)
             lines = []
@@ -327,7 +321,7 @@
             done.append((result[:, :HEAD_DIM] / result[:, HEAD_DIM:]).astype(BF16))
         attended = jnp.concatenate(done, axis=1)
         for side in range(2):
-            slots = slots_of[at + side + reach]
+            slots = slots_of[at + side]
             picks = (slot_at == slots[0:1]) | (slot_at == slots[1:2])
             picks = jnp.where(picks, 1.0, 0.0).astype(BF16)
             sent = jnp.dot(picks, attended[side * rows : (side + 1) * rows], preferred_element_type=F32).astype(BF16)
@@ -360,14 +354,13 @@
         in_specs=[ANYWHERE] * count,
         out_specs=[ANYWHERE] * count,
         scratch_shapes=[
-            pltpu.VMEM((count, rows, part), BF16),
+            pltpu.VMEM((count, deepest, part), BF16),
             pltpu.VMEM((total, rows, part), BF16),
-            pltpu.VMEM((total, rows + META, part), BF16),
             pltpu.VMEM((part // HEAD_DIM, total, rows, 2 * HEAD_DIM), BF16),
             pltpu.VMEM((total, 8, rows), F32),
             pltpu.VMEM((total, 8, rows), F32),
             pltpu.VMEM((count, count, most, part), BF16),
-            pltpu.SemaphoreType.DMA((count, 3)),
+            pltpu.SemaphoreType.DMA((count,)),
             pltpu.SemaphoreType.DMA((count, 2)),
         ],
         compiler_params=pltpu.CompilerParams(vmem_limit_bytes=VMEM_BYTES),
@@ -375,11 +368,12 @@
     )(*gathered)
 
 
-def expert_kernel(pieces, blocks, gain_ref, *refs):
-    row_refs, meta_refs, refs = refs[:blocks], refs[blocks : 2 * blocks], refs[2 * blocks :]
+def expert_kernel(pieces, blocks, turns, gain_ref, *refs):
+    some = len(turns)
+    row_refs, meta_refs, refs = refs[:blocks], refs[blocks : blocks + some], refs[blocks + some :]
     gate_refs, up_refs, down_refs = refs[:pieces], refs[pieces : 2 * pieces], refs[2 * pieces : 3 * pieces]
     refs = refs[3 * pieces :]
-    out_refs, refs = refs[:blocks], refs[blocks:]
+    out_refs, refs = refs[:some], refs[some:]
     held_rows, meta_all, gate_all, up_all, down_all, normed, hidden, answers = refs[:8]
     sems, row_sems, store_sems = refs[8:]
     parts, count, part = held_rows.shape
@@ -387,15 +381,15 @@
     wide = gate_all.shape[3]
     width = parts * part
     mine, expert = lax.axis_index("dp"), lax.axis_index("expert")
+    at = [(expert ^ turn) & (some - 1) for turn in turns]
+    first_row = pl.multiple_of(((expert ^ turns[0]) - at[0]) * most, 16)
     loads = []
     for turn in range(blocks):
-        source = expert ^ turn
-        loads += [
-            pltpu.make_async_copy(row_refs[turn], held_rows.at[source], row_sems.at[turn, 0]),
-            pltpu.make_async_copy(
-                meta_refs[turn].at[pl.ds(meta_refs[turn].shape[0] - META, META)], meta_all.at[source], row_sems.at[turn, 1]
-            ),
-        ]
+        rows = row_refs[turn].at[pl.ds(first_row, count)]
+        loads.append(pltpu.make_async_copy(rows, held_rows.at[expert ^ turn], row_sems.at[turn, 0]))
+    for number in range(some):
+        meta = meta_refs[number].at[pl.ds(meta_refs[number].shape[0] - META, META)]
+        loads.append(pltpu.make_async_copy(meta, meta_all.at[at[number]], row_sems.at[number, 1]))
 
     def tile_copies(step):
         tile = pl.ds(pl.multiple_of((mine ^ step) * wide, wide), wide)
@@ -411,13 +405,13 @@
 
     for load in loads:
         load.start()
+    for step in range(pieces):
+        for copy in tile_copies(step):
+            copy.start(priority=1)
+    for step in range(pieces):
+        down_copy(step).start(priority=1)
     for load in loads:
         load.wait()
-    for step in range(pieces):
-        for copy in tile_copies(step):
-            copy.start()
-    for step in range(pieces):
-        down_copy(step).start()
 
     squares = jnp.zeros((count, part), F32)
     for number in range(parts):
@@ -443,13 +437,13 @@
     rows = LANES
     slot_of = lax.broadcasted_iota(jnp.int32, (most, rows), 0).astype(F32) + (expert * most).astype(F32)
     weights, firsts = [], []
-    for number in range(blocks):
+    for number in range(some):
         meta = meta_all[number, :, :rows].astype(F32)
         total = jnp.zeros((most, rows), F32)
         for k in range(TOP):
             slot = meta[1 + 2 * k : 2 + 2 * k] * most + meta[2 + 2 * k : 3 + 2 * k]
-            at = 1 + 2 * TOP + 3 * k
-            weight = meta[at : at + 1] + meta[at + 1 : at + 2] + meta[at + 2 : at + 3]
+            line = 1 + 2 * TOP + 3 * k
+            weight = meta[line : line + 1] + meta[line + 1 : line + 2] + meta[line + 2 : line + 3]
             total = total + jnp.where(slot_of == slot, weight, 0.0)
             if k == 0:
                 firsts.append(jnp.sum(jnp.where(slot_of == slot, 1.0, 0.0), axis=1, keepdims=True))
@@ -465,50 +459,47 @@
             result = result + jnp.dot(hidden[piece], down_all[piece, :, lanes], preferred_element_type=F32)
         result = result.astype(BF16).astype(F32) * weight
         result = (held_rows[number].astype(F32) * first + result).astype(BF16)
-        for source in range(blocks):
+        for source in range(some):
             answers[source, :, lanes] = result[source * most : (source + 1) * most]
         if number % 2 == 1:
-            for turn in range(blocks):
-                some = pl.ds((number - 1) * part, 2 * part)
-                stores.append(
-                    pltpu.make_async_copy(
-                        answers.at[expert ^ turn, :, some], out_refs[turn].at[:, some], store_sems.at[turn, number // 2]
-                    )
-                )
+            columns = pl.ds((number - 1) * part, 2 * part)
+            for turn in range(some):
+                source, target = answers.at[at[turn], :, columns], out_refs[turn].at[:, columns]
+                stores.append(pltpu.make_async_copy(source, target, store_sems.at[turn, number // 2]))
                 stores[-1].start()
     for store in stores:
         store.wait()
 
 
-def run_expert(rows, gathered, gain, gates, ups, downs, most):
+def run_expert(turns, rows, gathered, gain, gates, ups, downs, most):
     blocks = len(rows)
-    count, part = rows[0].shape
+    count, part = len(turns) * most, rows[0].shape[1]
     width = blocks * part
     pieces = len(downs)
     wide = downs[1].shape[1]
     deep = width // pieces
     return pl.pallas_call(
-        functools.partial(expert_kernel, pieces, blocks),
-        out_shape=[jax.ShapeDtypeStruct((most, width), BF16)] * blocks,
+        functools.partial(expert_kernel, pieces, blocks, turns),
+        out_shape=[jax.ShapeDtypeStruct((most, width), BF16)] * len(turns),
         in_specs=[pl.BlockSpec(memory_space=pltpu.VMEM)]
-        + [ANYWHERE] * (2 * blocks + 3 * pieces),
-        out_specs=[ANYWHERE] * blocks,
+        + [ANYWHERE] * (blocks + len(turns) + 3 * pieces),
+        out_specs=[ANYWHERE] * len(turns),
         scratch_shapes=[
             pltpu.VMEM((blocks, count, part), BF16),
-            pltpu.VMEM((blocks, META, part), BF16),
+            pltpu.VMEM((len(turns), META, part), BF16),
             pltpu.VMEM((pieces, pieces, deep, wide), BF16),
             pltpu.VMEM((pieces, pieces, deep, wide), BF16),
             pltpu.VMEM((pieces, wide, width), BF16),
             pltpu.VMEM((count, width), BF16),
             pltpu.VMEM((pieces, count, wide), BF16),
-            pltpu.VMEM((blocks, most, width), BF16),
+            pltpu.VMEM((len(turns), most, width), BF16),
             pltpu.SemaphoreType.DMA((3, pieces, pieces)),
             pltpu.SemaphoreType.DMA((blocks, 2)),
             pltpu.SemaphoreType.DMA((blocks, blocks // 2)),
         ],
         compiler_params=pltpu.CompilerParams(vmem_limit_bytes=VMEM_BYTES),
         name="expert_rows",
-    )(gain[None, :], *rows, *gathered, *gates, *ups, *downs)
+    )(gain[None, :], *rows, *(gathered[turn] for turn in turns), *gates, *ups, *downs)
 
 
 def combine_kernel(blocks, slots_ref, own_ref, *refs):
@@ -575,6 +566,7 @@
 ):
     rows, width = queries.shape[1:]
     experts = lax.axis_size("expert")
+    half = experts // 2
     most = most_of(rows, experts)
     over = lax.axis_size("dp")
     weights = [gate_weight, up_weight, down_weight]
@@ -600,7 +592,9 @@
             pieces[number + 1] = flipped(pieces[number], "dp", 1)
     gate, up, down = ([pieces[number] for number in range(over)] for pieces in (gate, up, down))
     received = [block.reshape(experts * most, width // experts) for block in received]
-    answered = run_expert(received, gathered, norm_gain, gate, up, down, most)
+    answered = []
+    for turns in (range(half, experts), range(half)):
+        answered = [*run_expert(turns, received, gathered, norm_gain, gate, up, down, most), *answered]
     return combine(exchange(answered), slots)
 
 

time: 155 us -> 152 us (0.981)
  the two profiles are of different devices: /device:TPU:8 before, /device:TPU:0 now
where the time goes in v3:
time: 152 us
  waiting for transfers between devices  66.6 us (44%)
  starting transfers between devices  52.2 us (34%)
  Pallas kernels  30.1 us (20%)
  local copies, waits for them, and re-layouts  2.95 us (2%)
    ppermute x30, waiting for transfers between devices, flipped(): lax.ppermute(block, axis, [(i, i ^ bits) for i in range(lax.axis_size(axi...  66.6 us
    ppermute x30, starting transfers between devices, flipped(): lax.ppermute(block, axis, [(i, i ^ bits) for i in range(lax.axis_size(axi...  52.2 us
    pallas_call x2, Pallas kernels, run_expert(): pl.pallas_call(functools.partial(expert_kernel, pieces, blocks, turns), o...  16.9 us
    pallas_call x1, Pallas kernels, attend(): pl.pallas_call(functools.partial(attend_kernel, most, count), out_shape=[...  6.96 us
    pallas_call x1, Pallas kernels, pack(): pl.pallas_call(functools.partial(pack_kernel, owners), out_shape=[jax.Sha...  3.35 us
  transfers between devices with their start and end apart: 30, of which 14 were waited for; matrix products, arithmetic and copies ran while one was open for 0% of the time, Pallas kernels for 12%

profile of v3, /device:TPU:0, one launch (start us, length us, event | category | flops | bytes accessed | tf_op | source)
XLA Modules:
  0.0 152.0 jit_solution(4978311302338780446)
XLA Ops:
  0.0 3.0 %collective-permute-start.7 = (bf16[1,512,1024]{2,1,0:T(8,128)(2,1)}, bf16[1,512,1024]{2,1,0:T(8,128)(2,1)}, u32[]{:S(2)}, u32[]{:S(2)}) collective-permute-start(bf16[1,512,1024]{2,1,0:T(8,128)(2,1)} %refs_12_.1), channel_id=1, source_target_pairs={{0,16},{8,24},{16,0},{24,8},{1,17},{9,25},{17,1},{25,9},{2,18},{10... | collective-permute-start | bytes 3145736 | tf_op jit(solution)/shard_map/ppermute | solution.py:545
  3.0 3.4 %pack_by_heads.1 = (bf16[400,256]{1,0:T(8,128)(2,1)}, bf16[400,256]{1,0:T(8,128)(2,1)}, bf16[400,256]{1,0:T(8,128)(2,1)}, bf16[400,256]{1,0:T(8,128)(2,1)}, bf16...) custom-call(bf16[1,128,2048]{2,1,0:T(8,128)(2,1)} %q_ref.1, ...), custom_call_target="tpu_custom_call" | custom-call | tf_op jit(solution)/shard_map/pack_by_heads/pallas_call | solution.py:229
  6.3 1.6 %collective-permute-start = (bf16[400,256]{1,0:T(8,128)(2,1)}, bf16[400,256]{1,0:T(8,128)(2,1)}, u32[]{:S(2)}, u32[]{:S(2)}) collective-permute-start(bf16[400,256]{1,0:T(8,128)(2,1)} %get-tuple-element.75), channel_id=1, source_target_pairs={{0,1},{1,0},{2,3},{3,2},{4,5},{5,4},{6,7},{7,6},{8,9},{9,8},{10,11... | collective-permute-start | bytes 614408 | tf_op jit(solution)/shard_map/ppermute | solution.py:545
  7.9 1.6 %collective-permute-start.1 = (bf16[400,256]{1,0:T(8,128)(2,1)}, bf16[400,256]{1,0:T(8,128)(2,1)}, u32[]{:S(2)}, u32[]{:S(2)}) collective-permute-start(bf16[400,256]{1,0:T(8,128)(2,1)} %get-tuple-element.76), channel_id=1, source_target_pairs={{0,2},{1,3},{2,0},{3,1},{4,6},{5,7},{6,4},{7,5},{8,10},{9,11},{10,... | collective-permute-start | bytes 614408 | tf_op jit(solution)/shard_map/ppermute | solution.py:545
  9.9 2.6 %collective-permute-start.3 = (bf16[400,256]{1,0:T(8,128)(2,1)}, bf16[400,256]{1,0:T(8,128)(2,1)}, u32[]{:S(2)}, u32[]{:S(2)}) collective-permute-start(bf16[400,256]{1,0:T(8,128)(2,1)} %get-tuple-element.78), channel_id=1, source_target_pairs={{0,4},{1,5},{2,6},{3,7},{4,0},{5,1},{6,2},{7,3},{8,12},{9,13},{10,... | collective-permute-start | bytes 614408 | tf_op jit(solution)/shard_map/ppermute | solution.py:545
  13.6 3.7 %collective-permute-start.4 = (bf16[400,256]{1,0:T(8,128)(2,1)}, bf16[400,256]{1,0:T(8,128)(2,1)}, u32[]{:S(2)}, u32[]{:S(2)}) collective-permute-start(bf16[400,256]{1,0:T(8,128)(2,1)} %get-tuple-element.79), channel_id=1, source_target_pairs={{0,5},{1,4},{2,7},{3,6},{4,1},{5,0},{6,3},{7,2},{8,13},{9,12},{10,... | collective-permute-start | bytes 614408 | tf_op jit(solution)/shard_map/ppermute | solution.py:545
  17.3 6.4 %collective-permute-done.1.refs_2_.refs_10_ = bf16[400,256]{1,0:T(8,128)(2,1)} collective-permute-done((bf16[400,256]{1,0:T(8,128)(2,1)}, bf16[400,256]{1,0:T(8,128)(2,1)}, u32[]{:S(2)}, u32[]{:S(2)}) %collective-permute-start.1) | collective-permute-done | bytes 204832 | tf_op jit(solution)/shard_map/ppermute | solution.py:545
  23.8 2.3 %collective-permute-start.5 = (bf16[400,256]{1,0:T(8,128)(2,1)}, bf16[400,256]{1,0:T(8,128)(2,1)}, u32[]{:S(2)}, u32[]{:S(2)}) collective-permute-start(bf16[400,256]{1,0:T(8,128)(2,1)} %get-tuple-element.80), channel_id=1, source_target_pairs={{0,6},{1,7},{2,4},{3,5},{4,2},{5,3},{6,0},{7,1},{8,14},{9,15},{10,... | collective-permute-start | bytes 614408 | tf_op jit(solution)/shard_map/ppermute | solution.py:545
  26.2 3.4 %collective-permute-start.6 = (bf16[400,256]{1,0:T(8,128)(2,1)}, bf16[400,256]{1,0:T(8,128)(2,1)}, u32[]{:S(2)}, u32[]{:S(2)}) collective-permute-start(bf16[400,256]{1,0:T(8,128)(2,1)} %get-tuple-element.81), channel_id=1, source_target_pairs={{0,7},{1,6},{2,5},{3,4},{4,3},{5,2},{6,1},{7,0},{8,15},{9,14},{10,... | collective-permute-start | bytes 614408 | tf_op jit(solution)/shard_map/ppermute | solution.py:545
  30.1 11.1 %collective-permute-done.4.refs_5_.refs_9_ = bf16[400,256]{1,0:T(8,128)(2,1)} collective-permute-done((bf16[400,256]{1,0:T(8,128)(2,1)}, bf16[400,256]{1,0:T(8,128)(2,1)}, u32[]{:S(2)}, u32[]{:S(2)}) %collective-permute-start.4) | collective-permute-done | bytes 204832 | tf_op jit(solution)/shard_map/ppermute | solution.py:545
  42.3 7.0 %attend_and_route.1 = (bf16[8,48,256]{2,1,0:T(8,128)(2,1)}, bf16[8,48,256]{2,1,0:T(8,128)(2,1)}, bf16[8,48,256]{2,1,0:T(8,128)(2,1)}, bf16[8,48,256]{2,1,0:T(8,1...) custom-call(bf16[400,256]{1,0:T(8,128)(2,1)} %get-tuple-element.82.r, ...), custom_call_target="tpu_custom_call" | custom-call | tf_op jit(solution)/shard_map/attend_and_route/pallas_call | solution.py:351
  49.3 3.8 %collective-permute-done.11.refs_18_ = bf16[1,512,1024]{2,1,0:T(8,128)(2,1)} collective-permute-done((bf16[1,512,1024]{2,1,0:T(8,128)(2,1)}, bf16[1,512,1024]{2,1,0:T(8,128)(2,1)}, u32[]{:S(2)}, u32[]{:S(2)}) %collective-permute-start.11) | collective-permute-done | bytes 1048608 | tf_op jit(solution)/shard_map/ppermute | solution.py:545
  53.7 4.8 %collective-permute-start.14 = (bf16[8,48,256]{2,1,0:T(8,128)(2,1)}, bf16[8,48,256]{2,1,0:T(8,128)(2,1)S(1)}, u32[]{:S(2)}, u32[]{:S(2)}) collective-permute-start(bf16[8,48,256]{2,1,0:T(8,128)(2,1)} %get-tuple-element.104), channel_id=1, source_target_pairs={{0,2},{1,3},{2,0},{3,1},{4,6},{5,7},{6,4},{7,5},{8,10},{9,11},{10,... | collective-permute-start | bytes 589832 | tf_op jit(solution)/shard_map/ppermute | solution.py:545
  59.2 4.2 %collective-permute-start.16 = (bf16[8,48,256]{2,1,0:T(8,128)(2,1)}, bf16[8,48,256]{2,1,0:T(8,128)(2,1)S(1)}, u32[]{:S(2)}, u32[]{:S(2)}) collective-permute-start(bf16[8,48,256]{2,1,0:T(8,128)(2,1)} %get-tuple-element.106), channel_id=1, source_target_pairs={{0,4},{1,5},{2,6},{3,7},{4,0},{5,1},{6,2},{7,3},{8,12},{9,13},{10,... | collective-permute-start | bytes 589832 | tf_op jit(solution)/shard_map/ppermute | solution.py:545
  63.3 3.6 %collective-permute-start.17 = (bf16[8,48,256]{2,1,0:T(8,128)(2,1)}, bf16[8,48,256]{2,1,0:T(8,128)(2,1)S(1)}, u32[]{:S(2)}, u32[]{:S(2)}) collective-permute-start(bf16[8,48,256]{2,1,0:T(8,128)(2,1)} %get-tuple-element.107), channel_id=1, source_target_pairs={{0,5},{1,4},{2,7},{3,6},{4,1},{5,0},{6,3},{7,2},{8,13},{9,12},{10,... | collective-permute-start | bytes 589832 | tf_op jit(solution)/shard_map/ppermute | solution.py:545
  66.9 4.3 %collective-permute-done.14 = bf16[8,48,256]{2,1,0:T(8,128)(2,1)S(1)} collective-permute-done((bf16[8,48,256]{2,1,0:T(8,128)(2,1)}, bf16[8,48,256]{2,1,0:T(8,128)(2,1)S(1)}, u32[]{:S(2)}, u32[]{:S(2)}) %collective-permute-start.14) | collective-permute-done | bytes 196640 | tf_op jit(solution)/shard_map/ppermute | solution.py:545
  71.2 2.0 %collective-permute-start.18 = (bf16[8,48,256]{2,1,0:T(8,128)(2,1)}, bf16[8,48,256]{2,1,0:T(8,128)(2,1)S(1)}, u32[]{:S(2)}, u32[]{:S(2)}) collective-permute-start(bf16[8,48,256]{2,1,0:T(8,128)(2,1)} %get-tuple-element.108), channel_id=1, source_target_pairs={{0,6},{1,7},{2,4},{3,5},{4,2},{5,3},{6,0},{7,1},{8,14},{9,15},{10,... | collective-permute-start | bytes 589832 | tf_op jit(solution)/shard_map/ppermute | solution.py:545
  73.2 2.5 %collective-permute-done.15 = bf16[8,48,256]{2,1,0:T(8,128)(2,1)S(1)} collective-permute-done((bf16[8,48,256]{2,1,0:T(8,128)(2,1)}, bf16[8,48,256]{2,1,0:T(8,128)(2,1)S(1)}, u32[]{:S(2)}, u32[]{:S(2)}) %collective-permute-start.15) | collective-permute-done | bytes 196640 | tf_op jit(solution)/shard_map/ppermute | solution.py:545
  75.7 1.4 collective-permute-start.19
  77.0 13.0 %collective-permute-done.17 = bf16[8,48,256]{2,1,0:T(8,128)(2,1)S(1)} collective-permute-done((bf16[8,48,256]{2,1,0:T(8,128)(2,1)}, bf16[8,48,256]{2,1,0:T(8,128)(2,1)S(1)}, u32[]{:S(2)}, u32[]{:S(2)}) %collective-permute-start.17) | collective-permute-done | bytes 196640 | tf_op jit(solution)/shard_map/ppermute | solution.py:545
  91.2 1.8 %collective-permute-done.21.refs_19_ = bf16[1,512,1024]{2,1,0:T(8,128)(2,1)S(1)} collective-permute-done((bf16[1,512,1024]{2,1,0:T(8,128)(2,1)}, bf16[1,512,1024]{2,1,0:T(8,128)(2,1)S(1)}, u32[]{:S(2)}, u32[]{:S(2)}) %collective-permute-start.21) | collective-permute-done | bytes 1048608 | tf_op jit(solution)/shard_map/ppermute | solution.py:545
  95.3 8.4 %expert_rows.3 = (bf16[48,2048]{1,0:T(8,128)(2,1)}, bf16[48,2048]{1,0:T(8,128)(2,1)}, bf16[48,2048]{1,0:T(8,128)(2,1)}, bf16[48,2048]{1,0:T(8,128)(2,1)}) custom-call(f32[1,2048]{1,0:T(1,128)} %bitcast.32, bf16[384,256]{1,0:T(8,128)(2,1)} %bitcast.16, bf16[384,256]{1,0:T(8,128)(2,1)} %bitcast.18, bf16[384,256]{1,0:T(8,128)(2,1)} %bitcast.20, ...), custom_call_target="tpu_custom_call" | custom-call | tf_op jit(solution)/shard_map/expert_rows/pallas_call | solution.py:481
  103.8 8.5 %collective-permute-start.26 = (bf16[48,2048]{1,0:T(8,128)(2,1)}, bf16[48,2048]{1,0:T(8,128)(2,1)}, u32[]{:S(2)}, u32[]{:S(2)}) collective-permute-start(bf16[48,2048]{1,0:T(8,128)(2,1)} %get-tuple-element.137), channel_id=1, source_target_pairs={{0,4},{1,5},{2,6},{3,7},{4,0},{5,1},{6,2},{7,3},{8,12},{9,13},{10,... | collective-permute-start | bytes 589832 | tf_op jit(solution)/shard_map/ppermute | solution.py:545
  113.2 1.5 collective-permute-start.28
  114.7 2.4 %collective-permute-start.29 = (bf16[48,2048]{1,0:T(8,128)(2,1)}, bf16[48,2048]{1,0:T(8,128)(2,1)}, u32[]{:S(2)}, u32[]{:S(2)}) collective-permute-start(bf16[48,2048]{1,0:T(8,128)(2,1)} %get-tuple-element.140), channel_id=1, source_target_pairs={{0,7},{1,6},{2,5},{3,4},{4,3},{5,2},{6,1},{7,0},{8,15},{9,14},{10,... | collective-permute-start | bytes 589832 | tf_op jit(solution)/shard_map/ppermute | solution.py:545
  117.0 8.4 %expert_rows.2 = (bf16[48,2048]{1,0:T(8,128)(2,1)}, bf16[48,2048]{1,0:T(8,128)(2,1)}, bf16[48,2048]{1,0:T(8,128)(2,1)}, bf16[48,2048]{1,0:T(8,128)(2,1)}) custom-call(f32[1,2048]{1,0:T(1,128)} %bitcast.33, bf16[384,256]{1,0:T(8,128)(2,1)} %bitcast.17, bf16[384,256]{1,0:T(8,128)(2,1)} %bitcast.19, bf16[384,256]{1,0:T(8,128)(2,1)} %bitcast.21, ...), custom_call_target="tpu_custom_call" | custom-call | tf_op jit(solution)/shard_map/expert_rows/pallas_call | solution.py:481
  125.5 1.5 %collective-permute-start.23 = (bf16[48,2048]{1,0:T(8,128)(2,1)}, bf16[48,2048]{1,0:T(8,128)(2,1)S(1)}, u32[]{:S(2)}, u32[]{:S(2)}) collective-permute-start(bf16[48,2048]{1,0:T(8,128)(2,1)} %get-tuple-element.134), channel_id=1, source_target_pairs={{0,1},{1,0},{2,3},{3,2},{4,5},{5,4},{6,7},{7,6},{8,9},{9,8},{10,11... | collective-permute-start | bytes 589832 | tf_op jit(solution)/shard_map/ppermute | solution.py:545
  127.0 8.1 %collective-permute-done.26.refs_3_ = bf16[48,2048]{1,0:T(8,128)(2,1)} collective-permute-done((bf16[48,2048]{1,0:T(8,128)(2,1)}, bf16[48,2048]{1,0:T(8,128)(2,1)}, u32[]{:S(2)}, u32[]{:S(2)}) %collective-permute-start.26) | collective-permute-done | bytes 196640 | tf_op jit(solution)/shard_map/ppermute | solution.py:545
  135.1 5.1 %collective-permute-done.27.refs_4_ = bf16[48,2048]{1,0:T(8,128)(2,1)} collective-permute-done((bf16[48,2048]{1,0:T(8,128)(2,1)}, bf16[48,2048]{1,0:T(8,128)(2,1)}, u32[]{:S(2)}, u32[]{:S(2)}) %collective-permute-start.27) | collective-permute-done | bytes 196640 | tf_op jit(solution)/shard_map/ppermute | solution.py:545
  140.3 3.0 %collective-permute-done.24.refs_1_ = bf16[48,2048]{1,0:T(8,128)(2,1)S(1)} collective-permute-done((bf16[48,2048]{1,0:T(8,128)(2,1)}, bf16[48,2048]{1,0:T(8,128)(2,1)S(1)}, u32[]{:S(2)}, u32[]{:S(2)}) %collective-permute-start.24) | collective-permute-done | bytes 196640 | tf_op jit(solution)/shard_map/ppermute | solution.py:545
  143.3 4.8 %collective-permute-done.25.refs_2_ = bf16[48,2048]{1,0:T(8,128)(2,1)S(1)} collective-permute-done((bf16[48,2048]{1,0:T(8,128)(2,1)}, bf16[48,2048]{1,0:T(8,128)(2,1)S(1)}, u32[]{:S(2)}, u32[]{:S(2)}) %collective-permute-start.25) | collective-permute-done | bytes 196640 | tf_op jit(solution)/shard_map/ppermute | solution.py:545
  149.1 2.9 %combine_choices.1 = bf16[1,128,2048]{2,1,0:T(8,128)(2,1)} custom-call(f32[128,128]{1,0:T(8,128)S(1)} %copy-done.1, bf16[48,2048]{1,0:T(8,128)(2,1)S(1)} %copy-done, bf16[48,2048]{1,0:T(8,128)(2,1)S(1)} %collective-permute-done.23.refs_0_, bf16[48,2048]{1,0:T(8,128)(2,1)S(1)} %collective-permute-done.24.refs_1_, ...), custom_call_target="tpu_custom_call" | custom-call | tf_op jit(solution)/shard_map/combine_choices/pallas_call | solution.py:529
  (57 shorter events, 9.9 us)
Async XLA Ops:
  0.0 41.2 %collective-permute-start.7 = (bf16[1,512,1024]{2,1,0:T(8,128)(2,1)}, bf16[1,512,1024]{2,1,0:T(8,128)(2,1)}, u32[]{:S(2)}, u32[]{:S(2)}) collective-permute-start(bf16[1,512,1024]{2,1,0:T(8,128)(2,1)} %refs_12_.1), channel_id=1, source_target_pairs={{0,16},{8,24},{16,0},{24,8},{1,17},{9,25},{17,1},{25,9},{2,18},{10... | collective-permute-start | bytes 3145736 | tf_op jit(solution)/shard_map/ppermute | solution.py:545
  6.3 7.3 %collective-permute-start = (bf16[400,256]{1,0:T(8,128)(2,1)}, bf16[400,256]{1,0:T(8,128)(2,1)}, u32[]{:S(2)}, u32[]{:S(2)}) collective-permute-start(bf16[400,256]{1,0:T(8,128)(2,1)} %get-tuple-element.75), channel_id=1, source_target_pairs={{0,1},{1,0},{2,3},{3,2},{4,5},{5,4},{6,7},{7,6},{8,9},{9,8},{10,11... | collective-permute-start | bytes 614408 | tf_op jit(solution)/shard_map/ppermute | solution.py:545
  7.9 15.9 %collective-permute-start.1 = (bf16[400,256]{1,0:T(8,128)(2,1)}, bf16[400,256]{1,0:T(8,128)(2,1)}, u32[]{:S(2)}, u32[]{:S(2)}) collective-permute-start(bf16[400,256]{1,0:T(8,128)(2,1)} %get-tuple-element.76), channel_id=1, source_target_pairs={{0,2},{1,3},{2,0},{3,1},{4,6},{5,7},{6,4},{7,5},{8,10},{9,11},{10,... | collective-permute-start | bytes 614408 | tf_op jit(solution)/shard_map/ppermute | solution.py:545
  9.5 16.8 %collective-permute-start.2 = (bf16[400,256]{1,0:T(8,128)(2,1)}, bf16[400,256]{1,0:T(8,128)(2,1)}, u32[]{:S(2)}, u32[]{:S(2)}) collective-permute-start(bf16[400,256]{1,0:T(8,128)(2,1)} %get-tuple-element.77), channel_id=1, source_target_pairs={{0,3},{1,2},{2,1},{3,0},{4,7},{5,6},{6,5},{7,4},{8,11},{9,10},{10,... | collective-permute-start | bytes 614408 | tf_op jit(solution)/shard_map/ppermute | solution.py:545
  9.9 19.7 %collective-permute-start.3 = (bf16[400,256]{1,0:T(8,128)(2,1)}, bf16[400,256]{1,0:T(8,128)(2,1)}, u32[]{:S(2)}, u32[]{:S(2)}) collective-permute-start(bf16[400,256]{1,0:T(8,128)(2,1)} %get-tuple-element.78), channel_id=1, source_target_pairs={{0,4},{1,5},{2,6},{3,7},{4,0},{5,1},{6,2},{7,3},{8,12},{9,13},{10,... | collective-permute-start | bytes 614408 | tf_op jit(solution)/shard_map/ppermute | solution.py:545
  13.6 27.6 %collective-permute-start.4 = (bf16[400,256]{1,0:T(8,128)(2,1)}, bf16[400,256]{1,0:T(8,128)(2,1)}, u32[]{:S(2)}, u32[]{:S(2)}) collective-permute-start(bf16[400,256]{1,0:T(8,128)(2,1)} %get-tuple-element.79), channel_id=1, source_target_pairs={{0,5},{1,4},{2,7},{3,6},{4,1},{5,0},{6,3},{7,2},{8,13},{9,12},{10,... | collective-permute-start | bytes 614408 | tf_op jit(solution)/shard_map/ppermute | solution.py:545
  23.8 17.4 %collective-permute-start.5 = (bf16[400,256]{1,0:T(8,128)(2,1)}, bf16[400,256]{1,0:T(8,128)(2,1)}, u32[]{:S(2)}, u32[]{:S(2)}) collective-permute-start(bf16[400,256]{1,0:T(8,128)(2,1)} %get-tuple-element.80), channel_id=1, source_target_pairs={{0,6},{1,7},{2,4},{3,5},{4,2},{5,3},{6,0},{7,1},{8,14},{9,15},{10,... | collective-permute-start | bytes 614408 | tf_op jit(solution)/shard_map/ppermute | solution.py:545
  26.2 15.0 %collective-permute-start.6 = (bf16[400,256]{1,0:T(8,128)(2,1)}, bf16[400,256]{1,0:T(8,128)(2,1)}, u32[]{:S(2)}, u32[]{:S(2)}) collective-permute-start(bf16[400,256]{1,0:T(8,128)(2,1)} %get-tuple-element.81), channel_id=1, source_target_pairs={{0,7},{1,6},{2,5},{3,4},{4,3},{5,2},{6,1},{7,0},{8,15},{9,14},{10,... | collective-permute-start | bytes 614408 | tf_op jit(solution)/shard_map/ppermute | solution.py:545
  29.6 23.4 %collective-permute-start.11 = (bf16[1,512,1024]{2,1,0:T(8,128)(2,1)}, bf16[1,512,1024]{2,1,0:T(8,128)(2,1)}, u32[]{:S(2)}, u32[]{:S(2)}) collective-permute-start(bf16[1,512,1024]{2,1,0:T(8,128)(2,1)} %refs_16_.1), channel_id=1, source_target_pairs={{0,16},{8,24},{16,0},{24,8},{1,17},{9,25},{17,1},{25,9},{2,18},{10... | collective-permute-start | bytes 3145736 | tf_op jit(solution)/shard_map/ppermute | solution.py:545
  41.2 11.8 %collective-permute-start.8 = (bf16[1,512,1024]{2,1,0:T(8,128)(2,1)}, bf16[1,512,1024]{2,1,0:T(8,128)(2,1)}, u32[]{:S(2)}, u32[]{:S(2)}) collective-permute-start(bf16[1,512,1024]{2,1,0:T(8,128)(2,1)} %refs_12_.1), channel_id=1, source_target_pairs={{0,8},{8,0},{16,24},{24,16},{1,9},{9,1},{17,25},{25,17},{2,10},{10... | collective-permute-start | bytes 3145736 | tf_op jit(solution)/shard_map/ppermute | solution.py:545
  41.3 11.8 %collective-permute-start.9 = (bf16[1,512,1024]{2,1,0:T(8,128)(2,1)}, bf16[1,512,1024]{2,1,0:T(8,128)(2,1)}, u32[]{:S(2)}, u32[]{:S(2)}) collective-permute-start(bf16[1,512,1024]{2,1,0:T(8,128)(2,1)} %collective-permute-done.7.refs_14_), channel_id=1, source_target_pairs={{0,8},{8,0},{16,24},{24,16},{1,9},{9,1},{17,25},{25,17},{2,10},{10... | collective-permute-start | bytes 3145736 | tf_op jit(solution)/shard_map/ppermute | solution.py:545
  41.8 11.3 %collective-permute-start.10 = (bf16[1,512,1024]{2,1,0:T(8,128)(2,1)}, bf16[1,512,1024]{2,1,0:T(8,128)(2,1)}, u32[]{:S(2)}, u32[]{:S(2)}) collective-permute-start(bf16[1,512,1024]{2,1,0:T(8,128)(2,1)} %refs_16_.1), channel_id=1, source_target_pairs={{0,8},{8,0},{16,24},{24,16},{1,9},{9,1},{17,25},{25,17},{2,10},{10... | collective-permute-start | bytes 3145736 | tf_op jit(solution)/shard_map/ppermute | solution.py:545
  41.9 11.2 %collective-permute-start.12 = (bf16[1,256,2048]{2,1,0:T(8,128)(2,1)}, bf16[1,256,2048]{2,1,0:T(8,128)(2,1)}, u32[]{:S(2)}, u32[]{:S(2)}) collective-permute-start(bf16[1,256,2048]{2,1,0:T(8,128)(2,1)} %refs_20_.1), channel_id=1, source_target_pairs={{0,8},{8,0},{16,24},{24,16},{1,9},{9,1},{17,25},{25,17},{2,10},{10... | collective-permute-start | bytes 3145736 | tf_op jit(solution)/shard_map/ppermute | solution.py:545
  53.1 37.0 %collective-permute-start.20 = (bf16[1,256,2048]{2,1,0:T(8,128)(2,1)}, bf16[1,256,2048]{2,1,0:T(8,128)(2,1)S(1)}, u32[]{:S(2)}, u32[]{:S(2)}) collective-permute-start(bf16[1,256,2048]{2,1,0:T(8,128)(2,1)} %refs_20_.1), channel_id=1, source_target_pairs={{0,16},{8,24},{16,0},{24,8},{1,17},{9,25},{17,1},{25,9},{2,18},{10... | collective-permute-start | bytes 3145736 | tf_op jit(solution)/shard_map/ppermute | solution.py:545
  53.7 9.7 %collective-permute-start.13 = (bf16[8,48,256]{2,1,0:T(8,128)(2,1)}, bf16[8,48,256]{2,1,0:T(8,128)(2,1)S(1)}, u32[]{:S(2)}, u32[]{:S(2)}) collective-permute-start(bf16[8,48,256]{2,1,0:T(8,128)(2,1)} %get-tuple-element.103), channel_id=1, source_target_pairs={{0,1},{1,0},{2,3},{3,2},{4,5},{5,4},{6,7},{7,6},{8,9},{9,8},{10,11... | collective-permute-start | bytes 589832 | tf_op jit(solution)/shard_map/ppermute | solution.py:545
  53.7 17.6 %collective-permute-start.14 = (bf16[8,48,256]{2,1,0:T(8,128)(2,1)}, bf16[8,48,256]{2,1,0:T(8,128)(2,1)S(1)}, u32[]{:S(2)}, u32[]{:S(2)}) collective-permute-start(bf16[8,48,256]{2,1,0:T(8,128)(2,1)} %get-tuple-element.104), channel_id=1, source_target_pairs={{0,2},{1,3},{2,0},{3,1},{4,6},{5,7},{6,4},{7,5},{8,10},{9,11},{10,... | collective-permute-start | bytes 589832 | tf_op jit(solution)/shard_map/ppermute | solution.py:545
  58.5 17.2 %collective-permute-start.15 = (bf16[8,48,256]{2,1,0:T(8,128)(2,1)}, bf16[8,48,256]{2,1,0:T(8,128)(2,1)S(1)}, u32[]{:S(2)}, u32[]{:S(2)}) collective-permute-start(bf16[8,48,256]{2,1,0:T(8,128)(2,1)} %get-tuple-element.105), channel_id=1, source_target_pairs={{0,3},{1,2},{2,1},{3,0},{4,7},{5,6},{6,5},{7,4},{8,11},{9,10},{10,... | collective-permute-start | bytes 589832 | tf_op jit(solution)/shard_map/ppermute | solution.py:545
  59.2 17.9 %collective-permute-start.16 = (bf16[8,48,256]{2,1,0:T(8,128)(2,1)}, bf16[8,48,256]{2,1,0:T(8,128)(2,1)S(1)}, u32[]{:S(2)}, u32[]{:S(2)}) collective-permute-start(bf16[8,48,256]{2,1,0:T(8,128)(2,1)} %get-tuple-element.106), channel_id=1, source_target_pairs={{0,4},{1,5},{2,6},{3,7},{4,0},{5,1},{6,2},{7,3},{8,12},{9,13},{10,... | collective-permute-start | bytes 589832 | tf_op jit(solution)/shard_map/ppermute | solution.py:545
  63.3 32.0 %copy-start.5 = (bf16[8,48,256]{2,1,0:T(8,128)(2,1)}, bf16[8,48,256]{2,1,0:T(8,128)(2,1)S(1)}, u32[]{:S(2)}) copy-start(bf16[8,48,256]{2,1,0:T(8,128)(2,1)S(1)} %collective-permute-done.13) | copy-start | bytes 589828
  63.3 26.7 %collective-permute-start.17 = (bf16[8,48,256]{2,1,0:T(8,128)(2,1)}, bf16[8,48,256]{2,1,0:T(8,128)(2,1)S(1)}, u32[]{:S(2)}, u32[]{:S(2)}) collective-permute-start(bf16[8,48,256]{2,1,0:T(8,128)(2,1)} %get-tuple-element.107), channel_id=1, source_target_pairs={{0,5},{1,4},{2,7},{3,6},{4,1},{5,0},{6,3},{7,2},{8,13},{9,12},{10,... | collective-permute-start | bytes 589832 | tf_op jit(solution)/shard_map/ppermute | solution.py:545
  71.2 18.8 %collective-permute-start.18 = (bf16[8,48,256]{2,1,0:T(8,128)(2,1)}, bf16[8,48,256]{2,1,0:T(8,128)(2,1)S(1)}, u32[]{:S(2)}, u32[]{:S(2)}) collective-permute-start(bf16[8,48,256]{2,1,0:T(8,128)(2,1)} %get-tuple-element.108), channel_id=1, source_target_pairs={{0,6},{1,7},{2,4},{3,5},{4,2},{5,3},{6,0},{7,1},{8,14},{9,15},{10,... | collective-permute-start | bytes 589832 | tf_op jit(solution)/shard_map/ppermute | solution.py:545
  75.7 14.4 %collective-permute-start.19 = (bf16[8,48,256]{2,1,0:T(8,128)(2,1)}, bf16[8,48,256]{2,1,0:T(8,128)(2,1)S(1)}, u32[]{:S(2)}, u32[]{:S(2)}) collective-permute-start(bf16[8,48,256]{2,1,0:T(8,128)(2,1)} %get-tuple-element.109), channel_id=1, source_target_pairs={{0,7},{1,6},{2,5},{3,4},{4,3},{5,2},{6,1},{7,0},{8,15},{9,14},{10,... | collective-permute-start | bytes 589832 | tf_op jit(solution)/shard_map/ppermute | solution.py:545
  90.1 2.9 %collective-permute-start.21 = (bf16[1,512,1024]{2,1,0:T(8,128)(2,1)}, bf16[1,512,1024]{2,1,0:T(8,128)(2,1)S(1)}, u32[]{:S(2)}, u32[]{:S(2)}) collective-permute-start(bf16[1,512,1024]{2,1,0:T(8,128)(2,1)} %collective-permute-done.11.refs_18_), channel_id=1, source_target_pairs={{0,8},{8,0},{16,24},{24,16},{1,9},{9,1},{17,25},{25,17},{2,10},{10... | collective-permute-start | bytes 3145736 | tf_op jit(solution)/shard_map/ppermute | solution.py:545
  91.2 3.1 %collective-permute-start.22 = (bf16[1,256,2048]{2,1,0:T(8,128)(2,1)S(1)}, bf16[1,256,2048]{2,1,0:T(8,128)(2,1)S(1)}, u32[]{:S(2)}, u32[]{:S(2)}) collective-permute-start(bf16[1,256,2048]{2,1,0:T(8,128)(2,1)S(1)} %collective-permute-done.20.refs_22_), channel_id=1, source_target_pairs={{0,8},{8,0},{16,24},{24,16},{1,9},{9,1},{17,25},{25,17},{2,10},{10... | collective-permute-start | bytes 3145736 | tf_op jit(solution)/shard_map/ppermute | solution.py:545
  103.8 31.4 %collective-permute-start.26 = (bf16[48,2048]{1,0:T(8,128)(2,1)}, bf16[48,2048]{1,0:T(8,128)(2,1)}, u32[]{:S(2)}, u32[]{:S(2)}) collective-permute-start(bf16[48,2048]{1,0:T(8,128)(2,1)} %get-tuple-element.137), channel_id=1, source_target_pairs={{0,4},{1,5},{2,6},{3,7},{4,0},{5,1},{6,2},{7,3},{8,12},{9,13},{10,... | collective-permute-start | bytes 589832 | tf_op jit(solution)/shard_map/ppermute | solution.py:545
  112.2 28.0 %collective-permute-start.27 = (bf16[48,2048]{1,0:T(8,128)(2,1)}, bf16[48,2048]{1,0:T(8,128)(2,1)}, u32[]{:S(2)}, u32[]{:S(2)}) collective-permute-start(bf16[48,2048]{1,0:T(8,128)(2,1)} %get-tuple-element.138), channel_id=1, source_target_pairs={{0,5},{1,4},{2,7},{3,6},{4,1},{5,0},{6,3},{7,2},{8,13},{9,12},{10,... | collective-permute-start | bytes 589832 | tf_op jit(solution)/shard_map/ppermute | solution.py:545
  113.2 27.1 %collective-permute-start.28 = (bf16[48,2048]{1,0:T(8,128)(2,1)}, bf16[48,2048]{1,0:T(8,128)(2,1)}, u32[]{:S(2)}, u32[]{:S(2)}) collective-permute-start(bf16[48,2048]{1,0:T(8,128)(2,1)} %get-tuple-element.139), channel_id=1, source_target_pairs={{0,6},{1,7},{2,4},{3,5},{4,2},{5,3},{6,0},{7,1},{8,14},{9,15},{10,... | collective-permute-start | bytes 589832 | tf_op jit(solution)/shard_map/ppermute | solution.py:545
  114.7 33.5 %copy-start.1 = (f32[128,128]{1,0:T(8,128)S(1)}, f32[128,128]{1,0:T(8,128)}, u32[]{:S(2)}) copy-start(f32[128,128]{1,0:T(8,128)} %get-tuple-element.73.slots_ref) | copy-start | bytes 196612
  114.7 25.6 %collective-permute-start.29 = (bf16[48,2048]{1,0:T(8,128)(2,1)}, bf16[48,2048]{1,0:T(8,128)(2,1)}, u32[]{:S(2)}, u32[]{:S(2)}) collective-permute-start(bf16[48,2048]{1,0:T(8,128)(2,1)} %get-tuple-element.140), channel_id=1, source_target_pairs={{0,7},{1,6},{2,5},{3,4},{4,3},{5,2},{6,1},{7,0},{8,15},{9,14},{10,... | collective-permute-start | bytes 589832 | tf_op jit(solution)/shard_map/ppermute | solution.py:545
  125.5 14.8 %collective-permute-start.23 = (bf16[48,2048]{1,0:T(8,128)(2,1)}, bf16[48,2048]{1,0:T(8,128)(2,1)S(1)}, u32[]{:S(2)}, u32[]{:S(2)}) collective-permute-start(bf16[48,2048]{1,0:T(8,128)(2,1)} %get-tuple-element.134), channel_id=1, source_target_pairs={{0,1},{1,0},{2,3},{3,2},{4,5},{5,4},{6,7},{7,6},{8,9},{9,8},{10,11... | collective-permute-start | bytes 589832 | tf_op jit(solution)/shard_map/ppermute | solution.py:545
  135.1 8.2 %collective-permute-start.24 = (bf16[48,2048]{1,0:T(8,128)(2,1)}, bf16[48,2048]{1,0:T(8,128)(2,1)S(1)}, u32[]{:S(2)}, u32[]{:S(2)}) collective-permute-start(bf16[48,2048]{1,0:T(8,128)(2,1)} %get-tuple-element.135), channel_id=1, source_target_pairs={{0,2},{1,3},{2,0},{3,1},{4,6},{5,7},{6,4},{7,5},{8,10},{9,11},{10,... | collective-permute-start | bytes 589832 | tf_op jit(solution)/shard_map/ppermute | solution.py:545
  140.3 7.9 %collective-permute-start.25 = (bf16[48,2048]{1,0:T(8,128)(2,1)}, bf16[48,2048]{1,0:T(8,128)(2,1)S(1)}, u32[]{:S(2)}, u32[]{:S(2)}) collective-permute-start(bf16[48,2048]{1,0:T(8,128)(2,1)} %get-tuple-element.136), channel_id=1, source_target_pairs={{0,3},{1,2},{2,1},{3,0},{4,7},{5,6},{6,5},{7,4},{8,11},{9,10},{10,... | collective-permute-start | bytes 589832 | tf_op jit(solution)/shard_map/ppermute | solution.py:545
  (10 other events, 82.0 us)

commit v4 on v3

--- a/solution.py
+++ b/solution.py
@@ -497,45 +497,32 @@
             pltpu.SemaphoreType.DMA((blocks, 2)),
             pltpu.SemaphoreType.DMA((blocks, blocks // 2)),
         ],
-        compiler_params=pltpu.CompilerParams(vmem_limit_bytes=VMEM_BYTES),
+        compiler_params=pltpu.CompilerParams(vmem_limit_bytes=57344 * 1024),
         name="expert_rows",
     )(gain[None, :], *rows, *(gathered[turn] for turn in turns), *gates, *ups, *downs)
 
 
-def combine_kernel(blocks, slots_ref, own_ref, *refs):
-    row_refs, out_ref, own, slots, sems = refs[: blocks - 1], *refs[blocks - 1 :]
-    loads = [
-        pltpu.make_async_copy(slots_ref, slots, sems.at[0]),
-        pltpu.make_async_copy(own_ref, own, sems.at[1]),
-    ]
-    for load in loads:
-        load.start()
-    most = own.shape[0]
-    rows = slots.shape[0]
+def combine_kernel(blocks, slots_ref, *refs):
+    row_refs, out_ref = refs[:blocks], refs[blocks]
+    most = row_refs[0].shape[0]
+    rows = slots_ref.shape[0]
     column = lax.broadcasted_iota(jnp.int32, (rows, blocks * most), 1)
     slot_of = (((column // most) ^ lax.axis_index("expert")) * most + column % most).astype(F32)
-    loads[0].wait()
-    picks = (slot_of == slots[:, 0:1]) | (slot_of == slots[:, 1:2])
+    picks = (slot_of == slots_ref[:, 0:1]) | (slot_of == slots_ref[:, 1:2])
     picks = jnp.where(picks, 1.0, 0.0).astype(BF16)
-    loads[1].wait()
-    held = jnp.concatenate([own[...]] + [ref[...] for ref in row_refs], axis=0)
+    held = jnp.concatenate([ref[...] for ref in row_refs], axis=0)
     out_ref[0] = jnp.dot(picks, held, preferred_element_type=F32).astype(BF16)
 
 
 def combine(returned, slots):
     blocks = len(returned)
-    most, width = returned[0].shape
+    width = returned[0].shape[1]
     vmem = pl.BlockSpec(memory_space=pltpu.VMEM)
     return pl.pallas_call(
         functools.partial(combine_kernel, blocks),
         out_shape=jax.ShapeDtypeStruct((1, slots.shape[0], width), BF16),
-        in_specs=[pl.BlockSpec(memory_space=pltpu.HBM)] * 2 + [vmem] * (blocks - 1),
+        in_specs=[vmem] * (1 + blocks),
         out_specs=vmem,
-        scratch_shapes=[
-            pltpu.VMEM(returned[0].shape, BF16),
-            pltpu.VMEM(slots.shape, F32),
-            pltpu.SemaphoreType.DMA((2,)),
-        ],
         compiler_params=pltpu.CompilerParams(vmem_limit_bytes=24 * 1024 * 1024),
         name="combine_choices",
     )(slots, *returned)

time: 152 us -> 151 us (level)
  Pallas kernels: 30.1 us -> 28.5 us
    pallas_call x1, Pallas kernels: 2.9 us -> 1.3 us  [combine(): pl.pallas_call(functools.partial(combine_kernel, blocks), out_shape=jax.S...]
where the time goes in v4:
time: 151 us; the launch traced here: 150 us
  waiting for transfers between devices  67.1 us (44%)
  starting transfers between devices  52.6 us (35%)
  Pallas kernels  28.5 us (19%)
  local copies, waits for them, and re-layouts  1.88 us (1%)
    ppermute x30, waiting for transfers between devices, flipped(): lax.ppermute(block, axis, [(i, i ^ bits) for i in range(lax.axis_size(axi...  67.1 us
    ppermute x30, starting transfers between devices, flipped(): lax.ppermute(block, axis, [(i, i ^ bits) for i in range(lax.axis_size(axi...  52.6 us
    pallas_call x2, Pallas kernels, run_expert(): pl.pallas_call(functools.partial(expert_kernel, pieces, blocks, turns), o...  16.8 us
    pallas_call x1, Pallas kernels, attend(): pl.pallas_call(functools.partial(attend_kernel, most, count), out_shape=[...  6.96 us
    pallas_call x1, Pallas kernels, pack(): pl.pallas_call(functools.partial(pack_kernel, owners), out_shape=[jax.Sha...  3.35 us
  transfers between devices with their start and end apart: 30, of which 14 were waited for; matrix products, arithmetic and copies ran while one was open for 0% of the time, Pallas kernels for 12%

profile of v4, /device:TPU:0, one launch (start us, length us, event | category | flops | bytes accessed | tf_op | source)
XLA Modules:
  0.0 150.3 jit_solution(5771167172972936210)
XLA Ops:
  0.0 3.0 %collective-permute-start.7 = (bf16[1,512,1024]{2,1,0:T(8,128)(2,1)}, bf16[1,512,1024]{2,1,0:T(8,128)(2,1)}, u32[]{:S(2)}, u32[]{:S(2)}) collective-permute-start(bf16[1,512,1024]{2,1,0:T(8,128)(2,1)} %refs_12_.1), channel_id=1, source_target_pairs={{0,16},{8,24},{16,0},{24,8},{1,17},{9,25},{17,1},{25,9},{2,18},{10... | collective-permute-start | bytes 3145736 | tf_op jit(solution)/shard_map/ppermute | solution.py:532
  3.0 3.3 %pack_by_heads.1 = (bf16[400,256]{1,0:T(8,128)(2,1)}, bf16[400,256]{1,0:T(8,128)(2,1)}, bf16[400,256]{1,0:T(8,128)(2,1)}, bf16[400,256]{1,0:T(8,128)(2,1)}, bf16...) custom-call(bf16[1,128,2048]{2,1,0:T(8,128)(2,1)} %q_ref.1, ...), custom_call_target="tpu_custom_call" | custom-call | tf_op jit(solution)/shard_map/pack_by_heads/pallas_call | solution.py:229
  6.3 1.6 %collective-permute-start = (bf16[400,256]{1,0:T(8,128)(2,1)}, bf16[400,256]{1,0:T(8,128)(2,1)}, u32[]{:S(2)}, u32[]{:S(2)}) collective-permute-start(bf16[400,256]{1,0:T(8,128)(2,1)} %get-tuple-element.75), channel_id=1, source_target_pairs={{0,1},{1,0},{2,3},{3,2},{4,5},{5,4},{6,7},{7,6},{8,9},{9,8},{10,11... | collective-permute-start | bytes 614408 | tf_op jit(solution)/shard_map/ppermute | solution.py:532
  7.9 1.6 %collective-permute-start.1 = (bf16[400,256]{1,0:T(8,128)(2,1)}, bf16[400,256]{1,0:T(8,128)(2,1)}, u32[]{:S(2)}, u32[]{:S(2)}) collective-permute-start(bf16[400,256]{1,0:T(8,128)(2,1)} %get-tuple-element.76), channel_id=1, source_target_pairs={{0,2},{1,3},{2,0},{3,1},{4,6},{5,7},{6,4},{7,5},{8,10},{9,11},{10,... | collective-permute-start | bytes 614408 | tf_op jit(solution)/shard_map/ppermute | solution.py:532
  9.9 2.6 %collective-permute-start.3 = (bf16[400,256]{1,0:T(8,128)(2,1)}, bf16[400,256]{1,0:T(8,128)(2,1)}, u32[]{:S(2)}, u32[]{:S(2)}) collective-permute-start(bf16[400,256]{1,0:T(8,128)(2,1)} %get-tuple-element.78), channel_id=1, source_target_pairs={{0,4},{1,5},{2,6},{3,7},{4,0},{5,1},{6,2},{7,3},{8,12},{9,13},{10,... | collective-permute-start | bytes 614408 | tf_op jit(solution)/shard_map/ppermute | solution.py:532
  13.6 3.7 %collective-permute-start.4 = (bf16[400,256]{1,0:T(8,128)(2,1)}, bf16[400,256]{1,0:T(8,128)(2,1)}, u32[]{:S(2)}, u32[]{:S(2)}) collective-permute-start(bf16[400,256]{1,0:T(8,128)(2,1)} %get-tuple-element.79), channel_id=1, source_target_pairs={{0,5},{1,4},{2,7},{3,6},{4,1},{5,0},{6,3},{7,2},{8,13},{9,12},{10,... | collective-permute-start | bytes 614408 | tf_op jit(solution)/shard_map/ppermute | solution.py:532
  17.3 6.4 %collective-permute-done.1.refs_2_.refs_10_ = bf16[400,256]{1,0:T(8,128)(2,1)} collective-permute-done((bf16[400,256]{1,0:T(8,128)(2,1)}, bf16[400,256]{1,0:T(8,128)(2,1)}, u32[]{:S(2)}, u32[]{:S(2)}) %collective-permute-start.1) | collective-permute-done | bytes 204832 | tf_op jit(solution)/shard_map/ppermute | solution.py:532
  23.8 2.3 %collective-permute-start.5 = (bf16[400,256]{1,0:T(8,128)(2,1)}, bf16[400,256]{1,0:T(8,128)(2,1)}, u32[]{:S(2)}, u32[]{:S(2)}) collective-permute-start(bf16[400,256]{1,0:T(8,128)(2,1)} %get-tuple-element.80), channel_id=1, source_target_pairs={{0,6},{1,7},{2,4},{3,5},{4,2},{5,3},{6,0},{7,1},{8,14},{9,15},{10,... | collective-permute-start | bytes 614408 | tf_op jit(solution)/shard_map/ppermute | solution.py:532
  26.2 3.4 %collective-permute-start.6 = (bf16[400,256]{1,0:T(8,128)(2,1)}, bf16[400,256]{1,0:T(8,128)(2,1)}, u32[]{:S(2)}, u32[]{:S(2)}) collective-permute-start(bf16[400,256]{1,0:T(8,128)(2,1)} %get-tuple-element.81), channel_id=1, source_target_pairs={{0,7},{1,6},{2,5},{3,4},{4,3},{5,2},{6,1},{7,0},{8,15},{9,14},{10,... | collective-permute-start | bytes 614408 | tf_op jit(solution)/shard_map/ppermute | solution.py:532
  30.1 11.1 %collective-permute-done.4.refs_5_.refs_9_ = bf16[400,256]{1,0:T(8,128)(2,1)} collective-permute-done((bf16[400,256]{1,0:T(8,128)(2,1)}, bf16[400,256]{1,0:T(8,128)(2,1)}, u32[]{:S(2)}, u32[]{:S(2)}) %collective-permute-start.4) | collective-permute-done | bytes 204832 | tf_op jit(solution)/shard_map/ppermute | solution.py:532
  42.3 7.0 %attend_and_route.1 = (bf16[8,48,256]{2,1,0:T(8,128)(2,1)}, bf16[8,48,256]{2,1,0:T(8,128)(2,1)}, bf16[8,48,256]{2,1,0:T(8,128)(2,1)}, bf16[8,48,256]{2,1,0:T(8,1...) custom-call(bf16[400,256]{1,0:T(8,128)(2,1)} %get-tuple-element.82.r, ...), custom_call_target="tpu_custom_call" | custom-call | tf_op jit(solution)/shard_map/attend_and_route/pallas_call | solution.py:351
  49.3 3.8 %collective-permute-done.11.refs_18_ = bf16[1,512,1024]{2,1,0:T(8,128)(2,1)} collective-permute-done((bf16[1,512,1024]{2,1,0:T(8,128)(2,1)}, bf16[1,512,1024]{2,1,0:T(8,128)(2,1)}, u32[]{:S(2)}, u32[]{:S(2)}) %collective-permute-start.11) | collective-permute-done | bytes 1048608 | tf_op jit(solution)/shard_map/ppermute | solution.py:532
  53.6 4.8 %collective-permute-start.14 = (bf16[8,48,256]{2,1,0:T(8,128)(2,1)}, bf16[8,48,256]{2,1,0:T(8,128)(2,1)S(1)}, u32[]{:S(2)}, u32[]{:S(2)}) collective-permute-start(bf16[8,48,256]{2,1,0:T(8,128)(2,1)} %get-tuple-element.104), channel_id=1, source_target_pairs={{0,2},{1,3},{2,0},{3,1},{4,6},{5,7},{6,4},{7,5},{8,10},{9,11},{10,... | collective-permute-start | bytes 589832 | tf_op jit(solution)/shard_map/ppermute | solution.py:532
  59.1 4.2 %collective-permute-start.16 = (bf16[8,48,256]{2,1,0:T(8,128)(2,1)}, bf16[8,48,256]{2,1,0:T(8,128)(2,1)S(1)}, u32[]{:S(2)}, u32[]{:S(2)}) collective-permute-start(bf16[8,48,256]{2,1,0:T(8,128)(2,1)} %get-tuple-element.106), channel_id=1, source_target_pairs={{0,4},{1,5},{2,6},{3,7},{4,0},{5,1},{6,2},{7,3},{8,12},{9,13},{10,... | collective-permute-start | bytes 589832 | tf_op jit(solution)/shard_map/ppermute | solution.py:532
  63.3 3.6 %collective-permute-start.17 = (bf16[8,48,256]{2,1,0:T(8,128)(2,1)}, bf16[8,48,256]{2,1,0:T(8,128)(2,1)S(1)}, u32[]{:S(2)}, u32[]{:S(2)}) collective-permute-start(bf16[8,48,256]{2,1,0:T(8,128)(2,1)} %get-tuple-element.107), channel_id=1, source_target_pairs={{0,5},{1,4},{2,7},{3,6},{4,1},{5,0},{6,3},{7,2},{8,13},{9,12},{10,... | collective-permute-start | bytes 589832 | tf_op jit(solution)/shard_map/ppermute | solution.py:532
  66.9 4.2 %collective-permute-done.14 = bf16[8,48,256]{2,1,0:T(8,128)(2,1)S(1)} collective-permute-done((bf16[8,48,256]{2,1,0:T(8,128)(2,1)}, bf16[8,48,256]{2,1,0:T(8,128)(2,1)S(1)}, u32[]{:S(2)}, u32[]{:S(2)}) %collective-permute-start.14) | collective-permute-done | bytes 196640 | tf_op jit(solution)/shard_map/ppermute | solution.py:532
  71.2 2.0 %collective-permute-start.18 = (bf16[8,48,256]{2,1,0:T(8,128)(2,1)}, bf16[8,48,256]{2,1,0:T(8,128)(2,1)S(1)}, u32[]{:S(2)}, u32[]{:S(2)}) collective-permute-start(bf16[8,48,256]{2,1,0:T(8,128)(2,1)} %get-tuple-element.108), channel_id=1, source_target_pairs={{0,6},{1,7},{2,4},{3,5},{4,2},{5,3},{6,0},{7,1},{8,14},{9,15},{10,... | collective-permute-start | bytes 589832 | tf_op jit(solution)/shard_map/ppermute | solution.py:532
  73.2 2.5 %collective-permute-done.15 = bf16[8,48,256]{2,1,0:T(8,128)(2,1)S(1)} collective-permute-done((bf16[8,48,256]{2,1,0:T(8,128)(2,1)}, bf16[8,48,256]{2,1,0:T(8,128)(2,1)S(1)}, u32[]{:S(2)}, u32[]{:S(2)}) %collective-permute-start.15) | collective-permute-done | bytes 196640 | tf_op jit(solution)/shard_map/ppermute | solution.py:532
  75.7 1.4 collective-permute-start.19
  77.0 13.0 %collective-permute-done.17 = bf16[8,48,256]{2,1,0:T(8,128)(2,1)S(1)} collective-permute-done((bf16[8,48,256]{2,1,0:T(8,128)(2,1)}, bf16[8,48,256]{2,1,0:T(8,128)(2,1)S(1)}, u32[]{:S(2)}, u32[]{:S(2)}) %collective-permute-start.17) | collective-permute-done | bytes 196640 | tf_op jit(solution)/shard_map/ppermute | solution.py:532
  90.6 3.1 %collective-permute-done.21.refs_19_ = bf16[1,512,1024]{2,1,0:T(8,128)(2,1)S(1)} collective-permute-done((bf16[1,512,1024]{2,1,0:T(8,128)(2,1)}, bf16[1,512,1024]{2,1,0:T(8,128)(2,1)S(1)}, u32[]{:S(2)}, u32[]{:S(2)}) %collective-permute-start.21) | collective-permute-done | bytes 1048608 | tf_op jit(solution)/shard_map/ppermute | solution.py:532
  95.3 8.4 %expert_rows.3 = (bf16[48,2048]{1,0:T(8,128)(2,1)}, bf16[48,2048]{1,0:T(8,128)(2,1)}, bf16[48,2048]{1,0:T(8,128)(2,1)}, bf16[48,2048]{1,0:T(8,128)(2,1)}) custom-call(f32[1,2048]{1,0:T(1,128)} %bitcast.32, bf16[384,256]{1,0:T(8,128)(2,1)} %bitcast.16, bf16[384,256]{1,0:T(8,128)(2,1)} %bitcast.18, bf16[384,256]{1,0:T(8,128)(2,1)} %bitcast.20, ...), custom_call_target="tpu_custom_call" | custom-call | tf_op jit(solution)/shard_map/expert_rows/pallas_call | solution.py:481
  103.7 8.5 %collective-permute-start.26 = (bf16[48,2048]{1,0:T(8,128)(2,1)}, bf16[48,2048]{1,0:T(8,128)(2,1)S(1)}, u32[]{:S(2)}, u32[]{:S(2)}) collective-permute-start(bf16[48,2048]{1,0:T(8,128)(2,1)} %get-tuple-element.137), channel_id=1, source_target_pairs={{0,4},{1,5},{2,6},{3,7},{4,0},{5,1},{6,2},{7,3},{8,12},{9,13},{10,... | collective-permute-start | bytes 589832 | tf_op jit(solution)/shard_map/ppermute | solution.py:532
  113.1 1.5 collective-permute-start.28
  114.6 2.4 %collective-permute-start.29 = (bf16[48,2048]{1,0:T(8,128)(2,1)}, bf16[48,2048]{1,0:T(8,128)(2,1)S(1)}, u32[]{:S(2)}, u32[]{:S(2)}) collective-permute-start(bf16[48,2048]{1,0:T(8,128)(2,1)} %get-tuple-element.140), channel_id=1, source_target_pairs={{0,7},{1,6},{2,5},{3,4},{4,3},{5,2},{6,1},{7,0},{8,15},{9,14},{10,... | collective-permute-start | bytes 589832 | tf_op jit(solution)/shard_map/ppermute | solution.py:532
  117.0 8.4 %expert_rows.2 = (bf16[48,2048]{1,0:T(8,128)(2,1)}, bf16[48,2048]{1,0:T(8,128)(2,1)}, bf16[48,2048]{1,0:T(8,128)(2,1)}, bf16[48,2048]{1,0:T(8,128)(2,1)}) custom-call(f32[1,2048]{1,0:T(1,128)} %bitcast.33, bf16[384,256]{1,0:T(8,128)(2,1)} %bitcast.17, bf16[384,256]{1,0:T(8,128)(2,1)} %bitcast.19, bf16[384,256]{1,0:T(8,128)(2,1)} %bitcast.21, ...), custom_call_target="tpu_custom_call" | custom-call | tf_op jit(solution)/shard_map/expert_rows/pallas_call | solution.py:481
  125.4 1.5 %collective-permute-start.23 = (bf16[48,2048]{1,0:T(8,128)(2,1)}, bf16[48,2048]{1,0:T(8,128)(2,1)S(1)}, u32[]{:S(2)}, u32[]{:S(2)}) collective-permute-start(bf16[48,2048]{1,0:T(8,128)(2,1)} %get-tuple-element.134), channel_id=1, source_target_pairs={{0,1},{1,0},{2,3},{3,2},{4,5},{5,4},{6,7},{7,6},{8,9},{9,8},{10,11... | collective-permute-start | bytes 589832 | tf_op jit(solution)/shard_map/ppermute | solution.py:532
  126.9 8.0 %collective-permute-done.26.refs_4_ = bf16[48,2048]{1,0:T(8,128)(2,1)S(1)} collective-permute-done((bf16[48,2048]{1,0:T(8,128)(2,1)}, bf16[48,2048]{1,0:T(8,128)(2,1)S(1)}, u32[]{:S(2)}, u32[]{:S(2)}) %collective-permute-start.26) | collective-permute-done | bytes 196640 | tf_op jit(solution)/shard_map/ppermute | solution.py:532
  135.0 5.1 %collective-permute-done.27.refs_5_ = bf16[48,2048]{1,0:T(8,128)(2,1)S(1)} collective-permute-done((bf16[48,2048]{1,0:T(8,128)(2,1)}, bf16[48,2048]{1,0:T(8,128)(2,1)S(1)}, u32[]{:S(2)}, u32[]{:S(2)}) %collective-permute-start.27) | collective-permute-done | bytes 196640 | tf_op jit(solution)/shard_map/ppermute | solution.py:532
  140.1 3.1 %collective-permute-done.24.refs_2_ = bf16[48,2048]{1,0:T(8,128)(2,1)S(1)} collective-permute-done((bf16[48,2048]{1,0:T(8,128)(2,1)}, bf16[48,2048]{1,0:T(8,128)(2,1)S(1)}, u32[]{:S(2)}, u32[]{:S(2)}) %collective-permute-start.24) | collective-permute-done | bytes 196640 | tf_op jit(solution)/shard_map/ppermute | solution.py:532
  143.2 4.9 %collective-permute-done.25.refs_3_ = bf16[48,2048]{1,0:T(8,128)(2,1)S(1)} collective-permute-done((bf16[48,2048]{1,0:T(8,128)(2,1)}, bf16[48,2048]{1,0:T(8,128)(2,1)S(1)}, u32[]{:S(2)}, u32[]{:S(2)}) %collective-permute-start.25) | collective-permute-done | bytes 196640 | tf_op jit(solution)/shard_map/ppermute | solution.py:532
  149.0 1.3 combine_choices.1
  (57 shorter events, 8.6 us)
Async XLA Ops:
  0.0 41.2 %collective-permute-start.7 = (bf16[1,512,1024]{2,1,0:T(8,128)(2,1)}, bf16[1,512,1024]{2,1,0:T(8,128)(2,1)}, u32[]{:S(2)}, u32[]{:S(2)}) collective-permute-start(bf16[1,512,1024]{2,1,0:T(8,128)(2,1)} %refs_12_.1), channel_id=1, source_target_pairs={{0,16},{8,24},{16,0},{24,8},{1,17},{9,25},{17,1},{25,9},{2,18},{10... | collective-permute-start | bytes 3145736 | tf_op jit(solution)/shard_map/ppermute | solution.py:532
  6.3 7.3 %collective-permute-start = (bf16[400,256]{1,0:T(8,128)(2,1)}, bf16[400,256]{1,0:T(8,128)(2,1)}, u32[]{:S(2)}, u32[]{:S(2)}) collective-permute-start(bf16[400,256]{1,0:T(8,128)(2,1)} %get-tuple-element.75), channel_id=1, source_target_pairs={{0,1},{1,0},{2,3},{3,2},{4,5},{5,4},{6,7},{7,6},{8,9},{9,8},{10,11... | collective-permute-start | bytes 614408 | tf_op jit(solution)/shard_map/ppermute | solution.py:532
  7.9 15.9 %collective-permute-start.1 = (bf16[400,256]{1,0:T(8,128)(2,1)}, bf16[400,256]{1,0:T(8,128)(2,1)}, u32[]{:S(2)}, u32[]{:S(2)}) collective-permute-start(bf16[400,256]{1,0:T(8,128)(2,1)} %get-tuple-element.76), channel_id=1, source_target_pairs={{0,2},{1,3},{2,0},{3,1},{4,6},{5,7},{6,4},{7,5},{8,10},{9,11},{10,... | collective-permute-start | bytes 614408 | tf_op jit(solution)/shard_map/ppermute | solution.py:532
  9.5 16.8 %collective-permute-start.2 = (bf16[400,256]{1,0:T(8,128)(2,1)}, bf16[400,256]{1,0:T(8,128)(2,1)}, u32[]{:S(2)}, u32[]{:S(2)}) collective-permute-start(bf16[400,256]{1,0:T(8,128)(2,1)} %get-tuple-element.77), channel_id=1, source_target_pairs={{0,3},{1,2},{2,1},{3,0},{4,7},{5,6},{6,5},{7,4},{8,11},{9,10},{10,... | collective-permute-start | bytes 614408 | tf_op jit(solution)/shard_map/ppermute | solution.py:532
  9.9 19.7 %collective-permute-start.3 = (bf16[400,256]{1,0:T(8,128)(2,1)}, bf16[400,256]{1,0:T(8,128)(2,1)}, u32[]{:S(2)}, u32[]{:S(2)}) collective-permute-start(bf16[400,256]{1,0:T(8,128)(2,1)} %get-tuple-element.78), channel_id=1, source_target_pairs={{0,4},{1,5},{2,6},{3,7},{4,0},{5,1},{6,2},{7,3},{8,12},{9,13},{10,... | collective-permute-start | bytes 614408 | tf_op jit(solution)/shard_map/ppermute | solution.py:532
  13.6 27.6 %collective-permute-start.4 = (bf16[400,256]{1,0:T(8,128)(2,1)}, bf16[400,256]{1,0:T(8,128)(2,1)}, u32[]{:S(2)}, u32[]{:S(2)}) collective-permute-start(bf16[400,256]{1,0:T(8,128)(2,1)} %get-tuple-element.79), channel_id=1, source_target_pairs={{0,5},{1,4},{2,7},{3,6},{4,1},{5,0},{6,3},{7,2},{8,13},{9,12},{10,... | collective-permute-start | bytes 614408 | tf_op jit(solution)/shard_map/ppermute | solution.py:532
  23.8 17.4 %collective-permute-start.5 = (bf16[400,256]{1,0:T(8,128)(2,1)}, bf16[400,256]{1,0:T(8,128)(2,1)}, u32[]{:S(2)}, u32[]{:S(2)}) collective-permute-start(bf16[400,256]{1,0:T(8,128)(2,1)} %get-tuple-element.80), channel_id=1, source_target_pairs={{0,6},{1,7},{2,4},{3,5},{4,2},{5,3},{6,0},{7,1},{8,14},{9,15},{10,... | collective-permute-start | bytes 614408 | tf_op jit(solution)/shard_map/ppermute | solution.py:532
  26.2 15.0 %collective-permute-start.6 = (bf16[400,256]{1,0:T(8,128)(2,1)}, bf16[400,256]{1,0:T(8,128)(2,1)}, u32[]{:S(2)}, u32[]{:S(2)}) collective-permute-start(bf16[400,256]{1,0:T(8,128)(2,1)} %get-tuple-element.81), channel_id=1, source_target_pairs={{0,7},{1,6},{2,5},{3,4},{4,3},{5,2},{6,1},{7,0},{8,15},{9,14},{10,... | collective-permute-start | bytes 614408 | tf_op jit(solution)/shard_map/ppermute | solution.py:532
  29.6 23.4 %collective-permute-start.11 = (bf16[1,512,1024]{2,1,0:T(8,128)(2,1)}, bf16[1,512,1024]{2,1,0:T(8,128)(2,1)}, u32[]{:S(2)}, u32[]{:S(2)}) collective-permute-start(bf16[1,512,1024]{2,1,0:T(8,128)(2,1)} %refs_16_.1), channel_id=1, source_target_pairs={{0,16},{8,24},{16,0},{24,8},{1,17},{9,25},{17,1},{25,9},{2,18},{10... | collective-permute-start | bytes 3145736 | tf_op jit(solution)/shard_map/ppermute | solution.py:532
  41.2 11.8 %collective-permute-start.8 = (bf16[1,512,1024]{2,1,0:T(8,128)(2,1)}, bf16[1,512,1024]{2,1,0:T(8,128)(2,1)}, u32[]{:S(2)}, u32[]{:S(2)}) collective-permute-start(bf16[1,512,1024]{2,1,0:T(8,128)(2,1)} %refs_12_.1), channel_id=1, source_target_pairs={{0,8},{8,0},{16,24},{24,16},{1,9},{9,1},{17,25},{25,17},{2,10},{10... | collective-permute-start | bytes 3145736 | tf_op jit(solution)/shard_map/ppermute | solution.py:532
  41.3 11.8 %collective-permute-start.9 = (bf16[1,512,1024]{2,1,0:T(8,128)(2,1)}, bf16[1,512,1024]{2,1,0:T(8,128)(2,1)}, u32[]{:S(2)}, u32[]{:S(2)}) collective-permute-start(bf16[1,512,1024]{2,1,0:T(8,128)(2,1)} %collective-permute-done.7.refs_14_), channel_id=1, source_target_pairs={{0,8},{8,0},{16,24},{24,16},{1,9},{9,1},{17,25},{25,17},{2,10},{10... | collective-permute-start | bytes 3145736 | tf_op jit(solution)/shard_map/ppermute | solution.py:532
  41.8 11.3 %collective-permute-start.10 = (bf16[1,512,1024]{2,1,0:T(8,128)(2,1)}, bf16[1,512,1024]{2,1,0:T(8,128)(2,1)}, u32[]{:S(2)}, u32[]{:S(2)}) collective-permute-start(bf16[1,512,1024]{2,1,0:T(8,128)(2,1)} %refs_16_.1), channel_id=1, source_target_pairs={{0,8},{8,0},{16,24},{24,16},{1,9},{9,1},{17,25},{25,17},{2,10},{10... | collective-permute-start | bytes 3145736 | tf_op jit(solution)/shard_map/ppermute | solution.py:532
  41.9 11.2 %collective-permute-start.12 = (bf16[1,256,2048]{2,1,0:T(8,128)(2,1)}, bf16[1,256,2048]{2,1,0:T(8,128)(2,1)}, u32[]{:S(2)}, u32[]{:S(2)}) collective-permute-start(bf16[1,256,2048]{2,1,0:T(8,128)(2,1)} %refs_20_.1), channel_id=1, source_target_pairs={{0,8},{8,0},{16,24},{24,16},{1,9},{9,1},{17,25},{25,17},{2,10},{10... | collective-permute-start | bytes 3145736 | tf_op jit(solution)/shard_map/ppermute | solution.py:532
  53.1 37.0 %collective-permute-start.20 = (bf16[1,256,2048]{2,1,0:T(8,128)(2,1)}, bf16[1,256,2048]{2,1,0:T(8,128)(2,1)S(1)}, u32[]{:S(2)}, u32[]{:S(2)}) collective-permute-start(bf16[1,256,2048]{2,1,0:T(8,128)(2,1)} %refs_20_.1), channel_id=1, source_target_pairs={{0,16},{8,24},{16,0},{24,8},{1,17},{9,25},{17,1},{25,9},{2,18},{10... | collective-permute-start | bytes 3145736 | tf_op jit(solution)/shard_map/ppermute | solution.py:532
  53.6 9.7 %collective-permute-start.13 = (bf16[8,48,256]{2,1,0:T(8,128)(2,1)}, bf16[8,48,256]{2,1,0:T(8,128)(2,1)S(1)}, u32[]{:S(2)}, u32[]{:S(2)}) collective-permute-start(bf16[8,48,256]{2,1,0:T(8,128)(2,1)} %get-tuple-element.103), channel_id=1, source_target_pairs={{0,1},{1,0},{2,3},{3,2},{4,5},{5,4},{6,7},{7,6},{8,9},{9,8},{10,11... | collective-permute-start | bytes 589832 | tf_op jit(solution)/shard_map/ppermute | solution.py:532
  53.6 17.5 %collective-permute-start.14 = (bf16[8,48,256]{2,1,0:T(8,128)(2,1)}, bf16[8,48,256]{2,1,0:T(8,128)(2,1)S(1)}, u32[]{:S(2)}, u32[]{:S(2)}) collective-permute-start(bf16[8,48,256]{2,1,0:T(8,128)(2,1)} %get-tuple-element.104), channel_id=1, source_target_pairs={{0,2},{1,3},{2,0},{3,1},{4,6},{5,7},{6,4},{7,5},{8,10},{9,11},{10,... | collective-permute-start | bytes 589832 | tf_op jit(solution)/shard_map/ppermute | solution.py:532
  58.5 17.2 %collective-permute-start.15 = (bf16[8,48,256]{2,1,0:T(8,128)(2,1)}, bf16[8,48,256]{2,1,0:T(8,128)(2,1)S(1)}, u32[]{:S(2)}, u32[]{:S(2)}) collective-permute-start(bf16[8,48,256]{2,1,0:T(8,128)(2,1)} %get-tuple-element.105), channel_id=1, source_target_pairs={{0,3},{1,2},{2,1},{3,0},{4,7},{5,6},{6,5},{7,4},{8,11},{9,10},{10,... | collective-permute-start | bytes 589832 | tf_op jit(solution)/shard_map/ppermute | solution.py:532
  59.1 17.9 %collective-permute-start.16 = (bf16[8,48,256]{2,1,0:T(8,128)(2,1)}, bf16[8,48,256]{2,1,0:T(8,128)(2,1)S(1)}, u32[]{:S(2)}, u32[]{:S(2)}) collective-permute-start(bf16[8,48,256]{2,1,0:T(8,128)(2,1)} %get-tuple-element.106), channel_id=1, source_target_pairs={{0,4},{1,5},{2,6},{3,7},{4,0},{5,1},{6,2},{7,3},{8,12},{9,13},{10,... | collective-permute-start | bytes 589832 | tf_op jit(solution)/shard_map/ppermute | solution.py:532
  63.3 31.0 %copy-start.5 = (bf16[8,48,256]{2,1,0:T(8,128)(2,1)}, bf16[8,48,256]{2,1,0:T(8,128)(2,1)S(1)}, u32[]{:S(2)}) copy-start(bf16[8,48,256]{2,1,0:T(8,128)(2,1)S(1)} %collective-permute-done.13) | copy-start | bytes 589828
  63.3 26.7 %collective-permute-start.17 = (bf16[8,48,256]{2,1,0:T(8,128)(2,1)}, bf16[8,48,256]{2,1,0:T(8,128)(2,1)S(1)}, u32[]{:S(2)}, u32[]{:S(2)}) collective-permute-start(bf16[8,48,256]{2,1,0:T(8,128)(2,1)} %get-tuple-element.107), channel_id=1, source_target_pairs={{0,5},{1,4},{2,7},{3,6},{4,1},{5,0},{6,3},{7,2},{8,13},{9,12},{10,... | collective-permute-start | bytes 589832 | tf_op jit(solution)/shard_map/ppermute | solution.py:532
  71.2 18.8 %collective-permute-start.18 = (bf16[8,48,256]{2,1,0:T(8,128)(2,1)}, bf16[8,48,256]{2,1,0:T(8,128)(2,1)S(1)}, u32[]{:S(2)}, u32[]{:S(2)}) collective-permute-start(bf16[8,48,256]{2,1,0:T(8,128)(2,1)} %get-tuple-element.108), channel_id=1, source_target_pairs={{0,6},{1,7},{2,4},{3,5},{4,2},{5,3},{6,0},{7,1},{8,14},{9,15},{10,... | collective-permute-start | bytes 589832 | tf_op jit(solution)/shard_map/ppermute | solution.py:532
  75.7 14.4 %collective-permute-start.19 = (bf16[8,48,256]{2,1,0:T(8,128)(2,1)}, bf16[8,48,256]{2,1,0:T(8,128)(2,1)S(1)}, u32[]{:S(2)}, u32[]{:S(2)}) collective-permute-start(bf16[8,48,256]{2,1,0:T(8,128)(2,1)} %get-tuple-element.109), channel_id=1, source_target_pairs={{0,7},{1,6},{2,5},{3,4},{4,3},{5,2},{6,1},{7,0},{8,15},{9,14},{10,... | collective-permute-start | bytes 589832 | tf_op jit(solution)/shard_map/ppermute | solution.py:532
  90.1 3.7 %collective-permute-start.21 = (bf16[1,512,1024]{2,1,0:T(8,128)(2,1)}, bf16[1,512,1024]{2,1,0:T(8,128)(2,1)S(1)}, u32[]{:S(2)}, u32[]{:S(2)}) collective-permute-start(bf16[1,512,1024]{2,1,0:T(8,128)(2,1)} %collective-permute-done.11.refs_18_), channel_id=1, source_target_pairs={{0,8},{8,0},{16,24},{24,16},{1,9},{9,1},{17,25},{25,17},{2,10},{10... | collective-permute-start | bytes 3145736 | tf_op jit(solution)/shard_map/ppermute | solution.py:532
  90.1 4.1 %collective-permute-start.22 = (bf16[1,256,2048]{2,1,0:T(8,128)(2,1)S(1)}, bf16[1,256,2048]{2,1,0:T(8,128)(2,1)S(1)}, u32[]{:S(2)}, u32[]{:S(2)}) collective-permute-start(bf16[1,256,2048]{2,1,0:T(8,128)(2,1)S(1)} %collective-permute-done.20.refs_22_), channel_id=1, source_target_pairs={{0,8},{8,0},{16,24},{24,16},{1,9},{9,1},{17,25},{25,17},{2,10},{10... | collective-permute-start | bytes 3145736 | tf_op jit(solution)/shard_map/ppermute | solution.py:532
  103.7 31.3 %collective-permute-start.26 = (bf16[48,2048]{1,0:T(8,128)(2,1)}, bf16[48,2048]{1,0:T(8,128)(2,1)S(1)}, u32[]{:S(2)}, u32[]{:S(2)}) collective-permute-start(bf16[48,2048]{1,0:T(8,128)(2,1)} %get-tuple-element.137), channel_id=1, source_target_pairs={{0,4},{1,5},{2,6},{3,7},{4,0},{5,1},{6,2},{7,3},{8,12},{9,13},{10,... | collective-permute-start | bytes 589832 | tf_op jit(solution)/shard_map/ppermute | solution.py:532
  112.2 27.9 %collective-permute-start.27 = (bf16[48,2048]{1,0:T(8,128)(2,1)}, bf16[48,2048]{1,0:T(8,128)(2,1)S(1)}, u32[]{:S(2)}, u32[]{:S(2)}) collective-permute-start(bf16[48,2048]{1,0:T(8,128)(2,1)} %get-tuple-element.138), channel_id=1, source_target_pairs={{0,5},{1,4},{2,7},{3,6},{4,1},{5,0},{6,3},{7,2},{8,13},{9,12},{10,... | collective-permute-start | bytes 589832 | tf_op jit(solution)/shard_map/ppermute | solution.py:532
  113.1 27.0 %collective-permute-start.28 = (bf16[48,2048]{1,0:T(8,128)(2,1)}, bf16[48,2048]{1,0:T(8,128)(2,1)S(1)}, u32[]{:S(2)}, u32[]{:S(2)}) collective-permute-start(bf16[48,2048]{1,0:T(8,128)(2,1)} %get-tuple-element.139), channel_id=1, source_target_pairs={{0,6},{1,7},{2,4},{3,5},{4,2},{5,3},{6,0},{7,1},{8,14},{9,15},{10,... | collective-permute-start | bytes 589832 | tf_op jit(solution)/shard_map/ppermute | solution.py:532
  114.6 33.5 %copy-start.1 = (f32[128,128]{1,0:T(8,128)S(1)}, f32[128,128]{1,0:T(8,128)}, u32[]{:S(2)}) copy-start(f32[128,128]{1,0:T(8,128)} %get-tuple-element.73.slots_ref) | copy-start | bytes 196612
  114.6 25.5 %collective-permute-start.29 = (bf16[48,2048]{1,0:T(8,128)(2,1)}, bf16[48,2048]{1,0:T(8,128)(2,1)S(1)}, u32[]{:S(2)}, u32[]{:S(2)}) collective-permute-start(bf16[48,2048]{1,0:T(8,128)(2,1)} %get-tuple-element.140), channel_id=1, source_target_pairs={{0,7},{1,6},{2,5},{3,4},{4,3},{5,2},{6,1},{7,0},{8,15},{9,14},{10,... | collective-permute-start | bytes 589832 | tf_op jit(solution)/shard_map/ppermute | solution.py:532
  125.4 14.7 %collective-permute-start.23 = (bf16[48,2048]{1,0:T(8,128)(2,1)}, bf16[48,2048]{1,0:T(8,128)(2,1)S(1)}, u32[]{:S(2)}, u32[]{:S(2)}) collective-permute-start(bf16[48,2048]{1,0:T(8,128)(2,1)} %get-tuple-element.134), channel_id=1, source_target_pairs={{0,1},{1,0},{2,3},{3,2},{4,5},{5,4},{6,7},{7,6},{8,9},{9,8},{10,11... | collective-permute-start | bytes 589832 | tf_op jit(solution)/shard_map/ppermute | solution.py:532
  135.0 8.2 %collective-permute-start.24 = (bf16[48,2048]{1,0:T(8,128)(2,1)}, bf16[48,2048]{1,0:T(8,128)(2,1)S(1)}, u32[]{:S(2)}, u32[]{:S(2)}) collective-permute-start(bf16[48,2048]{1,0:T(8,128)(2,1)} %get-tuple-element.135), channel_id=1, source_target_pairs={{0,2},{1,3},{2,0},{3,1},{4,6},{5,7},{6,4},{7,5},{8,10},{9,11},{10,... | collective-permute-start | bytes 589832 | tf_op jit(solution)/shard_map/ppermute | solution.py:532
  140.1 7.9 %collective-permute-start.25 = (bf16[48,2048]{1,0:T(8,128)(2,1)}, bf16[48,2048]{1,0:T(8,128)(2,1)S(1)}, u32[]{:S(2)}, u32[]{:S(2)}) collective-permute-start(bf16[48,2048]{1,0:T(8,128)(2,1)} %get-tuple-element.136), channel_id=1, source_target_pairs={{0,3},{1,2},{2,1},{3,0},{4,7},{5,6},{6,5},{7,4},{8,11},{9,10},{10,... | collective-permute-start | bytes 589832 | tf_op jit(solution)/shard_map/ppermute | solution.py:532
  (10 other events, 79.1 us)
